TPU v7x, 32 devices: a whole 2x2x4 slice. The times are simulated.
32 devices in a mesh: dp: 8 (over y, x, core), mp: 4 (over z).
Axes of the slice: x: 2, y: 2, z: 4, core: 2. Of those that a mesh axis runs over, the one named last changes fastest.
Arguments:
- inputs: bfloat16 [8192, 2048], P('dp', 'mp'), may hold values from -6 to 6
- lengths: int32 [8, 4], P('dp'), may hold values from 0 to 1024, as said below
- cotangent: bfloat16 [8192, 2048], P('dp', 'mp'), may hold values from -6 to 6
- gains: float32 [2, 2048], replicated, may hold values from 0.4 to 1.6
- rnn_params: float32 [8, 2560], P(None, 'mp'), may hold values from -3 to 9
- rnn_in: bfloat16 [2048, 2560], P('dp', 'mp'), may hold values from -0.125 to 0.125
- branch_gate: bfloat16 [2048, 2560], P('dp', 'mp'), may hold values from -0.125 to 0.125
- recur_gate: bfloat16 [160, 2560], P('dp', 'mp'), may hold values from -0.5 to 0.5
- input_gate: bfloat16 [160, 2560], P('dp', 'mp'), may hold values from -0.5 to 0.5
- mlp_gate: bfloat16 [2048, 6144], P('dp', 'mp'), may hold values from -0.125 to 0.125
- mlp_up: bfloat16 [2048, 6144], P('dp', 'mp'), may hold values from -0.125 to 0.125
- rnn_out: bfloat16 [2560, 2048], P('mp', 'dp'), may hold values from -0.25 to 0.25
- mlp_down: bfloat16 [6144, 2048], P('mp', 'dp'), may hold values from -0.15625 to 0.15625
Outputs:
- output: bfloat16 [8192, 2048], P('dp', 'mp')
- input_grad: bfloat16 [8192, 2048], P('dp', 'mp')
- grad_gains: float32 [2, 2048], replicated
- grad_rnn_params: float32 [8, 2560], P(None, 'mp')
- grad_rnn_in: float32 [2048, 2560], P('dp', 'mp')
- grad_branch_gate: float32 [2048, 2560], P('dp', 'mp')
- grad_recur_gate: float32 [160, 2560], P('dp', 'mp')
- grad_input_gate: float32 [160, 2560], P('dp', 'mp')
- grad_mlp_gate: float32 [2048, 6144], P('dp', 'mp')
- grad_mlp_up: float32 [2048, 6144], P('dp', 'mp')
- grad_rnn_out: float32 [2560, 2048], P('mp', 'dp')
- grad_mlp_down: float32 [6144, 2048], P('mp', 'dp')
Inputs may be any that keep to these rules, and one draw needn't show every extreme that they name: In each bucket the lengths sum to at most 1024 and fill it from its start; slots may be empty; in every draw some bucket holds one sequence of 1024 tokens.
All inputs are finite; a program needn't handle non-finite values.
Results may differ from a plain program's by a relative error of at most 0.018.
Values may be sent and summed in bfloat16 or wider, within the bound.
A program may use at most 256 MiB of HBM per device.

v0:
```python
import jax
import jax.numpy as jnp
from jax import lax
from jax.sharding import PartitionSpec as P

EPS = 1e-06
DECAY_SCALE = 8.0
ROOT_FLOOR = 0.0001


def gelu_tanh(values):
    return jax.nn.gelu(values, approximate=True)


def rms_norm(values, gain):
    return values * lax.rsqrt(jnp.mean(values * values, axis=-1, keepdims=True) + EPS) * gain


def matmul(left, right):
    return jnp.dot(left, right, preferred_element_type=jnp.float32)


def inner_rows(left, right):
    return lax.dot_general(
        left, right, (((0,), (0,)), ((), ())), preferred_element_type=jnp.float32
    )


def inner_cols(left, right):
    return lax.dot_general(
        left, right, (((1,), (1,)), ((), ())), preferred_element_type=jnp.float32
    )


def segment_info(row_lengths, count):
    ends = jnp.cumsum(row_lengths)
    places = jnp.arange(count, dtype=jnp.int32)
    segment = jnp.sum((places[:, None] >= ends[None, :]).astype(jnp.int32), axis=1)
    before = jnp.concatenate([jnp.full((1,), -1, jnp.int32), segment[:-1]])
    fresh = segment != before
    live = segment < row_lengths.shape[0]
    return (segment, fresh, live)


def shift_down(values, steps, fill):
    head = jnp.full((steps,) + values.shape[1:], fill, values.dtype)
    return jnp.concatenate([head, values[:-steps]], axis=0)


def rnn_core(branch_in, recur_w, input_w, params, segment, fresh):
    taps = params.shape[0] - 4
    conv = params[0] * branch_in
    for step in range(1, taps):
        same = (shift_down(segment, step, -1) == segment)[:, None]
        conv = conv + params[step] * jnp.where(same, shift_down(branch_in, step, 0.0), 0.0)
    conv = conv + params[taps]
    rows, width = conv.shape
    span = recur_w.shape[0]
    grouped = conv.reshape(rows, width // span, span)
    rec = jnp.einsum(
        "tbk,kbj->tbj",
        grouped,
        recur_w.reshape(span, width // span, span),
        precision=lax.Precision.HIGHEST,
    ).reshape(rows, width)
    inp = jnp.einsum(
        "tbk,kbj->tbj",
        grouped,
        input_w.reshape(span, width // span, span),
        precision=lax.Precision.HIGHEST,
    ).reshape(rows, width)
    gate_r = jax.nn.sigmoid(rec + params[taps + 1])
    gate_i = jax.nn.sigmoid(inp + params[taps + 2])
    log_a = -DECAY_SCALE * gate_r * jax.nn.softplus(-params[taps + 3])
    starts = fresh[:, None]
    decay = jnp.where(starts, 0.0, jnp.exp(log_a))
    scale = jnp.where(starts, 1.0, jnp.sqrt(jnp.maximum(-jnp.expm1(2.0 * log_a), ROOT_FLOOR)))
    drive = scale * gate_i * conv

    def combine(earlier, later):
        return (earlier[0] * later[0], later[0] * earlier[1] + later[1])

    unused, state = lax.associative_scan(combine, (decay, drive), axis=0)
    return state


def gated_product(first, second):
    return first * gelu_tanh(second)


def mlp_product(gate_pre, up_pre):
    return gelu_tanh(gate_pre) * up_pre


def per_device(
    inputs,
    lengths,
    cotangent,
    gains,
    rnn_params,
    rnn_in,
    branch_gate,
    recur_gate,
    input_gate,
    mlp_gate,
    mlp_up,
    rnn_out,
    mlp_down,
):
    count = inputs.shape[0]
    width = inputs.shape[1]
    segment, fresh, live = segment_info(lengths[0], count)
    start = lax.axis_index("mp") * width
    gathered = (
        lax.all_gather(rnn_in, "dp", axis=0, tiled=True),
        lax.all_gather(branch_gate, "dp", axis=0, tiled=True),
        lax.all_gather(recur_gate, "dp", axis=0, tiled=True),
        lax.all_gather(input_gate, "dp", axis=0, tiled=True),
        lax.all_gather(mlp_gate, "dp", axis=0, tiled=True),
        lax.all_gather(mlp_up, "dp", axis=0, tiled=True),
        lax.all_gather(rnn_out, "dp", axis=1, tiled=True),
        lax.all_gather(mlp_down, "dp", axis=1, tiled=True),
    )
    full_in, full_gate, full_recur, full_input, full_mgate, full_up, full_out, full_down = gathered
    whole_in, whole_cot = (
        lax.all_gather(inputs, "mp", axis=1, tiled=True),
        lax.all_gather(cotangent, "mp", axis=1, tiled=True),
    )
    values = whole_in.astype(jnp.float32)
    normed = rms_norm(values, gains[0]).astype(jnp.bfloat16)
    branch_in = matmul(normed, full_in)
    branch_pre = matmul(normed, full_gate)
    recur_f = full_recur.astype(jnp.float32)
    input_f = full_input.astype(jnp.float32)
    state = rnn_core(branch_in, recur_f, input_f, rnn_params, segment, fresh)
    mixed = gated_product(state, branch_pre).astype(jnp.bfloat16)
    branch_part = lax.psum_scatter(matmul(mixed, full_out), "mp", scatter_dimension=1, tiled=True)
    middle_local = inputs.astype(jnp.float32) + branch_part
    middle = lax.all_gather(middle_local, "mp", axis=1, tiled=True)
    normed2 = rms_norm(middle, gains[1]).astype(jnp.bfloat16)
    gate_pre = matmul(normed2, full_mgate)
    up_pre = matmul(normed2, full_up)
    hidden = mlp_product(gate_pre, up_pre).astype(jnp.bfloat16)
    mlp_part = lax.psum_scatter(matmul(hidden, full_down), "mp", scatter_dimension=1, tiled=True)
    output = (middle_local + mlp_part).astype(jnp.bfloat16)
    grad_y = whole_cot * live[:, None].astype(jnp.bfloat16)
    grad_down = inner_rows(hidden, grad_y)
    grad_hidden = inner_cols(grad_y, full_down)
    unused, pull_mlp = jax.vjp(mlp_product, gate_pre, up_pre)
    grad_gate_pre, grad_up_pre = pull_mlp(grad_hidden)
    grad_gate_pre = grad_gate_pre.astype(jnp.bfloat16)
    grad_up_pre = grad_up_pre.astype(jnp.bfloat16)
    grad_mgate = inner_rows(normed2, grad_gate_pre)
    grad_up = inner_rows(normed2, grad_up_pre)
    normed2_part = inner_cols(grad_gate_pre, full_mgate) + inner_cols(grad_up_pre, full_up)
    grad_normed2 = lax.psum(normed2_part, "mp")
    unused, pull_norm2 = jax.vjp(rms_norm, middle, gains[1])
    middle_norm, grad_gain2 = pull_norm2(grad_normed2)
    grad_middle = grad_y.astype(jnp.float32) + middle_norm
    grad_branch_out = grad_middle.astype(jnp.bfloat16)
    grad_out = inner_rows(mixed, grad_branch_out)
    grad_mixed = inner_cols(grad_branch_out, full_out)
    unused, pull_mix = jax.vjp(gated_product, state, branch_pre)
    grad_state, grad_branch_pre = pull_mix(grad_mixed)
    grad_branch_pre = grad_branch_pre.astype(jnp.bfloat16)

    def recurrence(first, recur_w, input_w, params):
        return rnn_core(first, recur_w, input_w, params, segment, fresh)

    unused, pull_rnn = jax.vjp(recurrence, branch_in, recur_f, input_f, rnn_params)
    grad_branch_in, grad_recur, grad_input, grad_params = pull_rnn(grad_state)
    grad_branch_in = grad_branch_in.astype(jnp.bfloat16)
    grad_rnn_in = inner_rows(normed, grad_branch_in)
    grad_bgate = inner_rows(normed, grad_branch_pre)
    normed_part = inner_cols(grad_branch_in, full_in) + inner_cols(grad_branch_pre, full_gate)
    grad_normed = lax.psum(normed_part.astype(jnp.bfloat16), "mp").astype(jnp.float32)
    unused, pull_norm1 = jax.vjp(rms_norm, values, gains[0])
    values_norm, grad_gain1 = pull_norm1(grad_normed)
    grad_values = grad_middle + values_norm
    input_grad = lax.dynamic_slice_in_dim(grad_values, start, width, 1).astype(jnp.bfloat16)
    summed = (
        lax.psum_scatter(
            grad_rnn_in.astype(jnp.bfloat16), "dp", scatter_dimension=0, tiled=True
        ).astype(jnp.float32),
        lax.psum_scatter(
            grad_bgate.astype(jnp.bfloat16), "dp", scatter_dimension=0, tiled=True
        ).astype(jnp.float32),
        lax.psum_scatter(
            grad_recur.astype(jnp.bfloat16), "dp", scatter_dimension=0, tiled=True
        ).astype(jnp.float32),
        lax.psum_scatter(
            grad_input.astype(jnp.bfloat16), "dp", scatter_dimension=0, tiled=True
        ).astype(jnp.float32),
        lax.psum_scatter(
            grad_mgate.astype(jnp.bfloat16), "dp", scatter_dimension=0, tiled=True
        ).astype(jnp.float32),
        lax.psum_scatter(
            grad_up.astype(jnp.bfloat16), "dp", scatter_dimension=0, tiled=True
        ).astype(jnp.float32),
        lax.psum_scatter(
            grad_out.astype(jnp.bfloat16), "dp", scatter_dimension=1, tiled=True
        ).astype(jnp.float32),
        lax.psum_scatter(
            grad_down.astype(jnp.bfloat16), "dp", scatter_dimension=1, tiled=True
        ).astype(jnp.float32),
    )
    summed_small = (
        lax.psum(jnp.stack([grad_gain1, grad_gain2]).astype(jnp.bfloat16), "dp").astype(
            jnp.float32
        ),
        lax.psum(grad_params.astype(jnp.bfloat16), "dp").astype(jnp.float32),
    )
    return (
        output,
        input_grad,
        summed_small[0],
        summed_small[1],
        summed[0],
        summed[1],
        summed[2],
        summed[3],
        summed[4],
        summed[5],
        summed[6],
        summed[7],
    )


def solution(mesh):
    return jax.shard_map(
        per_device,
        mesh=mesh,
        in_specs=(
            P("dp", "mp"),
            P("dp", None),
            P("dp", "mp"),
            P(),
            P(None, "mp"),
            P("dp", "mp"),
            P("dp", "mp"),
            P("dp", "mp"),
            P("dp", "mp"),
            P("dp", "mp"),
            P("dp", "mp"),
            P("mp", "dp"),
            P("mp", "dp"),
        ),
        out_specs=(
            P("dp", "mp"),
            P("dp", "mp"),
            P(),
            P(None, "mp"),
            P("dp", "mp"),
            P("dp", "mp"),
            P("dp", "mp"),
            P("dp", "mp"),
            P("dp", "mp"),
            P("dp", "mp"),
            P("mp", "dp"),
            P("mp", "dp"),
        ),
        check_vma=False,
    )
```

profile of v0, /device:TPU:0, one launch (start us, length us, event | category | flops | bytes accessed | tf_op | source)
XLA Modules:
  0.0 2021.1 jit_solution(16723801871368058770)
XLA Ops:
  34.7 58.3 %all-gather.12.cloned.1.call-done = bf16[1024,2048]{1,0:T(8,128)(2,1)} async-done(((bf16[1024,512]{1,0:T(8,128)(2,1)}), bf16[1024,2048]{1,0:T(8,128)(2,1)}) %all-gather.12.cloned.1.call-update) | async-done | bytes 4194320 | tf_op jit(solution)/shard_map/all_gather | solution.py:126
  96.2 27.4 %all-gather.14.cloned.1.call-done = bf16[2048,640]{1,0:T(8,128)(2,1)} async-done(((bf16[256,640]{1,0:T(8,128)(2,1)}), bf16[2048,640]{1,0:T(8,128)(2,1)}) %all-gather.14.cloned.1.call-update) | async-done | bytes 2621456 | tf_op jit(solution)/shard_map/all_gather | solution.py:115
  290.6 144.5 %reduce-scatter.9.cloned.1.call-done = f32[1024,512]{1,0:T(8,128)} async-done(((f32[1024,2048]{1,0:T(8,128)}), f32[1024,512]{1,0:T(8,128)}) %reduce-scatter.9.cloned.1.call-update) | async-done | bytes 2097168 | tf_op jit(solution)/shard_map/reduce_scatter | solution.py:137
  441.6 147.6 %all-gather.20.cloned.1.call-done = f32[1024,2048]{1,0:T(8,128)} async-done(((f32[1024,512]{1,0:T(8,128)}), f32[1024,2048]{1,0:T(8,128)}) %all-gather.20.cloned.1.call-update) | async-done | bytes 8388624 | tf_op jit(solution)/shard_map/all_gather | solution.py:139
  597.8 37.1 %all-gather.22.cloned.1.call-done = bf16[2048,1536]{1,0:T(8,128)(2,1)} async-done(((bf16[256,1536]{1,0:T(8,128)(2,1)}), bf16[2048,1536]{1,0:T(8,128)(2,1)}) %all-gather.22.cloned.1.call-update) | async-done | bytes 6291472 | tf_op jit(solution)/shard_map/all_gather | solution.py:119
  634.9 11.9 fusion.111
  646.8 35.5 %all-gather.24.cloned.1.call-done = bf16[2048,1536]{1,0:T(8,128)(2,1)} async-done(((bf16[256,1536]{1,0:T(8,128)(2,1)}), bf16[2048,1536]{1,0:T(8,128)(2,1)}) %all-gather.24.cloned.1.call-update) | async-done | bytes 6291472 | tf_op jit(solution)/shard_map/all_gather | solution.py:120
  682.4 11.7 fusion.112
  694.1 70.7 %all-gather.28.cloned.1.call-done = bf16[1024,2048]{1,0:T(8,128)(2,1)} async-done(((bf16[1024,512]{1,0:T(8,128)(2,1)}), bf16[1024,2048]{1,0:T(8,128)(2,1)}) %all-gather.28.cloned.1.call-update) | async-done | bytes 4194320 | tf_op jit(solution)/shard_map/all_gather | solution.py:127
  764.7 47.0 %all-gather.26.cloned.1.call-done = bf16[1536,2048]{1,0:T(8,128)(2,1)} async-done(((bf16[1536,256]{1,0:T(8,128)(2,1)}), bf16[1536,2048]{1,0:T(8,128)(2,1)}) %all-gather.26.cloned.1.call-update) | async-done | bytes 6291472 | tf_op jit(solution)/shard_map/all_gather | solution.py:122
  811.7 19.2 multiply_convert_fusion.2
  851.6 290.9 %all-reduce.119.cloned.1.call-done = f32[1024,2048]{1,0:T(8,128)} async-done(((f32[1024,2048]{1,0:T(8,128)}), f32[1024,2048]{1,0:T(8,128)}) %all-reduce.119.cloned.1.call-update) | async-done | bytes 8388624 | tf_op jit(solution)/shard_map/psum | solution.py:156
  1156.9 11.5 fusion.18
  1329.3 11.6 convolution_convert_fusion.1
  1340.9 11.7 convolution_convert_fusion
  1408.9 11.8 fusion.113
  1438.3 62.9 %reduce-scatter.19.cloned.1.call-done = bf16[256,1536]{1,0:T(8,128)(2,1)} async-done(((bf16[2048,1536]{1,0:T(8,128)(2,1)}), bf16[256,1536]{1,0:T(8,128)(2,1)}) %reduce-scatter.19.cloned.1.call-update) | async-done | bytes 786448 | tf_op jit(solution)/shard_map/reduce_scatter | solution.py:197
  1503.7 62.5 %reduce-scatter.23.cloned.1.call-done = bf16[1536,256]{1,0:T(8,128)(2,1)} async-done(((bf16[1536,2048]{1,0:T(8,128)(2,1)}), bf16[1536,256]{1,0:T(8,128)(2,1)}) %reduce-scatter.23.cloned.1.call-update) | async-done | bytes 786448 | tf_op jit(solution)/shard_map/reduce_scatter | solution.py:203
  1568.6 44.9 %reduce-scatter.13.cloned.1.call-done = bf16[256,640]{1,0:T(8,128)(2,1)} async-done(((bf16[2048,640]{1,0:T(8,128)(2,1)}), bf16[256,640]{1,0:T(8,128)(2,1)}) %reduce-scatter.13.cloned.1.call-update) | async-done | bytes 327696 | tf_op jit(solution)/shard_map/reduce_scatter | solution.py:182
  1615.3 45.4 %reduce-scatter.21.cloned.1.call-done = bf16[640,256]{1,0:T(8,128)(2,1)} async-done(((bf16[640,2048]{1,0:T(8,128)(2,1)}), bf16[640,256]{1,0:T(8,128)(2,1)}) %reduce-scatter.21.cloned.1.call-update) | async-done | bytes 327696 | tf_op jit(solution)/shard_map/reduce_scatter | solution.py:200
  1662.5 45.4 %reduce-scatter.15.cloned.1.call-done = bf16[256,640]{1,0:T(8,128)(2,1)} async-done(((bf16[2048,640]{1,0:T(8,128)(2,1)}), bf16[256,640]{1,0:T(8,128)(2,1)}) %reduce-scatter.15.cloned.1.call-update) | async-done | bytes 327696 | tf_op jit(solution)/shard_map/reduce_scatter | solution.py:185
  1709.7 155.6 %all-reduce.121.cloned.1.call-done = bf16[1024,2048]{1,0:T(8,128)(2,1)} async-done(((bf16[1024,2048]{1,0:T(8,128)(2,1)}), bf16[1024,2048]{1,0:T(8,128)(2,1)}) %all-reduce.121.cloned.1.call-update) | async-done | bytes 4194320 | tf_op jit(solution)/shard_map/psum | solution.py:176
  1873.3 25.5 %all-reduce.113 = (bf16[2,2048]{1,0:T(2,128)(2,1)S(1)}, bf16[8,640]{1,0:T(8,128)(2,1)S(1)}) all-reduce(bf16[2,2048]{1,0:T(2,128)(2,1)S(1)} %pad_maximum_fusion.8, bf16[8,640]{1,0:T(8,128)(2,1)S(1)} %add_convert_fusion.3), channel_id=1, replica_groups=mesh['dp'=8,'mp'=4] {'dp'}, use_global_device_ids=true, to_apply=%region_12.13 | all-reduce | flops 9216 | bytes 36864 | tf_op jit(solution)/shard_map/psum | solution.py:208
  1904.6 106.4 %reduce-scatter.11.cloned.1.call-done = f32[1024,512]{1,0:T(8,128)} async-done(((f32[1024,2048]{1,0:T(8,128)}), f32[1024,512]{1,0:T(8,128)}) %reduce-scatter.11.cloned.1.call-update) | async-done | bytes 2097168 | tf_op jit(solution)/shard_map/reduce_scatter | solution.py:144
  (749 shorter events, 505.6 us)
Async XLA Ops:
  7.2 85.9 %all-gather.12.cloned.1.call-start = ((), (), s32[]{:S(2)}) async-start(), calls=%async_computation.8 | async-start | bytes 5242880 | tf_op jit(solution)/shard_map/all_gather | solution.py:126
  7.9 115.7 %all-gather.14.cloned.1.call-start = ((), (), s32[]{:S(2)}) async-start(), calls=%async_computation.9 | async-start | bytes 2949120 | tf_op jit(solution)/shard_map/all_gather | solution.py:115
  8.7 261.8 %all-gather.16.cloned.1.call-start = ((), (), s32[]{:S(2)}) async-start(), calls=%async_computation.10 | async-start | bytes 2949120 | tf_op jit(solution)/shard_map/all_gather | solution.py:116
  9.4 272.2 %all-gather.18.cloned.1.call-start = ((), (), s32[]{:S(2)}) async-start(), calls=%async_computation.11 | async-start | bytes 2949120 | tf_op jit(solution)/shard_map/all_gather | solution.py:121
  10.0 425.1 %reduce-scatter.9.cloned.1.call-start = ((), (), s32[]{:S(2)}) async-start(), calls=%async_computation.12 | async-start | bytes 10485760 | tf_op jit(solution)/shard_map/reduce_scatter | solution.py:137
  13.4 138.2 %copy-start.119 = (f32[640]{0:T(1024)}, f32[640]{0:T(1024)S(1)}, u32[]{:S(2)}) copy-start(f32[640]{0:T(1024)S(1)} %get-tuple-element.131) | copy-start | bytes 7684
  13.5 138.2 %copy-start.121 = (f32[640]{0:T(1024)}, f32[640]{0:T(1024)S(1)}, u32[]{:S(2)}) copy-start(f32[640]{0:T(1024)S(1)} %get-tuple-element.137) | copy-start | bytes 7684
  290.6 298.7 %all-gather.20.cloned.1.call-start = ((), (), s32[]{:S(2)}) async-start(), calls=%async_computation.13 | async-start | bytes 10485760 | tf_op jit(solution)/shard_map/all_gather | solution.py:139
  438.8 196.1 %all-gather.22.cloned.1.call-start = ((), (), s32[]{:S(2)}) async-start(), calls=%async_computation.14 | async-start | bytes 7077888 | tf_op jit(solution)/shard_map/all_gather | solution.py:119
  439.5 242.8 %all-gather.24.cloned.1.call-start = ((), (), s32[]{:S(2)}) async-start(), calls=%async_computation.15 | async-start | bytes 7077888 | tf_op jit(solution)/shard_map/all_gather | solution.py:120
  440.3 324.5 %all-gather.28.cloned.1.call-start = ((), (), s32[]{:S(2)}) async-start(), calls=%async_computation.18 | async-start | bytes 5242880 | tf_op jit(solution)/shard_map/all_gather | solution.py:127
  441.0 370.7 %all-gather.26.cloned.1.call-start = ((), (), s32[]{:S(2)}) async-start(), calls=%async_computation.16 | async-start | bytes 7077888 | tf_op jit(solution)/shard_map/all_gather | solution.py:122
  441.6 700.9 %all-reduce.119.cloned.1.call-start = ((), (), s32[]{:S(2)}) async-start(), calls=%async_computation.19 | async-start | bytes 16777216 | tf_op jit(solution)/shard_map/psum | solution.py:156
  646.8 164.9 %copy-start.183 = (bf16[1024]{0:T(1024)(128)(2,1)S(1)}, bf16[1024]{0:T(1024)(128)(2,1)}, u32[]{:S(2)}) copy-start(bf16[1024]{0:T(1024)(128)(2,1)} %get-tuple-element.162) | copy-start | bytes 6148
  851.6 579.1 %all-reduce.123.cloned.1.call-start = ((), (), s32[]{:S(2)}) async-start(), calls=%async_computation.27 | async-start | bytes 819200
  1317.7 118.2 %reduce-scatter.17.cloned.1.call-start = ((), (), s32[]{:S(2)}) async-start(), calls=%async_computation.23 | async-start | bytes 7077888 | tf_op jit(solution)/shard_map/reduce_scatter | solution.py:194
  1329.2 172.0 %reduce-scatter.19.cloned.1.call-start = ((), (), s32[]{:S(2)}) async-start(), calls=%async_computation.24 | async-start | bytes 7077888 | tf_op jit(solution)/shard_map/reduce_scatter | solution.py:197
  1340.9 225.3 %reduce-scatter.23.cloned.1.call-start = ((), (), s32[]{:S(2)}) async-start(), calls=%async_computation.26 | async-start | bytes 7077888 | tf_op jit(solution)/shard_map/reduce_scatter | solution.py:203
  1352.6 260.8 %reduce-scatter.13.cloned.1.call-start = ((), (), s32[]{:S(2)}) async-start(), calls=%async_computation.21 | async-start | bytes 2949120 | tf_op jit(solution)/shard_map/reduce_scatter | solution.py:182
  1379.9 280.7 %reduce-scatter.21.cloned.1.call-start = ((), (), s32[]{:S(2)}) async-start(), calls=%async_computation.25 | async-start | bytes 2949120 | tf_op jit(solution)/shard_map/reduce_scatter | solution.py:200
  1389.4 318.4 %reduce-scatter.15.cloned.1.call-start = ((), (), s32[]{:S(2)}) async-start(), calls=%async_computation.22 | async-start | bytes 2949120 | tf_op jit(solution)/shard_map/reduce_scatter | solution.py:185
  1397.7 467.7 %all-reduce.121.cloned.1.call-start = ((), (), s32[]{:S(2)}) async-start(), calls=%async_computation.20 | async-start | bytes 8388608 | tf_op jit(solution)/shard_map/psum | solution.py:176
  1408.6 602.5 %reduce-scatter.11.cloned.1.call-start = ((), (), s32[]{:S(2)}) async-start(), calls=%async_computation.17 | async-start | bytes 10485760 | tf_op jit(solution)/shard_map/reduce_scatter | solution.py:144
  1709.7 190.4 %copy-start.155 = (f32[1024]{0:T(1024)S(1)}, f32[1024]{0:T(1024)}, u32[]{:S(2)}) copy-start(f32[1024]{0:T(1024)} %copy-done.154) | copy-start | bytes 12292
  (189 other events, 2649.6 us)
Sparse Core Ops, SparseCore 0:
  9.6 83.4 all-gather.11
  95.0 28.6 all-gather.13
  125.5 30.1 all-gather.15
  157.4 30.4 all-gather.17
  290.7 144.3 reduce-scatter.8
  438.9 150.3 all-gather.19
  591.2 43.7 all-gather.21
  636.8 45.5 all-gather.23
  683.9 80.7 all-gather.27
  766.5 45.1 all-gather.25
  851.7 290.8 all-reduce.118
  1317.8 52.5 all-reduce.122
  1373.8 61.9 reduce-scatter.16
  1439.5 61.7 reduce-scatter.18
  1504.4 61.7 reduce-scatter.22
  1569.7 43.6 reduce-scatter.12
  1617.0 43.6 reduce-scatter.20
  1664.2 43.6 reduce-scatter.14
  1710.4 154.9 all-reduce.120
  1867.6 143.4 reduce-scatter.10
where the time goes:
time: 2030 us; the launch traced here: 2020 us
  waiting for transfers between devices  1390 us (68%)
  local copies, waits for them, and re-layouts  221 us (11%)
  matrix products  203 us (10%)
  other arithmetic  141 us (7%)
  blocking collectives  45.6 us (2%)
    psum x1, waiting for transfers between devices, per_device(): grad_normed2 = lax.psum(normed2_part, 'mp')  291 us
    psum x1, waiting for transfers between devices, per_device(): lax.psum(normed_part.astype(jnp.bfloat16), 'mp').astype(jnp.float32)  156 us
    all_gather x1, waiting for transfers between devices, per_device(): middle = lax.all_gather(middle_local, 'mp', axis=1, tiled=True)  148 us
    reduce_scatter x1, waiting for transfers between devices, per_device(): lax.psum_scatter(matmul(mixed, full_out), 'mp', scatter_dimension=1, tile...  144 us
    reduce_scatter x1, waiting for transfers between devices, per_device(): lax.psum_scatter(matmul(hidden, full_down), 'mp', scatter_dimension=1, ti...  106 us
    pad x79, local copies, waits for them, and re-layouts, rnn_core(): unused, state = lax.associative_scan(combine, (decay, drive), axis=0)  94.2 us
    slice x78, local copies, waits for them, and re-layouts, rnn_core(): unused, state = lax.associative_scan(combine, (decay, drive), axis=0)  92.5 us
    all_gather x1, waiting for transfers between devices, per_device(): lax.all_gather(cotangent, 'mp', axis=1, tiled=True)  70.7 us
  transfers between devices with their start and end apart: 20, of which 17 were waited for; matrix products, arithmetic and copies ran while one was open for 16% of the time, Pallas kernels for 0%

commit v1 on v0

v1 whole, which is shorter than its diff:
```python
import functools

import jax
import jax.numpy as jnp
from jax import lax
from jax.experimental import pallas as pl
from jax.experimental.pallas import tpu as pltpu
from jax.sharding import PartitionSpec as P

EPS = 1e-06
DECAY_SCALE = 8.0
ROOT_FLOOR = 0.0001
TAPS = 4
LANES = 8
CHUNKS = 2
TILE = 32
F32 = jnp.float32
BF16 = jnp.bfloat16
VMEM_BYTES = 56 * 1024 * 1024


def matmul(left, right):
    return jnp.dot(left, right, preferred_element_type=F32)


def inner_rows(left, right):
    return lax.dot_general(left, right, (((0,), (0,)), ((), ())), preferred_element_type=F32)


def inner_cols(left, right):
    return lax.dot_general(left, right, (((1,), (1,)), ((), ())), preferred_element_type=F32)


def gelu_and_slope(values):
    outer = 0.7978845608028654
    inner = 0.044715
    square = values * values
    bent = jnp.tanh(outer * values * (1.0 + inner * square))
    half = 0.5 * (1.0 + bent)
    slope = half + 0.5 * values * (1.0 - bent * bent) * outer * (1.0 + 3.0 * inner * square)
    return values * half, slope


def gelu(values):
    outer = 0.7978845608028654
    inner = 0.044715
    bent = jnp.tanh(outer * values * (1.0 + inner * values * values))
    return values * (0.5 * (1.0 + bent))


def one_less_exp(values):
    near = -values * (1.0 + 0.5 * values * (1.0 + (values / 3.0) * (1.0 + 0.25 * values)))
    return jnp.where(values > -0.02, near, 1.0 - jnp.exp(values))


def after(value, *earlier):
    return lax.optimization_barrier((value,) + earlier)[0]


def line_gather(mine, axis, size):
    place = lax.axis_index(axis)
    width = mine.shape[1]
    right, left = mine, mine
    rights, lefts = {}, {}
    for step in range(1, size):
        right = lax.ppermute(right, axis, [(i, i + 1) for i in range(step - 1, size - 1)])
        left = lax.ppermute(left, axis, [(i + 1, i) for i in range(size - step)])
        rights[step], lefts[step] = right, left
    whole = jnp.zeros((mine.shape[0], size * width), mine.dtype)
    for step in range(size):
        block = mine if step == 0 else lefts[step] + rights[size - step]
        spot = lax.rem(place + step, size) * width
        whole = lax.dynamic_update_slice_in_dim(whole, block, spot, 1)
    return whole


def line_scatter(part, axis, size):
    place = lax.axis_index(axis)
    width = part.shape[1] // size

    def block(index):
        spot = jnp.clip(index, 0, size - 1) * width
        return lax.dynamic_slice_in_dim(part, spot, width, 1).astype(F32)

    right, left = None, None
    for step in range(1, size):
        going = block(size - step + place)
        if right is not None:
            going = going + right.astype(F32)
        right = lax.ppermute(going.astype(BF16), axis, [(i, i + 1) for i in range(step)])
        going = block(place - (size - step))
        if left is not None:
            going = going + left.astype(F32)
        left = lax.ppermute(
            going.astype(BF16), axis, [(i, i - 1) for i in range(size - step, size)]
        )
    return block(place) + right.astype(F32) + left.astype(F32)


def line_sum(value, axis, size):
    bit = 1
    while bit < size:
        value = value + lax.ppermute(value, axis, [(i, i ^ bit) for i in range(size)])
        bit *= 2
    return value


def pair_gather(mine, axis, size):
    place = lax.axis_index(axis)
    bit = 1
    while bit < size:
        other = lax.ppermute(mine, axis, [(i, i ^ bit) for i in range(size)])
        upper = (place & bit) != 0
        mine = jnp.concatenate(
            [jnp.where(upper, other, mine), jnp.where(upper, mine, other)], axis=0
        )
        bit *= 2
    return mine


def pair_scatter(part, axis, size):
    place = lax.axis_index(axis)
    part = part.astype(F32)
    bit = size // 2
    while bit >= 1:
        upper = (place & bit) != 0
        low, high = jnp.split(part, 2, axis=0)
        going = jnp.where(upper, low, high).astype(BF16)
        came = lax.ppermute(going, axis, [(i, i ^ bit) for i in range(size)])
        part = jnp.where(upper, high, low) + came.astype(F32)
        bit //= 2
    return part


def swap(size, bit):
    return [(i, i ^ bit) for i in range(size)]


def cross(size):
    return [(i, i ^ 4 if i % 2 == 0 else i ^ 2) for i in range(size)]


def square_gather(mine, axis, size):
    if size != 8:
        return pair_gather(mine, axis, size)
    place = lax.axis_index(axis)
    rows = mine.shape[0]
    by_x = lax.ppermute(mine, axis, swap(size, 2))
    by_y = lax.ppermute(mine, axis, swap(size, 4))
    onward = jnp.where((place & 1) == 0, by_x, by_y)
    far = lax.ppermute(onward, axis, cross(size))
    held = {0: mine, 2: by_x, 4: by_y, 6: far}
    for bits in (0, 2, 4, 6):
        held[bits + 1] = lax.ppermute(held[bits], axis, swap(size, 1))
    whole = jnp.zeros((size * rows,) + mine.shape[1:], mine.dtype)
    for bits, block in held.items():
        whole = lax.dynamic_update_slice_in_dim(whole, block, (place ^ bits) * rows, 0)
    return whole


def square_scatter(part, axis, size):
    if size != 8:
        return pair_scatter(part, axis, size)
    place = lax.axis_index(axis)
    core = place & 1
    chip = lax.shift_right_logical(place, 1)
    split = part.reshape(size // 2, 2, part.shape[0] // size, part.shape[1])
    going = lax.dynamic_index_in_dim(split, 1 - core, 1, keepdims=False)
    came = lax.ppermute(going, axis, swap(size, 1))
    kept = lax.dynamic_index_in_dim(split, core, 1, keepdims=False)
    both = (kept.astype(F32) + came.astype(F32)).astype(BF16)

    def pick(index):
        return lax.dynamic_index_in_dim(both, index, 0, keepdims=False)

    far = lax.ppermute(pick(chip ^ 3), axis, cross(size)).astype(F32)
    none = jnp.zeros((), F32)
    to_x = pick(chip ^ 1).astype(F32) + jnp.where(core == 0, far, none)
    to_y = pick(chip ^ 2).astype(F32) + jnp.where(core == 1, far, none)
    by_x = lax.ppermute(to_x.astype(BF16), axis, swap(size, 2))
    by_y = lax.ppermute(to_y.astype(BF16), axis, swap(size, 4))
    return pick(chip).astype(F32) + by_x.astype(F32) + by_y.astype(F32)


def tile_loop(count, body):
    lax.fori_loop(0, count, lambda i, c: (body(i), c)[1], 0)


def rows_at(index, size):
    return pl.ds(pl.multiple_of(index * size, size), size)


def put(ref, rows, values):
    for j in range(ref.shape[0]):
        ref[j, rows, :] = values[:, j * 128 : (j + 1) * 128]


def get(ref, rows):
    return jnp.concatenate([ref[j, rows, :] for j in range(ref.shape[0])], axis=1)


def rnn_forward_kernel(
    both_ref, halo_ref, start_ref, mask_ref, gates_ref, params_ref,
    mixed_ref, conv_ref, r_ref, i_ref, state_ref, end_ref,
    padded, high, low, decay, drive,
):
    count, width = conv_ref.shape
    seg = count // 8
    tiles = count // TILE
    padded[0:8, :] = halo_ref[...]
    padded[8:, :] = both_ref[:, 0:width]

    def convolve(t):
        span = padded[pl.ds(pl.multiple_of(t * TILE, TILE), TILE + 8), :]
        mask = mask_ref[rows_at(t, TILE), :]
        conv = params_ref[0:1, :] * span[8:, :] + params_ref[TAPS : TAPS + 1, :]
        for k in range(1, TAPS):
            moved = span[8 - k : 8 - k + TILE, :]
            conv = conv + params_ref[k : k + 1, :] * (moved * mask[:, k : k + 1])
        conv_ref[rows_at(t, TILE), :] = conv
        top = conv.astype(BF16)
        high[rows_at(t, TILE), :] = top
        low[rows_at(t, TILE), :] = (conv - top.astype(F32)).astype(BF16)

    tile_loop(tiles, convolve)

    block = min(256, count)

    def gate(t):
        rows = rows_at(t, block)
        weights = gates_ref[...]
        both = jnp.dot(high[rows, :], weights, preferred_element_type=F32)
        both = both + jnp.dot(low[rows, :], weights, preferred_element_type=F32)
        r_ref[rows, :] = both[:, 0:width]
        i_ref[rows, :] = both[:, width:]

    tile_loop(count // block, gate)

    strength = DECAY_SCALE * jax.nn.softplus(-params_ref[TAPS + 3 : TAPS + 4, :])

    def prepare(t):
        rows = rows_at(t, TILE)
        keep = mask_ref[rows, :][:, 0:1]
        r = jax.nn.sigmoid(r_ref[rows, :] + params_ref[TAPS + 1 : TAPS + 2, :])
        i = jax.nn.sigmoid(i_ref[rows, :] + params_ref[TAPS + 2 : TAPS + 3, :])
        log_a = -strength * r
        scale = jnp.sqrt(jnp.maximum(one_less_exp(2.0 * log_a), ROOT_FLOOR))
        scale = jnp.where(keep > 0.0, scale, 1.0)
        put(decay, rows, jnp.exp(log_a) * keep)
        put(drive, rows, scale * i * conv_ref[rows, :])
        r_ref[rows, :] = r
        i_ref[rows, :] = i

    tile_loop(tiles, prepare)

    def scan(t, carry):
        held, prod = carry
        rows = pl.ds(t, 8, stride=seg)
        a = get(decay, rows)
        held = a * held + get(drive, rows)
        prod = a * prod
        put(drive, rows, held)
        put(decay, rows, prod)
        return held, prod

    shape = (8, width)
    held, prod = lax.fori_loop(0, seg, scan, (jnp.zeros(shape, F32), jnp.ones(shape, F32)))
    carry = start_ref[0:1, :]
    carries = []
    for s in range(8):
        carries.append(carry)
        carry = prod[s : s + 1, :] * carry + held[s : s + 1, :]
    end_ref[...] = jnp.broadcast_to(carry, shape)

    small = min(TILE, seg)
    for s in range(8):

        def finish(t, s=s):
            rows = pl.ds(pl.multiple_of(s * seg + t * small, small), small)
            state = get(drive, rows) + get(decay, rows) * carries[s]
            state_ref[rows, :] = state
            mixed_ref[rows, :] = (state * gelu(both_ref[rows, width:])).astype(BF16)

        tile_loop(seg // small, finish)


def rnn_forward(both, halo, start, mask, gates, params):
    count, width = both.shape[0], both.shape[1] // 2
    full = jax.ShapeDtypeStruct((count, width), F32)
    return pl.pallas_call(
        rnn_forward_kernel,
        out_shape=(
            jax.ShapeDtypeStruct((count, width), BF16),
            full, full, full, full,
            jax.ShapeDtypeStruct((8, width), F32),
        ),
        scratch_shapes=[
            pltpu.VMEM((count + 8, width), F32),
            pltpu.VMEM((count, width), BF16),
            pltpu.VMEM((count, width), BF16),
            pltpu.VMEM((width // 128, count, 128), F32),
            pltpu.VMEM((width // 128, count, 128), F32),
        ],
        compiler_params=pltpu.CompilerParams(vmem_limit_bytes=VMEM_BYTES),
        cost_estimate=pl.CostEstimate(
            flops=4 * count * width * 2 * width, bytes_accessed=count * width * 30,
            transcendentals=count * width * 6,
        ),
        name="rnn_forward",
    )(both, halo, start, mask, gates, params)


def rnn_backward_kernel(
    gm_ref, both_ref, halo_ref, start_ref, conv_ref, r_ref, i_ref, state_ref, mask_ref,
    gates_ref, params_ref, back_ref, tail_ref,
    grads_ref, rates_ref, dparams_ref, back_out_ref, tail_out_ref,
    padded, before, decay, adjoint, coef, dconv, sums,
):
    count, width = conv_ref.shape
    seg = count // 8
    tiles = count // TILE
    padded[0:8, :] = halo_ref[...]
    padded[8:, :] = both_ref[:, 0:width]
    before[0:8, :] = start_ref[...]
    before[8:, :] = state_ref[...]
    strength = DECAY_SCALE * jax.nn.softplus(-params_ref[TAPS + 3 : TAPS + 4, :])

    def prepare(t):
        rows = rows_at(t, TILE)
        keep = mask_ref[rows, :][:, 0:1]
        gm = gm_ref[rows, :]
        value, slope = gelu_and_slope(both_ref[rows, width:])
        put(adjoint, rows, gm * value)
        grads_ref[rows, width:] = (gm * state_ref[rows, :] * slope).astype(BF16)
        put(decay, rows, jnp.exp(-strength * r_ref[rows, :]) * keep)

    tile_loop(tiles, prepare)

    def scan(t, carry):
        held, prod = carry
        rows = pl.ds(seg - 1 - t, 8, stride=seg)
        a = get(decay, rows)
        total = get(adjoint, rows) + held
        put(adjoint, rows, total)
        put(coef, rows, prod)
        return a * total, a * prod

    shape = (8, width)
    held, prod = lax.fori_loop(0, seg, scan, (jnp.zeros(shape, F32), jnp.ones(shape, F32)))
    carry = back_ref[0:1, :]
    carries = [None] * 8
    for s in reversed(range(8)):
        carries[s] = carry
        carry = prod[s : s + 1, :] * carry + held[s : s + 1, :]
    back_out_ref[...] = jnp.broadcast_to(carry, shape)

    sums[...] = jnp.zeros_like(sums)

    def fold(values):
        return jnp.sum(values.reshape(-1, 8, width), axis=0)

    small = min(TILE, seg)
    for s in range(8):

        def chain(t, s=s):
            base = pl.multiple_of(s * seg + t * small, small)
            rows = pl.ds(base, small)
            keep = mask_ref[rows, :][:, 0:1]
            a = get(adjoint, rows) + get(coef, rows) * carries[s]
            r, i, conv = r_ref[rows, :], i_ref[rows, :], conv_ref[rows, :]
            fall = get(decay, rows)
            prior = before[pl.ds(base, small + 8), :][7 : 7 + small, :]
            room = one_less_exp(-2.0 * strength * r)
            bound = jnp.maximum(room, ROOT_FLOOR)
            inverse = lax.rsqrt(bound)
            live = keep > 0.0
            scale = jnp.where(live, bound * inverse, 1.0)
            open_ = jnp.where(room > ROOT_FLOOR, inverse, 0.0)
            driven = a * i
            dlog = fall * (a * prior - fall * driven * conv * open_)
            common = a * scale
            drec = dlog * (-strength) * r * (1.0 - r)
            dinp = common * conv * i * (1.0 - i)
            rates_ref[rows, 0:width] = drec.astype(BF16)
            rates_ref[rows, width:] = dinp.astype(BF16)
            dconv[rows, :] = common * i
            sums[5] += fold(drec)
            sums[6] += fold(dinp)
            sums[7] += fold(dlog * r)

        tile_loop(seg // small, chain)

    block = min(256, count)

    def spread(t):
        rows = rows_at(t, block)
        dconv[rows, :] += lax.dot_general(
            rates_ref[rows, :], gates_ref[...], (((1,), (1,)), ((), ())),
            preferred_element_type=F32,
        )

    tile_loop(count // block, spread)
    dconv[count:, :] = tail_ref[...]
    tail_out_ref[...] = dconv[0:8, :]

    def unconvolve(t):
        base = pl.multiple_of(t * TILE, TILE)
        rows = pl.ds(base, TILE)
        span = dconv[pl.ds(base, TILE + 8), :]
        mask = mask_ref[pl.ds(base, TILE + 8), :]
        source = padded[pl.ds(base, TILE + 8), :]
        here = span[0:TILE, :]
        out = params_ref[0:1, :] * here
        sums[0] += fold(here * source[8:, :])
        sums[4] += fold(here)
        for k in range(1, TAPS):
            kept = span * mask[:, k : k + 1]
            out = out + params_ref[k : k + 1, :] * kept[k : k + TILE, :]
            sums[k] += fold(kept[0:TILE, :] * source[8 - k : 8 - k + TILE, :])
        grads_ref[rows, 0:width] = out.astype(BF16)

    tile_loop(tiles, unconvolve)
    for k in range(8):
        dparams_ref[k : k + 1, :] = jnp.sum(sums[k], axis=0, keepdims=True)
    dparams_ref[TAPS + 3 : TAPS + 4, :] = (
        DECAY_SCALE
        * jax.nn.sigmoid(-params_ref[TAPS + 3 : TAPS + 4, :])
        * jnp.sum(sums[TAPS + 3], axis=0, keepdims=True)
    )


def rnn_backward(gm, both, halo, start, saved, mask, gates, params, back, tail):
    conv, r, i, state = saved
    count, width = conv.shape
    return pl.pallas_call(
        rnn_backward_kernel,
        out_shape=(
            jax.ShapeDtypeStruct((count, 2 * width), BF16),
            jax.ShapeDtypeStruct((count, 2 * width), BF16),
            jax.ShapeDtypeStruct((8, width), F32),
            jax.ShapeDtypeStruct((8, width), F32),
            jax.ShapeDtypeStruct((8, width), F32),
        ),
        scratch_shapes=[
            pltpu.VMEM((count + 8, width), F32),
            pltpu.VMEM((count + 8, width), F32),
            pltpu.VMEM((width // 128, count, 128), F32),
            pltpu.VMEM((width // 128, count, 128), F32),
            pltpu.VMEM((width // 128, count, 128), F32),
            pltpu.VMEM((count + 8, width), F32),
            pltpu.VMEM((8, 8, width), F32),
        ],
        compiler_params=pltpu.CompilerParams(vmem_limit_bytes=VMEM_BYTES),
        cost_estimate=pl.CostEstimate(
            flops=2 * count * width * 2 * width, bytes_accessed=count * width * 36,
            transcendentals=count * width * 6,
        ),
        name="rnn_backward",
    )(gm, both, halo, start, conv, r, i, state, mask, gates, params, back, tail)


def make_masks(row_lengths, count):
    ends = jnp.cumsum(row_lengths)
    places = jnp.arange(-TAPS, count, dtype=jnp.int32)
    segment = jnp.sum((places[:, None] >= ends[None, :]).astype(jnp.int32), axis=1)
    segment = jnp.where(places < 0, -1, segment)
    now = segment[TAPS:]
    same = [(segment[TAPS - k : TAPS - k + count] == now).astype(F32) for k in range(1, TAPS)]
    blank = jnp.zeros((count,), F32)
    columns = [same[0]] + same + [blank] * (LANES - TAPS)
    live = now < row_lengths.shape[0]
    return jnp.stack(columns, axis=1), live


def dense_gates(gates, width):
    span = gates.shape[0]
    tiled = jnp.tile(gates, (width // span, 1))
    row = lax.broadcasted_iota(jnp.int32, tiled.shape, 0) // span
    column = (lax.broadcasted_iota(jnp.int32, tiled.shape, 1) % width) // span
    return jnp.where(row == column, tiled, jnp.zeros((), tiled.dtype))


def diagonal_blocks(dense, span):
    width = dense.shape[0]
    column = (lax.broadcasted_iota(jnp.int32, (1, 2 * width), 1) % width) // span
    total = jnp.zeros((span, 2 * width), F32)
    for b in range(width // span):
        total = total + jnp.where(column == b, dense[b * span : (b + 1) * span], 0.0)
    return total


def per_device(
    dp, mp,
    inputs, lengths, cotangent, gains, rnn_params, rnn_in, branch_gate, recur_gate, input_gate,
    mlp_gate, mlp_up, rnn_out, mlp_down,
):
    count, part = inputs.shape
    width = rnn_in.shape[1]
    hidden_width = mlp_gate.shape[1]
    span = recur_gate.shape[0] * dp
    features = part * mp
    step = count // CHUNKS
    spot = lax.axis_index("mp") * part

    def cut(values):
        return [values[c * step : (c + 1) * step] for c in range(CHUNKS)]

    def mine(values):
        return lax.dynamic_slice_in_dim(values, spot, part, values.ndim - 1)

    gates = pair_gather(jnp.concatenate([recur_gate, input_gate], axis=1), "dp", dp)
    w_in = square_gather(jnp.concatenate([rnn_in, branch_gate], axis=1), "dp", dp)
    w_out = square_gather(after(rnn_out.T, w_in), "dp", dp)
    w_up = square_gather(
        after(jnp.concatenate([mlp_gate, mlp_up], axis=1), w_out), "dp", dp
    )
    w_down = square_gather(after(mlp_down.T, w_up), "dp", dp)

    in_parts = cut(inputs)
    wholes = []
    for c in range(CHUNKS):
        source = in_parts[c] if c == 0 else after(in_parts[c], wholes[-1])
        wholes.append(line_gather(source, "mp", mp))
    cots = []
    cot_parts = cut(cotangent)
    for c in range(CHUNKS):
        cots.append(line_gather(after(cot_parts[c], wholes[-1], *cots[-1:]), "mp", mp))

    mask, live = make_masks(lengths[0], count)
    masks = cut(mask)
    mask_tail = jnp.concatenate([mask, jnp.zeros((8, LANES), F32)], axis=0)
    tail_masks = [mask_tail[c * step : (c + 1) * step + 8] for c in range(CHUNKS)]
    lives = cut(live[:, None])
    dense = dense_gates(gates, width)

    blank = jnp.zeros((8, width), F32)
    halo, start = blank, blank
    halos, starts, boths, saves, mixes, norms, scales1 = [], [], [], [], [], [], []
    for c in range(CHUNKS):
        values = wholes[c].astype(F32)
        s1 = lax.rsqrt(jnp.mean(values * values, axis=1, keepdims=True) + EPS)
        normed = (values * s1 * gains[0]).astype(BF16)
        both = matmul(normed, w_in)
        mixed, conv, r, i, state, end = rnn_forward(
            both, halo, start, masks[c], dense, rnn_params
        )
        halos.append(halo)
        starts.append(start)
        halo, start = both[-8:, :width], end
        boths.append(both)
        saves.append((conv, r, i, state))
        mixes.append(mixed)
        norms.append(normed)
        scales1.append(s1)

    outputs, hiddens, gates_up, norms2, gbos, locals_, gms = [], [], [], [], [], [], []
    gain2_total = 0.0
    for c in range(CHUNKS):
        branch = line_scatter(inner_cols(mixes[c], w_out).astype(BF16), "mp", mp)
        middle_mine = in_parts[c].astype(F32) + branch
        middle = line_gather(middle_mine.astype(BF16), "mp", mp).astype(F32)
        s2 = lax.rsqrt(jnp.mean(middle * middle, axis=1, keepdims=True) + EPS)
        normed2 = (middle * s2 * gains[1]).astype(BF16)
        pre = matmul(normed2, w_up)
        gate_pre, up_pre = pre[:, :hidden_width], pre[:, hidden_width:]
        value, slope = gelu_and_slope(gate_pre)
        hidden = (value * up_pre).astype(BF16)
        grad_y = jnp.where(lives[c], cots[c], jnp.zeros((), BF16))
        grad_hidden = matmul(grad_y, w_down)
        pulled = jnp.concatenate(
            [
                (grad_hidden * up_pre * slope).astype(BF16),
                (grad_hidden * value).astype(BF16),
            ],
            axis=1,
        )
        gn2_part = inner_cols(pulled, w_up).astype(BF16)
        gn2_mine = line_scatter(gn2_part, "mp", mp)
        gn2 = line_gather(gn2_mine.astype(BF16), "mp", mp).astype(F32)
        g = gn2 * gains[1]
        mean = jnp.mean(g * middle, axis=1, keepdims=True)
        gbo = (grad_y.astype(F32) + s2 * g - middle * (s2 * s2 * s2 * mean)).astype(BF16)
        gain2_total = gain2_total + jnp.sum(gn2 * (middle * s2), axis=0)
        local = (
            jnp.where(lives[c], cotangent[c * step : (c + 1) * step].astype(F32), 0.0)
            + s2 * (gn2_mine * mine(gains[1]))
            - middle_mine * (s2 * s2 * s2 * mean)
        )
        mlp = line_scatter(inner_cols(hidden, w_down).astype(BF16), "mp", mp)
        outputs.append((middle_mine + mlp).astype(BF16))
        hiddens.append(hidden)
        gates_up.append(pulled)
        norms2.append(normed2)
        gbos.append(gbo)
        locals_.append(local)
        gms.append(matmul(gbo, w_out))
        cots[c] = grad_y

    grad_up = square_scatter(
        inner_rows(jnp.concatenate(norms2), jnp.concatenate(gates_up)).astype(BF16), "dp", dp
    )
    grad_down = square_scatter(
        inner_rows(jnp.concatenate(cots), jnp.concatenate(hiddens)).astype(BF16), "dp", dp
    )
    grad_out = square_scatter(
        inner_rows(jnp.concatenate(gbos), jnp.concatenate(mixes)).astype(BF16), "dp", dp
    )

    back, tail = blank, blank
    pulls, rates, grads_in = [None] * CHUNKS, [None] * CHUNKS, [None] * CHUNKS
    gain1_total, params_total = 0.0, 0.0
    for c in reversed(range(CHUNKS)):
        pull, rate, dparams, back, tail = rnn_backward(
            gms[c], boths[c], halos[c], starts[c], saves[c], tail_masks[c], dense, rnn_params,
            back, tail,
        )
        params_total = params_total + dparams
        pulls[c], rates[c] = pull, rate
        gn1_part = inner_cols(pull, w_in).astype(BF16)
        values = wholes[c].astype(F32)
        scaled = gn1_part.astype(F32) * values
        gain1_total = gain1_total + jnp.sum(scaled * scales1[c], axis=0)
        dots = jnp.sum(scaled * gains[0], axis=1).reshape(8, -1)
        mean = (line_sum(dots, "mp", mp) / features).reshape(-1, 1)
        gn1_mine = line_scatter(gn1_part, "mp", mp)
        s1 = scales1[c]
        grad = (
            locals_[c]
            + s1 * (gn1_mine * mine(gains[0]))
            - in_parts[c].astype(F32) * (s1 * s1 * s1 * mean)
        )
        grads_in[c] = grad.astype(BF16)

    grad_in = square_scatter(
        inner_rows(jnp.concatenate(norms), jnp.concatenate(pulls)).astype(BF16), "dp", dp
    )
    convs = jnp.concatenate([s[0] for s in saves]).astype(BF16)
    grad_gates = pair_scatter(
        diagonal_blocks(inner_rows(convs, jnp.concatenate(rates)), span), "dp", dp
    )
    grad_params = line_sum(params_total, "dp", dp)
    grad_gain1 = line_sum(line_sum(gain1_total.reshape(8, -1), "dp", dp), "mp", mp)
    grad_gain2 = line_sum(gain2_total.reshape(8, -1), "dp", dp)
    return (
        jnp.concatenate(outputs),
        jnp.concatenate(grads_in),
        jnp.stack([grad_gain1.reshape(-1), grad_gain2.reshape(-1)]),
        grad_params,
        grad_in[:, :width],
        grad_in[:, width:],
        grad_gates[:, :width],
        grad_gates[:, width:],
        grad_up[:, :hidden_width],
        grad_up[:, hidden_width:],
        grad_out.T,
        grad_down.T,
    )


def solution(mesh):
    return jax.shard_map(
        functools.partial(per_device, mesh.shape["dp"], mesh.shape["mp"]),
        mesh=mesh,
        in_specs=(
            P("dp", "mp"),
            P("dp", None),
            P("dp", "mp"),
            P(),
            P(None, "mp"),
            P("dp", "mp"),
            P("dp", "mp"),
            P("dp", "mp"),
            P("dp", "mp"),
            P("dp", "mp"),
            P("dp", "mp"),
            P("mp", "dp"),
            P("mp", "dp"),
        ),
        out_specs=(
            P("dp", "mp"),
            P("dp", "mp"),
            P(),
            P(None, "mp"),
            P("dp", "mp"),
            P("dp", "mp"),
            P("dp", "mp"),
            P("dp", "mp"),
            P("dp", "mp"),
            P("dp", "mp"),
            P("mp", "dp"),
            P("mp", "dp"),
        ),
        check_vma=False,
    )
```

time: 2030 us -> 1040 us (0.51)
  waiting for transfers between devices: 1390 us -> 294 us
  starting transfers between devices: 1.27 us -> 268 us
  local copies, waits for them, and re-layouts: 221 us -> 110 us
  Pallas kernels: 0 us -> 73.2 us
  matrix products: 203 us -> 148 us
  blocking collectives: 45.6 us -> 0 us
    reduce_scatter x8 -> x0, waiting for transfers between devices: 516 us -> none  [the longest x1 144 us: per_device(): lax.psum_scatter(matmul(mixed, full_out), 'mp', scatter_dimension=1, tile...]
    psum x2 -> x0, waiting for transfers between devices: 447 us -> none  [the longest x1 291 us: per_device(): grad_normed2 = lax.psum(normed2_part, 'mp')]
    all_gather x9 -> x0, waiting for transfers between devices: 424 us -> none  [the longest x1 148 us: per_device(): middle = lax.all_gather(middle_local, 'mp', axis=1, tiled=True)]
    ppermute x0 -> x161, waiting for transfers between devices: none -> 294 us  [the longest x24 111 us: line_gather(): left = lax.ppermute(left, axis, [(i + 1, i) for i in range(size - step)])]
    ppermute x0 -> x161, starting transfers between devices: none -> 268 us  [the longest x24 110 us: line_scatter(): lax.ppermute(going.astype(BF16), axis, [(i, i + 1) for i in range(step)])]
    pad x79 -> x0, local copies, waits for them, and re-layouts: 94.2 us -> none  [rnn_core(): unused, state = lax.associative_scan(combine, (decay, drive), axis=0)]
    slice x79 -> x10, local copies, waits for them, and re-layouts: 93.4 us -> 9.5 us  [the longest x3 2.77 us: cut(): return [values[c * step:(c + 1) * step] for c in range(CHUNKS)]]
    pallas_call x0 -> x4, Pallas kernels: none -> 73.2 us  [the longest x2 38.4 us: rnn_backward(): pl.pallas_call(rnn_backward_kernel, out_shape=(jax.ShapeDtypeStruct((coun...]
  transfers between devices with their start and end apart: 20 -> 161, of which waited for: 17 -> 51; matrix products, arithmetic and copies ran while one was open for 16% -> 35% of each run, Pallas kernels for 0% -> 7%
where the time goes in v1:
time: 1040 us; the launch traced here: 1020 us
  waiting for transfers between devices  294 us (28%)
  starting transfers between devices  268 us (26%)
  matrix products  148 us (14%)
  other arithmetic  124 us (12%)
  local copies, waits for them, and re-layouts  110 us (11%)
  Pallas kernels  73.2 us (7%)
    ppermute x24, waiting for transfers between devices, line_gather(): left = lax.ppermute(left, axis, [(i + 1, i) for i in range(size - step)])  111 us
    ppermute x24, starting transfers between devices, line_scatter(): lax.ppermute(going.astype(BF16), axis, [(i, i + 1) for i in range(step)])  110 us
    ppermute x24, waiting for transfers between devices, line_scatter(): lax.ppermute(going.astype(BF16), axis, [(i, i + 1) for i in range(step)])  79.6 us
    dot_general x8, matrix products, matmul(): return jnp.dot(left, right, preferred_element_type=F32)  59.1 us
    ppermute x24, starting transfers between devices, line_gather(): lax.ppermute(right, axis, [(i, i + 1) for i in range(step - 1, size - 1)])  53.6 us
    dot_general x8, matrix products, inner_cols(): lax.dot_general(left, right, (((1,), (1,)), ((), ())), preferred_element_...  49.1 us
    dot_general x5, matrix products, inner_rows(): lax.dot_general(left, right, (((0,), (0,)), ((), ())), preferred_element_...  40.1 us
    pallas_call x2, Pallas kernels, rnn_backward(): pl.pallas_call(rnn_backward_kernel, out_shape=(jax.ShapeDtypeStruct((coun...  38.4 us
  transfers between devices with their start and end apart: 161, of which 51 were waited for; matrix products, arithmetic and copies ran while one was open for 35% of the time, Pallas kernels for 7%

profile of v1, /device:TPU:0, one launch (start us, length us, event | category | flops | bytes accessed | tf_op | source)
XLA Modules:
  0.0 1021.7 jit_solution(8866470868469577319)
XLA Ops:
  29.8 13.4 %collective-permute-done = bf16[512,512]{1,0:T(8,128)(2,1)S(1)} collective-permute-done((bf16[512,512]{1,0:T(8,128)(2,1)}, bf16[512,512]{1,0:T(8,128)(2,1)S(1)}, u32[]{:S(2)}, u32[]{:S(2)}) %collective-permute-start) | collective-permute-done | bytes 524320 | tf_op jit(solution)/shard_map/ppermute | solution.py:67
  93.7 17.4 %rnn_forward.2 = (bf16[512,640]{1,0:T(8,128)(2,1)}, f32[512,640]{1,0:T(8,128)}, f32[512,640]{1,0:T(8,128)}, f32[512,640]{1,0:T(8,128)}, f32[512,640]{1,0:T(8,128)}, /*index=5*/f32[8,640]{1,0:T(8,128)}) custom-call(f32[512,1280]{1,0:T(8,128)} %fusion.157.both_ref, f32[8,640]{1,0:T(8,128)} %broadcast_in_dim.122.halo_ref.start_ref.back_ref.tail_ref, ...), custom_call_target="tpu_custom_call" | custom-call | flops 1677721600 | bytes 9830400 | tf_op jit(solution)/shard_map/rnn_forward/pallas_call | solution.py:290
  120.4 9.7 collective-permute-done.23
  234.3 9.7 collective-permute-done.33
  267.8 17.5 %rnn_forward.3 = (bf16[512,640]{1,0:T(8,128)(2,1)}, f32[512,640]{1,0:T(8,128)}, f32[512,640]{1,0:T(8,128)}, f32[512,640]{1,0:T(8,128)}, f32[512,640]{1,0:T(8,128)}, /*index=5*/f32[8,640]{1,0:T(8,128)}) custom-call(f32[512,1280]{1,0:T(8,128)} %fusion.159.both_ref, f32[8,640]{1,0:T(8,128)} %slice.145.halo_ref, f32[8,640]{1,0:T(8,128)} %get-tuple-element.42.start_ref, ...), custom_call_target="tpu_custom_call" | custom-call | flops 1677721600 | bytes 9830400 | tf_op jit(solution)/shard_map/rnn_forward/pallas_call | solution.py:290
  330.7 8.5 fusion.158
  348.2 9.6 collective-permute-start.98
  364.3 10.3 %collective-permute-done.66 = bf16[512,512]{1,0:T(8,128)(2,1)S(1)} collective-permute-done((bf16[512,512]{1,0:T(8,128)(2,1)S(1)}, bf16[512,512]{1,0:T(8,128)(2,1)S(1)}, u32[]{:S(2)}, u32[]{:S(2)}) %collective-permute-start.66) | collective-permute-done | bytes 524320 | tf_op jit(solution)/shard_map/ppermute | solution.py:94
  399.1 11.0 %multiply_convert_fusion.3 = (bf16[512,1536]{1,0:T(8,128)(2,1)S(1)}, bf16[512,1536]{1,0:T(8,128)(2,1)}, bf16[512,1536]{1,0:T(8,128)(2,1)}) fusion(f32[512,3072]{1,0:T(8,128)} %fusion.158, bf16[512,2048]{1,0:T(8,128)(2,1)S(1)} %copy-done.54, bf16[2048,1536]{0,1:T(8,128)(2,1)} %constant_dynamic-update-slice_fusion.6), kind=kOutput, calls=%fused_computation.108 | convolution fusion | flops 3240099840 | bytes 19398656 | tf_op jit(solution)/shard_map/dot_general | solution.py:23
  410.2 8.6 fusion.76
  502.5 14.4 %collective-permute-done.92 = bf16[512,512]{1,0:T(8,128)(2,1)S(1)} collective-permute-done((bf16[512,512]{1,0:T(8,128)(2,1)S(1)}, bf16[512,512]{1,0:T(8,128)(2,1)S(1)}, u32[]{:S(2)}, u32[]{:S(2)}) %collective-permute-start.92) | collective-permute-done | bytes 524320 | tf_op jit(solution)/shard_map/ppermute | solution.py:66
  523.8 9.7 collective-permute-start.51
  537.7 17.7 %collective-permute-done.96 = bf16[512,512]{1,0:T(8,128)(2,1)S(1)} collective-permute-done((bf16[512,512]{1,0:T(8,128)(2,1)S(1)}, bf16[512,512]{1,0:T(8,128)(2,1)S(1)}, u32[]{:S(2)}, u32[]{:S(2)}) %collective-permute-start.96) | collective-permute-done | bytes 524320 | tf_op jit(solution)/shard_map/ppermute | solution.py:67
  562.4 8.6 fusion.160
  571.0 10.6 %multiply_convert_fusion.1 = (bf16[512,1536]{1,0:T(8,128)(2,1)S(1)}, bf16[512,1536]{1,0:T(8,128)(2,1)}, bf16[512,1536]{1,0:T(8,128)(2,1)}) fusion(f32[512,3072]{1,0:T(8,128)} %fusion.160, bf16[512,2048]{1,0:T(8,128)(2,1)S(1)} %copy-done.56, bf16[2048,1536]{0,1:T(8,128)(2,1)} %constant_dynamic-update-slice_fusion.6), kind=kOutput, calls=%fused_computation.106 | convolution fusion | flops 3240099840 | bytes 19398656 | tf_op jit(solution)/shard_map/dot_general | solution.py:23
  581.5 8.6 fusion.73
  648.9 19.7 %convolution_convert_fusion = bf16[2048,3072]{1,0:T(8,128)(2,1)} fusion(bf16[512,1536]{1,0:T(8,128)(2,1)} %get-tuple-element.81, bf16[512,1536]{1,0:T(8,128)(2,1)} %copy-done.122, bf16[512,1536]{1,0:T(8,128)(2,1)} %get-tuple-element.79, bf16[512,1536]{1,0:T(8,128)(2,1)} %copy-done.121, bf16[512,2048]{1,0:T(8,128)(2,1)} %copy-done.65, ...), kind=kOutput, calls=%fused_computation.2 | convolution fusion | flops 12924747776 | bytes 23068672 | tf_op jit(solution)/shard_map/dot_general | solution.py:27
  709.8 9.8 collective-permute-done.109
  725.9 10.4 %collective-permute-done.113 = bf16[512,512]{1,0:T(8,128)(2,1)S(1)} collective-permute-done((bf16[512,512]{1,0:T(8,128)(2,1)S(1)}, bf16[512,512]{1,0:T(8,128)(2,1)S(1)}, u32[]{:S(2)}, u32[]{:S(2)}) %collective-permute-start.113) | collective-permute-done | bytes 524320 | tf_op jit(solution)/shard_map/ppermute | solution.py:67
  739.5 11.9 %collective-permute-done.114 = bf16[512,512]{1,0:T(8,128)(2,1)S(1)} collective-permute-done((bf16[512,512]{1,0:T(8,128)(2,1)S(1)}, bf16[512,512]{1,0:T(8,128)(2,1)S(1)}, u32[]{:S(2)}, u32[]{:S(2)}) %collective-permute-start.114) | collective-permute-done | bytes 524320 | tf_op jit(solution)/shard_map/ppermute | solution.py:67
  768.5 19.1 %rnn_backward.2 = (bf16[512,1280]{1,0:T(8,128)(2,1)}, bf16[512,1280]{1,0:T(8,128)(2,1)}, f32[8,640]{1,0:T(8,128)}, f32[8,640]{1,0:T(8,128)}, f32[8,640]{1,0:T(8,128)}) custom-call(f32[512,640]{1,0:T(8,128)} %fusion.162.gm_ref, f32[512,1280]{1,0:T(8,128)} %fusion.159.both_ref, f32[8,640]{1,0:T(8,128)} %slice.145.halo_ref, ...), custom_call_target="tpu_custom_call" | custom-call | flops 838860800 | bytes 11796480 | tf_op jit(solution)/shard_map/rnn_backward/pallas_call | solution.py:435
  787.6 19.3 %rnn_backward.3 = (bf16[512,1280]{1,0:T(8,128)(2,1)}, bf16[512,1280]{1,0:T(8,128)(2,1)}, f32[8,640]{1,0:T(8,128)}, f32[8,640]{1,0:T(8,128)}, f32[8,640]{1,0:T(8,128)}) custom-call(f32[512,640]{1,0:T(8,128)} %fusion.161.gm_ref, f32[512,1280]{1,0:T(8,128)} %fusion.157.both_ref, f32[8,640]{1,0:T(8,128)} %broadcast_in_dim.122.halo_ref.start_ref.back_ref.tail_ref, ...), custom_call_target="tpu_custom_call" | custom-call | flops 838860800 | bytes 11796480 | tf_op jit(solution)/shard_map/rnn_backward/pallas_call | solution.py:435
  947.2 12.9 %collective-permute-start.117 = (bf16[512,512]{1,0:T(8,128)(2,1)S(1)}, bf16[512,512]{1,0:T(8,128)(2,1)S(1)}, u32[]{:S(2)}, u32[]{:S(2)}) collective-permute-start(bf16[512,512]{1,0:T(8,128)(2,1)S(1)} %copy-done.77), channel_id=1, source_target_pairs={{0,1},{1,2},{2,3},{4,5},{5,6},{6,7},{8,9},{9,10},{10,11},{12,13},{... | collective-permute-start | bytes 1572872 | tf_op jit(solution)/shard_map/ppermute | solution.py:90
  992.9 23.8 %collective-permute-done.151 = bf16[256,3072]{1,0:T(8,128)(2,1)S(1)} collective-permute-done((bf16[256,3072]{1,0:T(8,128)(2,1)S(1)}, bf16[256,3072]{1,0:T(8,128)(2,1)S(1)}, u32[]{:S(2)}, u32[]{:S(2)}) %collective-permute-start.151) | collective-permute-done | bytes 1572896 | tf_op jit(solution)/shard_map/ppermute | solution.py:180
  (821 shorter events, 705.1 us)
Async XLA Ops:
  4.2 39.6 %collective-permute-start.6 = (bf16[256,1280]{1,0:T(8,128)(2,1)}, bf16[256,1280]{1,0:T(8,128)(2,1)}, u32[]{:S(2)}, u32[]{:S(2)}) collective-permute-start(bf16[256,1280]{1,0:T(8,128)(2,1)} %constant_dynamic-update-slice_fusion.40), channel_id=1, source_target_pairs={{0,8},{4,12},{8,0},{12,4},{16,24},{20,28},{24,16},{28,20},{1,9},{5... | collective-permute-start | bytes 1966088 | tf_op jit(solution)/shard_map/ppermute | solution.py:148
  7.2 40.0 %collective-permute-start.7 = (bf16[256,1280]{1,0:T(8,128)(2,1)}, bf16[256,1280]{1,0:T(8,128)(2,1)}, u32[]{:S(2)}, u32[]{:S(2)}) collective-permute-start(bf16[256,1280]{1,0:T(8,128)(2,1)} %constant_dynamic-update-slice_fusion.40), channel_id=1, source_target_pairs={{0,16},{4,20},{8,24},{12,28},{16,0},{20,4},{24,8},{28,12},{1,17},{... | collective-permute-start | bytes 1966088 | tf_op jit(solution)/shard_map/ppermute | solution.py:149
  8.7 54.1 %collective-permute-start.9 = (bf16[256,1280]{1,0:T(8,128)(2,1)}, bf16[256,1280]{1,0:T(8,128)(2,1)}, u32[]{:S(2)}, u32[]{:S(2)}) collective-permute-start(bf16[256,1280]{1,0:T(8,128)(2,1)} %constant_dynamic-update-slice_fusion.40), channel_id=1, source_target_pairs={{0,4},{4,0},{8,12},{12,8},{16,20},{20,16},{24,28},{28,24},{1,5},{5... | collective-permute-start | bytes 1966088 | tf_op jit(solution)/shard_map/ppermute | solution.py:154
  151.8 43.8 %collective-permute-start.38 = (bf16[256,3072]{1,0:T(8,128)(2,1)}, bf16[256,3072]{1,0:T(8,128)(2,1)}, u32[]{:S(2)}, u32[]{:S(2)}) collective-permute-start(bf16[256,3072]{1,0:T(8,128)(2,1)} %pad_maximum_fusion), channel_id=1, source_target_pairs={{0,4},{4,0},{8,12},{12,8},{16,20},{20,16},{24,28},{28,24},{1,5},{5... | collective-permute-start | bytes 4718600 | tf_op jit(solution)/shard_map/ppermute | solution.py:154
  195.6 49.8 %collective-permute-start.39 = (bf16[256,3072]{1,0:T(8,128)(2,1)}, bf16[256,3072]{1,0:T(8,128)(2,1)S(1)}, u32[]{:S(2)}, u32[]{:S(2)}) collective-permute-start(bf16[256,3072]{1,0:T(8,128)(2,1)} %collective-permute-done.35), channel_id=1, source_target_pairs={{0,4},{4,0},{8,12},{12,8},{16,20},{20,16},{24,28},{28,24},{1,5},{5... | collective-permute-start | bytes 4718600 | tf_op jit(solution)/shard_map/ppermute | solution.py:154
  244.0 44.5 %collective-permute-start.32 = (bf16[512,512]{1,0:T(8,128)(2,1)}, bf16[512,512]{1,0:T(8,128)(2,1)}, u32[]{:S(2)}, u32[]{:S(2)}) collective-permute-start(bf16[512,512]{1,0:T(8,128)(2,1)} %collective-permute-done.31), channel_id=1, source_target_pairs={{2,3},{6,7},{10,11},{14,15},{18,19},{22,23},{26,27},{30,31}} | collective-permute-start | bytes 1572872 | tf_op jit(solution)/shard_map/ppermute | solution.py:66
  245.4 50.5 %collective-permute-start.34 = (bf16[512,512]{1,0:T(8,128)(2,1)}, bf16[512,512]{1,0:T(8,128)(2,1)}, u32[]{:S(2)}, u32[]{:S(2)}) collective-permute-start(bf16[512,512]{1,0:T(8,128)(2,1)} %collective-permute-done.33), channel_id=1, source_target_pairs={{1,0},{5,4},{9,8},{13,12},{17,16},{21,20},{25,24},{29,28}} | collective-permute-start | bytes 1572872 | tf_op jit(solution)/shard_map/ppermute | solution.py:67
  248.0 78.0 %collective-permute-start.41 = (bf16[256,3072]{1,0:T(8,128)(2,1)}, bf16[256,3072]{1,0:T(8,128)(2,1)S(1)}, u32[]{:S(2)}, u32[]{:S(2)}) collective-permute-start(bf16[256,3072]{1,0:T(8,128)(2,1)} %collective-permute-done.37), channel_id=1, source_target_pairs={{0,4},{4,0},{8,12},{12,8},{16,20},{20,16},{24,28},{28,24},{1,5},{5... | collective-permute-start | bytes 4718600 | tf_op jit(solution)/shard_map/ppermute | solution.py:154
  255.3 52.4 %collective-permute-start.80 = (bf16[512,512]{1,0:T(8,128)(2,1)S(1)}, bf16[512,512]{1,0:T(8,128)(2,1)}, u32[]{:S(2)}, u32[]{:S(2)}) collective-permute-start(bf16[512,512]{1,0:T(8,128)(2,1)S(1)} %get-tuple-element.44), channel_id=1, source_target_pairs={{0,1},{1,2},{2,3},{4,5},{5,6},{6,7},{8,9},{9,10},{10,11},{12,13},{... | collective-permute-start | bytes 1572872 | tf_op jit(solution)/shard_map/ppermute | solution.py:66
  257.5 50.8 %collective-permute-start.79 = (bf16[512,512]{1,0:T(8,128)(2,1)S(1)}, bf16[512,512]{1,0:T(8,128)(2,1)}, u32[]{:S(2)}, u32[]{:S(2)}) collective-permute-start(bf16[512,512]{1,0:T(8,128)(2,1)S(1)} %get-tuple-element.44), channel_id=1, source_target_pairs={{1,0},{2,1},{3,2},{5,4},{6,5},{7,6},{9,8},{10,9},{11,10},{13,12},{... | collective-permute-start | bytes 1572872 | tf_op jit(solution)/shard_map/ppermute | solution.py:67
  317.5 45.9 %collective-permute-start.63 = (bf16[512,512]{1,0:T(8,128)(2,1)S(1)}, bf16[512,512]{1,0:T(8,128)(2,1)S(1)}, u32[]{:S(2)}, u32[]{:S(2)}) collective-permute-start(bf16[512,512]{1,0:T(8,128)(2,1)S(1)} %get-tuple-element.124), channel_id=1, source_target_pairs={{0,1},{1,2},{2,3},{4,5},{5,6},{6,7},{8,9},{9,10},{10,11},{12,13},{... | collective-permute-start | bytes 1572872 | tf_op jit(solution)/shard_map/ppermute | solution.py:90
  381.4 54.4 %collective-permute-start.68 = (bf16[512,512]{1,0:T(8,128)(2,1)}, bf16[512,512]{1,0:T(8,128)(2,1)}, u32[]{:S(2)}, u32[]{:S(2)}) collective-permute-start(bf16[512,512]{1,0:T(8,128)(2,1)} %get-tuple-element.77), channel_id=1, source_target_pairs={{0,1},{1,2},{2,3},{4,5},{5,6},{6,7},{8,9},{9,10},{10,11},{12,13},{... | collective-permute-start | bytes 1572872 | tf_op jit(solution)/shard_map/ppermute | solution.py:66
  392.6 44.0 %collective-permute-start.67 = (bf16[512,512]{1,0:T(8,128)(2,1)}, bf16[512,512]{1,0:T(8,128)(2,1)}, u32[]{:S(2)}, u32[]{:S(2)}) collective-permute-start(bf16[512,512]{1,0:T(8,128)(2,1)} %get-tuple-element.77), channel_id=1, source_target_pairs={{1,0},{2,1},{3,2},{5,4},{6,5},{7,6},{9,8},{10,9},{11,10},{13,12},{... | collective-permute-start | bytes 1572872 | tf_op jit(solution)/shard_map/ppermute | solution.py:67
  393.9 40.5 %collective-permute-start.101 = (bf16[512,512]{1,0:T(8,128)(2,1)}, bf16[512,512]{1,0:T(8,128)(2,1)}, u32[]{:S(2)}, u32[]{:S(2)}) collective-permute-start(bf16[512,512]{1,0:T(8,128)(2,1)} %collective-permute-done.97), channel_id=1, source_target_pairs={{1,0},{2,1},{5,4},{6,5},{9,8},{10,9},{13,12},{14,13},{17,16},{18,1... | collective-permute-start | bytes 1572872 | tf_op jit(solution)/shard_map/ppermute | solution.py:67
  395.2 42.7 %collective-permute-start.100 = (bf16[512,512]{1,0:T(8,128)(2,1)}, bf16[512,512]{1,0:T(8,128)(2,1)}, u32[]{:S(2)}, u32[]{:S(2)}) collective-permute-start(bf16[512,512]{1,0:T(8,128)(2,1)} %collective-permute-done.99), channel_id=1, source_target_pairs={{2,3},{6,7},{10,11},{14,15},{18,19},{22,23},{26,27},{30,31}} | collective-permute-start | bytes 1572872 | tf_op jit(solution)/shard_map/ppermute | solution.py:66
  435.8 40.5 %collective-permute-start.69 = (bf16[512,512]{1,0:T(8,128)(2,1)}, bf16[512,512]{1,0:T(8,128)(2,1)S(1)}, u32[]{:S(2)}, u32[]{:S(2)}) collective-permute-start(bf16[512,512]{1,0:T(8,128)(2,1)} %collective-permute-done.68), channel_id=1, source_target_pairs={{1,2},{2,3},{5,6},{6,7},{9,10},{10,11},{13,14},{14,15},{17,18},{18... | collective-permute-start | bytes 1572872 | tf_op jit(solution)/shard_map/ppermute | solution.py:66
  436.6 40.5 %collective-permute-start.71 = (bf16[512,512]{1,0:T(8,128)(2,1)}, bf16[512,512]{1,0:T(8,128)(2,1)S(1)}, u32[]{:S(2)}, u32[]{:S(2)}) collective-permute-start(bf16[512,512]{1,0:T(8,128)(2,1)} %collective-permute-done.67), channel_id=1, source_target_pairs={{1,0},{2,1},{5,4},{6,5},{9,8},{10,9},{13,12},{14,13},{17,16},{18,1... | collective-permute-start | bytes 1572872 | tf_op jit(solution)/shard_map/ppermute | solution.py:67
  477.0 42.7 %collective-permute-start.72 = (bf16[512,512]{1,0:T(8,128)(2,1)S(1)}, bf16[512,512]{1,0:T(8,128)(2,1)S(1)}, u32[]{:S(2)}, u32[]{:S(2)}) collective-permute-start(bf16[512,512]{1,0:T(8,128)(2,1)S(1)} %collective-permute-done.71), channel_id=1, source_target_pairs={{1,0},{5,4},{9,8},{13,12},{17,16},{21,20},{25,24},{29,28}} | collective-permute-start | bytes 1572872 | tf_op jit(solution)/shard_map/ppermute | solution.py:67
  523.8 160.0 %collective-permute-start.51 = (bf16[512,512]{1,0:T(8,128)(2,1)}, bf16[512,512]{1,0:T(8,128)(2,1)}, u32[]{:S(2)}, u32[]{:S(2)}) collective-permute-start(bf16[512,512]{1,0:T(8,128)(2,1)} %get-tuple-element.112), channel_id=1, source_target_pairs={{0,1},{1,2},{2,3},{4,5},{5,6},{6,7},{8,9},{9,10},{10,11},{12,13},{... | collective-permute-start | bytes 1572872 | tf_op jit(solution)/shard_map/ppermute | solution.py:90
  636.1 85.5 %collective-permute-start.157 = (bf16[4,256,1536]{1,2,0:T(8,128)(2,1)}, bf16[4,256,1536]{1,2,0:T(8,128)(2,1)}, u32[]{:S(2)}, u32[]{:S(2)}) collective-permute-start(bf16[4,256,1536]{1,2,0:T(8,128)(2,1)} %bitcast.136), channel_id=1, source_target_pairs={{0,4},{4,0},{8,12},{12,8},{16,20},{20,16},{24,28},{28,24},{1,5},{5... | collective-permute-start | bytes 9437192 | tf_op jit(solution)/shard_map/ppermute | solution.py:169
  703.0 229.6 %collective-permute-start.149 = (bf16[4,256,3072]{2,1,0:T(8,128)(2,1)}, bf16[4,256,3072]{2,1,0:T(8,128)(2,1)}, u32[]{:S(2)}, u32[]{:S(2)}) collective-permute-start(bf16[4,256,3072]{2,1,0:T(8,128)(2,1)} %dynamic-slice_bitcast_fusion), channel_id=1, source_target_pairs={{0,4},{4,0},{8,12},{12,8},{16,20},{20,16},{24,28},{28,24},{1,5},{5... | collective-permute-start | bytes 18874376 | tf_op jit(solution)/shard_map/ppermute | solution.py:169
  725.4 156.0 %collective-permute-start.158 = (bf16[256,1536]{0,1:T(8,128)(2,1)}, bf16[256,1536]{0,1:T(8,128)(2,1)}, u32[]{:S(2)}, u32[]{:S(2)}) collective-permute-start(bf16[256,1536]{0,1:T(8,128)(2,1)} %dynamic-slice_bitcast_fusion.3), channel_id=1, source_target_pairs={{0,16},{4,12},{8,24},{12,4},{16,0},{20,28},{24,8},{28,20},{1,17},{... | collective-permute-start | bytes 2359304 | tf_op jit(solution)/shard_map/ppermute | solution.py:176
  859.3 50.2 %collective-permute-start.153 = (bf16[4,256,640]{1,2,0:T(8,128)(2,1)}, bf16[4,256,640]{1,2,0:T(8,128)(2,1)S(1)}, u32[]{:S(2)}, u32[]{:S(2)}) collective-permute-start(bf16[4,256,640]{1,2,0:T(8,128)(2,1)} %bitcast.138), channel_id=1, source_target_pairs={{0,4},{4,0},{8,12},{12,8},{16,20},{20,16},{24,28},{28,24},{1,5},{5... | collective-permute-start | bytes 3932168 | tf_op jit(solution)/shard_map/ppermute | solution.py:169
  897.5 42.8 %collective-permute-start.142 = (bf16[4,256,1280]{2,1,0:T(8,128)(2,1)}, bf16[4,256,1280]{2,1,0:T(8,128)(2,1)}, u32[]{:S(2)}, u32[]{:S(2)}) collective-permute-start(bf16[4,256,1280]{2,1,0:T(8,128)(2,1)} %dynamic-slice_bitcast_fusion.1), channel_id=1, source_target_pairs={{0,4},{4,0},{8,12},{12,8},{16,20},{20,16},{24,28},{28,24},{1,5},{5... | collective-permute-start | bytes 7864328 | tf_op jit(solution)/shard_map/ppermute | solution.py:169
  (269 other events, 5166.4 us)

commit v2 on v1

--- a/solution.py
+++ b/solution.py
@@ -459,6 +459,611 @@
     )(gm, both, halo, start, conv, r, i, state, mask, gates, params, back, tail)
 
 
+MESH = pl.DeviceIdType.MESH
+
+
+class Spread:
+    def __init__(self, place, size, blocks, sent, came):
+        self.place, self.size = place, size
+        self.blocks, self.sent, self.came = blocks, sent, came
+
+    def copy(self, slot, j, way, k):
+        ref = self.blocks.at[slot, j]
+        return pltpu.make_async_remote_copy(
+            src_ref=ref, dst_ref=ref, send_sem=self.sent.at[slot, k],
+            recv_sem=self.came.at[slot, j], device_id={"mp": self.place + way},
+            device_id_type=MESH,
+        )
+
+    def moves(self, s):
+        z, n = self.place, self.size
+        return (
+            ((z - s >= 0) & (z < n - 1), z - s, 1, 2 * s),
+            ((z + s <= n - 1) & (z > 0), z + s, -1, 2 * s + 1),
+        )
+
+    def step(self, slot, s):
+        for valid, j, way, k in self.moves(s):
+
+            @pl.when(valid)
+            def _(j=j, way=way, k=k):
+                copy = self.copy(slot, j, way, k)
+                if s > 0:
+                    copy.wait_recv()
+                copy.start()
+
+    def finish(self, slot):
+        z, n = self.place, self.size
+
+        @pl.when(z == 0)
+        def _():
+            for j in range(1, n):
+                self.copy(slot, j, 1, 0).wait_recv()
+
+        @pl.when(z == n - 1)
+        def _():
+            for j in range(n - 1):
+                self.copy(slot, j, -1, 0).wait_recv()
+
+    def drain(self, slot):
+        for s in range(self.size - 1):
+            for valid, j, way, k in self.moves(s):
+
+                @pl.when(valid)
+                def _(j=j, way=way, k=k):
+                    self.copy(slot, j, way, k).wait_send()
+
+
+class Fold:
+    def __init__(self, place, size, parts, rights, lefts, sent, came_right, came_left):
+        self.place, self.size = place, size
+        self.parts, self.rights, self.lefts = parts, rights, lefts
+        self.sent, self.came_right, self.came_left = sent, came_right, came_left
+
+    def right(self, slot, j, k):
+        return pltpu.make_async_remote_copy(
+            src_ref=self.parts.at[slot, j], dst_ref=self.rights.at[slot, k],
+            send_sem=self.sent.at[slot, j], recv_sem=self.came_right.at[slot, k],
+            device_id={"mp": self.place + 1}, device_id_type=MESH,
+        )
+
+    def left(self, slot, j, k):
+        return pltpu.make_async_remote_copy(
+            src_ref=self.parts.at[slot, j], dst_ref=self.lefts.at[slot, k],
+            send_sem=self.sent.at[slot, j], recv_sem=self.came_left.at[slot, k],
+            device_id={"mp": self.place - 1}, device_id_type=MESH,
+        )
+
+    def clear(self):
+        for slot in range(self.parts.shape[0]):
+            last = self.size - 2
+            blank = jnp.zeros(self.rights.shape[2:], BF16)
+            self.rights[slot, last] = blank
+            self.lefts[slot, last] = blank
+
+    def start(self, slot):
+        z, n = self.place, self.size
+
+        @pl.when(z == 0)
+        def _():
+            for j in reversed(range(1, n)):
+                self.right(slot, j, n - 1 - j).start()
+
+        @pl.when(z == n - 1)
+        def _():
+            for j in range(n - 1):
+                self.left(slot, j, j).start()
+
+    def step(self, slot, s):
+        z, n = self.place, self.size
+        back = n - 1 - z
+
+        @pl.when((z >= 1) & (z <= n - 2) & (s >= z))
+        def _():
+            j = n - 1 + z - s
+            self.right(slot, j, s - 1).wait_recv()
+            self.add(slot, j, self.rights, s - 1)
+            self.right(slot, j, s).start()
+
+        @pl.when((back >= 1) & (back <= n - 2) & (s >= back))
+        def _():
+            j = s - back
+            self.left(slot, j, s - 1).wait_recv()
+            self.add(slot, j, self.lefts, s - 1)
+            self.left(slot, j, s).start()
+
+    def add(self, slot, j, came, k):
+        self.parts[slot, j] = (
+            self.parts[slot, j].astype(F32) + came[slot, k].astype(F32)
+        ).astype(BF16)
+
+    def finish(self, slot):
+        z, n = self.place, self.size
+
+        @pl.when(z >= 1)
+        def _():
+            self.right(slot, z, n - 2).wait_recv()
+
+        @pl.when(z <= n - 2)
+        def _():
+            self.left(slot, z, n - 2).wait_recv()
+
+    def total(self, slot, rows):
+        z, n = self.place, self.size
+        return (
+            self.parts[slot, z, rows, :].astype(F32)
+            + self.rights[slot, n - 2, rows, :].astype(F32)
+            + self.lefts[slot, n - 2, rows, :].astype(F32)
+        )
+
+    def drain(self, slot):
+        for j in range(self.size):
+
+            @pl.when(j != self.place)
+            def _(j=j):
+                self.right(slot, j, 0).wait_send()
+
+
+def partners(d):
+    core, x, y = lax.rem(d, 2), lax.rem(lax.div(d, 2), 2), lax.div(d, 4)
+    return core, d + 1 - 2 * core, d + 2 - 4 * x, d + 4 - 8 * y
+
+
+class Square:
+    def __init__(self, d, shard, whole, sent, came, own):
+        self.d, self.shard, self.whole = d, shard, whole
+        self.sent, self.came, self.own = sent, came, own
+        self.core, self.by_core, self.by_x, self.by_y = partners(d)
+
+    def rows(self, d):
+        count = self.shard.shape[0]
+        return self.whole.at[pl.ds(pl.multiple_of(d * count, count), count), :]
+
+    def copy(self, src, origin, target, sent, came):
+        return pltpu.make_async_remote_copy(
+            src_ref=src, dst_ref=self.rows(origin), send_sem=self.sent.at[sent],
+            recv_sem=self.came.at[came], device_id={"dp": target}, device_id_type=MESH,
+        )
+
+    def local(self):
+        return pltpu.make_async_copy(self.shard, self.rows(self.d), self.own)
+
+    def far(self):
+        return partners(self.by_x)[3]
+
+    def first(self):
+        return (
+            self.copy(self.shard, self.d, self.by_x, 0, 2),
+            self.copy(self.shard, self.d, self.by_y, 1, 4),
+            self.copy(self.shard, self.d, self.by_core, 2, 1),
+        )
+
+    def start(self):
+        for copy in self.first():
+            copy.start()
+        self.local().start()
+
+    def step_one(self):
+        x_rows, y_rows = self.rows(self.by_x), self.rows(self.by_y)
+        by_x = self.copy(x_rows, self.by_x, self.by_core, 3, 2)
+        by_y = self.copy(y_rows, self.by_y, self.by_core, 4, 4)
+        by_x.wait_recv()
+
+        @pl.when(self.core == 0)
+        def _():
+            self.copy(x_rows, self.by_x, self.by_y, 5, 6).start()
+
+        self.copy(x_rows, self.by_x, self.by_core, 3, 3).start()
+        by_y.wait_recv()
+
+        @pl.when(self.core == 1)
+        def _():
+            self.copy(y_rows, self.by_y, self.by_x, 5, 6).start()
+
+        self.copy(y_rows, self.by_y, self.by_core, 4, 5).start()
+
+    def step_two(self):
+        far = self.far()
+        rows = self.rows(far)
+        self.copy(rows, far, self.by_core, 6, 6).wait_recv()
+        self.copy(rows, far, self.by_core, 6, 7).start()
+
+    def finish(self):
+        for k in (1, 3, 5, 7):
+            self.copy(self.shard, self.d, self.by_core, 0, k).wait_recv()
+        self.local().wait()
+
+    def drain(self):
+        for k in range(7):
+            self.copy(self.shard, self.d, self.by_core, k, 0).wait_send()
+
+
+def middle_kernel(dp, mp, chunks, *refs):
+    (
+        mixed_ref, x_ref, cot_ref, live_ref, gains_ref, mine_ref, wout_ref, up_ref, down_ref,
+        output_ref, gm_ref, gbo_ref, local_ref, hidden_ref, pulled_ref, norm_ref, grady_ref,
+        gain_ref,
+        w_up, w_down, cots, mids, gn2s, mid_mine, gn2_mine,
+        parts1, rights1, lefts1, parts2, rights2, lefts2, parts3, rights3, lefts3,
+        norm, hidden, pulled, gbo, gm, local, out,
+        spread_sent, spread_came, fold_sent, fold_right, fold_left,
+        square_sent, square_came, square_own, load_sem, store_sem,
+    ) = refs
+    step, part = x_ref.shape[0] // chunks, x_ref.shape[1]
+    features = part * mp
+    hidden_width = w_down.shape[1]
+    z, d = lax.axis_index("mp"), lax.axis_index("dp")
+    square = dp == 8
+
+    folds = [
+        Fold(z, mp, p, r, l, fold_sent.at[k], fold_right.at[k], fold_left.at[k])
+        for k, (p, r, l) in enumerate(
+            ((parts1, rights1, lefts1), (parts2, rights2, lefts2), (parts3, rights3, lefts3))
+        )
+    ]
+    rs1, rs2, rs3 = folds
+    ag2, ag3, ag4 = [
+        Spread(z, mp, b, spread_sent.at[k], spread_came.at[k])
+        for k, b in enumerate((cots, mids, gn2s))
+    ]
+    for fold in folds:
+        fold.clear()
+
+    barrier = pltpu.get_barrier_semaphore()
+
+    @pl.when(z > 0)
+    def _():
+        pl.semaphore_signal(barrier, inc=1, device_id={"mp": z - 1}, device_id_type=MESH)
+
+    @pl.when(z < mp - 1)
+    def _():
+        pl.semaphore_signal(barrier, inc=1, device_id={"mp": z + 1}, device_id_type=MESH)
+
+    count = jnp.where((z > 0) & (z < mp - 1), 2, 1)
+    if square:
+        for other in partners(d)[1:]:
+            pl.semaphore_signal(barrier, inc=1, device_id={"dp": other}, device_id_type=MESH)
+        count = count + 3
+    pl.semaphore_wait(barrier, count)
+
+    if square:
+        squares = [
+            Square(d, up_ref, w_up, square_sent.at[0], square_came.at[0], square_own.at[0]),
+            Square(d, down_ref, w_down, square_sent.at[1], square_came.at[1], square_own.at[1]),
+        ]
+        for item in squares:
+            item.start()
+    else:
+        loads = [
+            pltpu.make_async_copy(up_ref, w_up, square_own.at[0]),
+            pltpu.make_async_copy(down_ref, w_down, square_own.at[1]),
+        ]
+        for item in loads:
+            item.start()
+
+    def chunk_rows(c):
+        return pl.ds(c * step, step)
+
+    def store(buffer, target, c, k):
+        return pltpu.make_async_copy(buffer, target.at[chunk_rows(c), :], store_sem.at[k])
+
+    def own_cot(c):
+        return pltpu.make_async_copy(cot_ref.at[chunk_rows(c), :], cots.at[c, z], load_sem.at[c])
+
+    for c in range(chunks):
+        own_cot(c).start()
+
+    gain_ref[...] = jnp.zeros_like(gain_ref)
+    tiles = step // TILE
+
+    def fill(fold, slot, left, weights):
+        def body(j):
+            rows = pl.ds(pl.multiple_of(j * part, part), part)
+            fold.parts[slot, j] = inner_cols(left, weights[rows, :]).astype(BF16)
+
+        tile_loop(mp, body)
+
+    def branch(c):
+        fill(rs1, c % 2, mixed_ref[chunk_rows(c), :], wout_ref)
+
+    def join(c):
+        def body(t):
+            rows = rows_at(t, TILE)
+            base = pl.ds(pl.multiple_of(c * step + t * TILE, TILE), TILE)
+            total = x_ref[base, :].astype(F32) + rs1.total(c % 2, rows)
+            mid_mine[c, rows, :] = total
+            mids[c, z, rows, :] = total.astype(BF16)
+
+        tile_loop(tiles, body)
+
+    def stats(c, rows):
+        blocks = [mids[c, j, rows, :].astype(F32) for j in range(mp)]
+        square_sum = sum(jnp.sum(b * b, axis=1, keepdims=True) for b in blocks)
+        return blocks, lax.rsqrt(square_sum / features + EPS)
+
+    def block_cols(j):
+        return slice(j * part, (j + 1) * part)
+
+    def normalise(c):
+        def body(t):
+            rows = rows_at(t, TILE)
+            base = pl.ds(pl.multiple_of(c * step + t * TILE, TILE), TILE)
+            blocks, s2 = stats(c, rows)
+            live = live_ref[base, :][:, 0:1]
+            for j in range(mp):
+                norm[rows, block_cols(j)] = (
+                    blocks[j] * s2 * gains_ref[1:2, block_cols(j)]
+                ).astype(BF16)
+                cots[c, j, rows, :] = (cots[c, j, rows, :].astype(F32) * live).astype(BF16)
+
+        tile_loop(tiles, body)
+
+    def grad_y_copies(c):
+        return [
+            pltpu.make_async_copy(
+                cots.at[c, j], grady_ref.at[chunk_rows(c), pl.ds(j * part, part)],
+                store_sem.at[8 + j],
+            )
+            for j in range(mp)
+        ]
+
+    def mlp_first(c):
+        if c > 0:
+            store(norm, norm_ref, c, 0).wait()
+            store(hidden, hidden_ref, c, 1).wait()
+            store(pulled, pulled_ref, c, 2).wait()
+            for copy in grad_y_copies(c - 1):
+                copy.wait()
+        ag2.drain(c)
+        normalise(c)
+        store(norm, norm_ref, c, 0).start()
+        for copy in grad_y_copies(c):
+            copy.start()
+        size = 256
+
+        def body(t):
+            near = pl.ds(pl.multiple_of(t * size, size), size)
+            off = pl.ds(pl.multiple_of(hidden_width + t * size, size), size)
+            gate = matmul(norm[...], w_up[:, near])
+            up = matmul(norm[...], w_up[:, off])
+            grad = sum(
+                matmul(cots[c, j], w_down[block_cols(j), near]) for j in range(mp)
+            )
+            value, slope = gelu_and_slope(gate)
+            hidden[:, near] = (value * up).astype(BF16)
+            pulled[:, near] = (grad * up * slope).astype(BF16)
+            pulled[:, off] = (grad * value).astype(BF16)
+
+        tile_loop(hidden_width // size, body)
+        store(hidden, hidden_ref, c, 1).start()
+        store(pulled, pulled_ref, c, 2).start()
+
+    def mlp_second(c):
+        slot = c % 2
+        if c > 1:
+            rs3.drain(slot)
+        fill(rs3, slot, pulled[...], w_up)
+        rs3.start(slot)
+
+    def mlp_third(c):
+        slot = c % 2
+        if c > 1:
+            rs2.drain(slot)
+        fill(rs2, slot, hidden[...], w_down)
+
+    def gather_grad(c):
+        slot = c % 2
+
+        def body(t):
+            rows = rows_at(t, TILE)
+            total = rs3.total(slot, rows)
+            gn2_mine[slot, rows, :] = total
+            gn2s[slot, z, rows, :] = total.astype(BF16)
+
+        tile_loop(tiles, body)
+        ag4.step(slot, 0)
+
+    def norm_back(c):
+        slot = c % 2
+        if c > 0:
+            store(gbo, gbo_ref, c, 3).wait()
+            store(local, local_ref, c, 4).wait()
+            store(gm, gm_ref, c, 5).wait()
+
+        def body(t):
+            rows = rows_at(t, TILE)
+            blocks, s2 = stats(c, rows)
+            grads = [gn2s[slot, j, rows, :].astype(F32) for j in range(mp)]
+            scaled = [grads[j] * gains_ref[1:2, block_cols(j)] for j in range(mp)]
+            mean = (
+                sum(jnp.sum(scaled[j] * blocks[j], axis=1, keepdims=True) for j in range(mp))
+                / features
+            )
+            fall = s2 * s2 * s2 * mean
+            for j in range(mp):
+                grad_y = cots[c, j, rows, :].astype(F32)
+                gbo[rows, block_cols(j)] = (
+                    grad_y + s2 * scaled[j] - blocks[j] * fall
+                ).astype(BF16)
+                gain_ref[:, block_cols(j)] += jnp.sum(
+                    (grads[j] * (blocks[j] * s2)).reshape(-1, 8, part), axis=0
+                )
+            local[rows, :] = (
+                cots[c, z, rows, :].astype(F32)
+                + s2 * (gn2_mine[slot, rows, :] * mine_ref[1:2, :])
+                - mid_mine[c, rows, :] * fall
+            )
+
+        tile_loop(tiles, body)
+        gm[...] = matmul(gbo[...], wout_ref[...])
+        store(gbo, gbo_ref, c, 3).start()
+        store(local, local_ref, c, 4).start()
+        store(gm, gm_ref, c, 5).start()
+
+    def make_output(c):
+        if c > 0:
+            store(out, output_ref, c, 6).wait()
+
+        def body(t):
+            rows = rows_at(t, TILE)
+            out[rows, :] = (mid_mine[c, rows, :] + rs2.total(c % 2, rows)).astype(BF16)
+
+        tile_loop(tiles, body)
+        store(out, output_ref, c, 6).start()
+
+    def has(c):
+        return 0 <= c < chunks
+
+    for r in range(chunks + 3):
+        if has(r):
+            if r > 1:
+                rs1.drain(r % 2)
+            branch(r)
+            rs1.start(r % 2)
+            own_cot(r).wait()
+        if has(r - 1):
+            ag3.step(r - 1, 0)
+        if has(r):
+            ag2.step(r, 0)
+        if has(r - 3):
+            gather_grad(r - 3)
+            rs2.start((r - 3) % 2)
+        if r == 0 and square:
+            squares[0].step_one()
+        if r == 1 and square:
+            squares[1].step_one()
+        if r == 2:
+            if square:
+                squares[0].step_two()
+                squares[1].step_two()
+                for item in squares:
+                    item.finish()
+            else:
+                for item in loads:
+                    item.wait()
+        if has(r - 2):
+            mlp_first(r - 2)
+        for s in range(1, mp - 1):
+            if has(r):
+                rs1.step(r % 2, s)
+            if has(r - 1):
+                ag3.step(r - 1, s)
+            if has(r - 3):
+                ag4.step((r - 3) % 2, s)
+            if has(r):
+                ag2.step(r, s)
+            if has(r - 3):
+                rs2.step((r - 3) % 2, s)
+            if s == 1 and has(r - 2):
+                mlp_second(r - 2)
+        if has(r):
+            rs1.finish(r % 2)
+            join(r)
+        if has(r - 1):
+            ag3.finish(r - 1)
+        if has(r):
+            ag2.finish(r)
+        if has(r - 2):
+            rs3.step((r - 2) % 2, 1)
+            mlp_third(r - 2)
+        if has(r - 3):
+            ag4.finish((r - 3) % 2)
+            norm_back(r - 3)
+            ag4.drain((r - 3) % 2)
+        if has(r - 2):
+            for s in range(2, mp - 1):
+                rs3.step((r - 2) % 2, s)
+        if has(r - 3):
+            rs2.finish((r - 3) % 2)
+            make_output(r - 3)
+        if has(r - 2):
+            rs3.finish((r - 2) % 2)
+
+    last = chunks - 1
+    for k, (buffer, target) in enumerate(
+        (
+            (norm, norm_ref), (hidden, hidden_ref), (pulled, pulled_ref), (gbo, gbo_ref),
+            (local, local_ref), (gm, gm_ref), (out, output_ref),
+        )
+    ):
+        store(buffer, target, last, k).wait()
+    for copy in grad_y_copies(last):
+        copy.wait()
+    for c in range(chunks):
+        ag3.drain(c)
+    for slot in range(2):
+        for fold in folds:
+            fold.drain(slot)
+    if square:
+        for item in squares:
+            item.drain()
+
+
+def middle(dp, mp, chunks, mixed, inputs, cotangent, live, gains, mine, w_out, up, down):
+    count, part = inputs.shape
+    width, hidden_width = mixed.shape[1], down.shape[1]
+    step, features = count // chunks, part * mp
+
+    def fold_buffers():
+        return [
+            pltpu.VMEM((2, mp, step, part), BF16),
+            pltpu.VMEM((2, mp - 1, step, part), BF16),
+            pltpu.VMEM((2, mp - 1, step, part), BF16),
+        ]
+
+    dma = pltpu.SemaphoreType.DMA
+    any_, vmem = pl.BlockSpec(memory_space=pl.ANY), pl.BlockSpec(memory_space=pltpu.VMEM)
+    return pl.pallas_call(
+        functools.partial(middle_kernel, dp, mp, chunks),
+        in_specs=[vmem, vmem, any_, vmem, vmem, vmem, vmem, any_, any_],
+        out_specs=[any_] * 8 + [vmem],
+        out_shape=(
+            jax.ShapeDtypeStruct((count, part), BF16),
+            jax.ShapeDtypeStruct((count, width), F32),
+            jax.ShapeDtypeStruct((count, features), BF16),
+            jax.ShapeDtypeStruct((count, part), F32),
+            jax.ShapeDtypeStruct((count, hidden_width), BF16),
+            jax.ShapeDtypeStruct((count, 2 * hidden_width), BF16),
+            jax.ShapeDtypeStruct((count, features), BF16),
+            jax.ShapeDtypeStruct((count, features), BF16),
+            jax.ShapeDtypeStruct((8, features), F32),
+        ),
+        scratch_shapes=[
+            pltpu.VMEM((features, 2 * hidden_width), BF16),
+            pltpu.VMEM((features, hidden_width), BF16),
+            pltpu.VMEM((chunks, mp, step, part), BF16),
+            pltpu.VMEM((chunks, mp, step, part), BF16),
+            pltpu.VMEM((2, mp, step, part), BF16),
+            pltpu.VMEM((chunks, step, part), F32),
+            pltpu.VMEM((2, step, part), F32),
+        ]
+        + fold_buffers() + fold_buffers() + fold_buffers()
+        + [
+            pltpu.VMEM((step, features), BF16),
+            pltpu.VMEM((step, hidden_width), BF16),
+            pltpu.VMEM((step, 2 * hidden_width), BF16),
+            pltpu.VMEM((step, features), BF16),
+            pltpu.VMEM((step, width), F32),
+            pltpu.VMEM((step, part), F32),
+            pltpu.VMEM((step, part), BF16),
+            dma((3, chunks, 2 * mp)),
+            dma((3, chunks, mp)),
+            dma((3, 2, mp)),
+            dma((3, 2, mp)),
+            dma((3, 2, mp)),
+            dma((2, 8)),
+            dma((2, 8)),
+            dma((2,)),
+            dma((chunks,)),
+            dma((12,)),
+        ],
+        compiler_params=pltpu.CompilerParams(
+            collective_id=0, has_side_effects=True, vmem_limit_bytes=62 * 1024 * 1024
+        ),
+        name="middle",
+    )(mixed, inputs, cotangent, live, gains, mine, w_out, up, down)
+
+
 def make_masks(row_lengths, count):
     ends = jnp.cumsum(row_lengths)
     places = jnp.arange(-TAPS, count, dtype=jnp.int32)
@@ -511,26 +1116,21 @@
     gates = pair_gather(jnp.concatenate([recur_gate, input_gate], axis=1), "dp", dp)
     w_in = square_gather(jnp.concatenate([rnn_in, branch_gate], axis=1), "dp", dp)
     w_out = square_gather(after(rnn_out.T, w_in), "dp", dp)
-    w_up = square_gather(
-        after(jnp.concatenate([mlp_gate, mlp_up], axis=1), w_out), "dp", dp
-    )
-    w_down = square_gather(after(mlp_down.T, w_up), "dp", dp)
+    up = jnp.concatenate([mlp_gate, mlp_up], axis=1)
+    down = mlp_down.T
+    if dp != 8:
+        up, down = square_gather(up, "dp", dp), square_gather(down, "dp", dp)
 
     in_parts = cut(inputs)
     wholes = []
     for c in range(CHUNKS):
         source = in_parts[c] if c == 0 else after(in_parts[c], wholes[-1])
         wholes.append(line_gather(source, "mp", mp))
-    cots = []
-    cot_parts = cut(cotangent)
-    for c in range(CHUNKS):
-        cots.append(line_gather(after(cot_parts[c], wholes[-1], *cots[-1:]), "mp", mp))
-
     mask, live = make_masks(lengths[0], count)
     masks = cut(mask)
     mask_tail = jnp.concatenate([mask, jnp.zeros((8, LANES), F32)], axis=0)
     tail_masks = [mask_tail[c * step : (c + 1) * step + 8] for c in range(CHUNKS)]
-    lives = cut(live[:, None])
+    live = jnp.broadcast_to(live[:, None], (count, LANES)).astype(F32)
     dense = dense_gates(gates, width)
 
     blank = jnp.zeros((8, width), F32)
@@ -553,57 +1153,20 @@
         norms.append(normed)
         scales1.append(s1)
 
-    outputs, hiddens, gates_up, norms2, gbos, locals_, gms = [], [], [], [], [], [], []
-    gain2_total = 0.0
-    for c in range(CHUNKS):
-        branch = line_scatter(inner_cols(mixes[c], w_out).astype(BF16), "mp", mp)
-        middle_mine = in_parts[c].astype(F32) + branch
-        middle = line_gather(middle_mine.astype(BF16), "mp", mp).astype(F32)
-        s2 = lax.rsqrt(jnp.mean(middle * middle, axis=1, keepdims=True) + EPS)
-        normed2 = (middle * s2 * gains[1]).astype(BF16)
-        pre = matmul(normed2, w_up)
-        gate_pre, up_pre = pre[:, :hidden_width], pre[:, hidden_width:]
-        value, slope = gelu_and_slope(gate_pre)
-        hidden = (value * up_pre).astype(BF16)
-        grad_y = jnp.where(lives[c], cots[c], jnp.zeros((), BF16))
-        grad_hidden = matmul(grad_y, w_down)
-        pulled = jnp.concatenate(
-            [
-                (grad_hidden * up_pre * slope).astype(BF16),
-                (grad_hidden * value).astype(BF16),
-            ],
-            axis=1,
-        )
-        gn2_part = inner_cols(pulled, w_up).astype(BF16)
-        gn2_mine = line_scatter(gn2_part, "mp", mp)
-        gn2 = line_gather(gn2_mine.astype(BF16), "mp", mp).astype(F32)
-        g = gn2 * gains[1]
-        mean = jnp.mean(g * middle, axis=1, keepdims=True)
-        gbo = (grad_y.astype(F32) + s2 * g - middle * (s2 * s2 * s2 * mean)).astype(BF16)
-        gain2_total = gain2_total + jnp.sum(gn2 * (middle * s2), axis=0)
-        local = (
-            jnp.where(lives[c], cotangent[c * step : (c + 1) * step].astype(F32), 0.0)
-            + s2 * (gn2_mine * mine(gains[1]))
-            - middle_mine * (s2 * s2 * s2 * mean)
-        )
-        mlp = line_scatter(inner_cols(hidden, w_down).astype(BF16), "mp", mp)
-        outputs.append((middle_mine + mlp).astype(BF16))
-        hiddens.append(hidden)
-        gates_up.append(pulled)
-        norms2.append(normed2)
-        gbos.append(gbo)
-        locals_.append(local)
-        gms.append(matmul(gbo, w_out))
-        cots[c] = grad_y
+    output, gm, gbo, local, hidden, pulled, normed2, grad_y, gain2 = middle(
+        dp, mp, 4, jnp.concatenate(mixes), inputs, cotangent, live, gains, mine(gains), w_out,
+        up, down,
+    )
+    gms, locals_ = cut(gm), cut(local)
 
     grad_up = square_scatter(
-        inner_rows(jnp.concatenate(norms2), jnp.concatenate(gates_up)).astype(BF16), "dp", dp
+        inner_rows(normed2, pulled).astype(BF16), "dp", dp
     )
     grad_down = square_scatter(
-        inner_rows(jnp.concatenate(cots), jnp.concatenate(hiddens)).astype(BF16), "dp", dp
+        inner_rows(grad_y, hidden).astype(BF16), "dp", dp
     )
     grad_out = square_scatter(
-        inner_rows(jnp.concatenate(gbos), jnp.concatenate(mixes)).astype(BF16), "dp", dp
+        inner_rows(gbo, jnp.concatenate(mixes)).astype(BF16), "dp", dp
     )
 
     back, tail = blank, blank
@@ -640,9 +1203,9 @@
     )
     grad_params = line_sum(params_total, "dp", dp)
     grad_gain1 = line_sum(line_sum(gain1_total.reshape(8, -1), "dp", dp), "mp", mp)
-    grad_gain2 = line_sum(gain2_total.reshape(8, -1), "dp", dp)
+    grad_gain2 = line_sum(jnp.sum(gain2, axis=0).reshape(8, -1), "dp", dp)
     return (
-        jnp.concatenate(outputs),
+        output,
         jnp.concatenate(grads_in),
         jnp.stack([grad_gain1.reshape(-1), grad_gain2.reshape(-1)]),
         grad_params,

time: 1040 us -> 890 us (0.86); the launches traced: 1020 us -> 883 us
  Pallas kernels: 73.2 us -> 423 us
  starting transfers between devices: 268 us -> 97.3 us
  waiting for transfers between devices: 294 us -> 186 us
  other arithmetic: 124 us -> 42.4 us
  matrix products: 148 us -> 68.7 us
  local copies, waits for them, and re-layouts: 110 us -> 63.6 us
    pallas_call x0 -> x1, Pallas kernels: none -> 349 us  [middle(): pl.pallas_call(functools.partial(middle_kernel, dp, mp, chunks), in_specs...]
    ppermute x24 -> x6, starting transfers between devices: 110 us -> 29.1 us  [line_scatter(): lax.ppermute(going.astype(BF16), axis, [(i, i + 1) for i in range(step)])]
    ppermute x24 -> x6, waiting for transfers between devices: 111 us -> 35.1 us  [line_gather(): left = lax.ppermute(left, axis, [(i + 1, i) for i in range(size - step)])]
    ppermute x4, waiting for transfers between devices: 2.44 us -> 52.3 us  [square_scatter(): by_y = lax.ppermute(to_y.astype(BF16), axis, swap(size, 4))]
    dot_general x8 -> x2, matrix products: 59.1 us -> 13.8 us  [matmul(): return jnp.dot(left, right, preferred_element_type=F32)]
    ppermute x24 -> x6, waiting for transfers between devices: 79.6 us -> 36.1 us  [line_scatter(): lax.ppermute(going.astype(BF16), axis, [(i, i + 1) for i in range(step)])]
    ppermute x24 -> x6, starting transfers between devices: 53.6 us -> 13.7 us  [line_gather(): lax.ppermute(right, axis, [(i, i + 1) for i in range(step - 1, size - 1)])]
    dot_general x8 -> x2, matrix products: 49.1 us -> 13.2 us  [inner_cols(): lax.dot_general(left, right, (((1,), (1,)), ((), ())), preferred_element_...]
  transfers between devices with their start and end apart: 161 -> 75, of which waited for: 51 -> 24; matrix products, arithmetic and copies ran while one was open for 35% -> 13% of each run, Pallas kernels for 7% -> 0%
where the time goes in v2:
time: 890 us; the launch traced here: 883 us
  Pallas kernels  423 us (48%)
  waiting for transfers between devices  186 us (21%)
  starting transfers between devices  97.3 us (11%)
  matrix products  68.7 us (8%)
  local copies, waits for them, and re-layouts  63.6 us (7%)
  other arithmetic  42.4 us (5%)
    pallas_call x1, Pallas kernels, middle(): pl.pallas_call(functools.partial(middle_kernel, dp, mp, chunks), in_specs...  349 us
    ppermute x4, waiting for transfers between devices, square_scatter(): by_y = lax.ppermute(to_y.astype(BF16), axis, swap(size, 4))  52.3 us
    dot_general x5, matrix products, inner_rows(): lax.dot_general(left, right, (((0,), (0,)), ((), ())), preferred_element_...  41.6 us
    pallas_call x2, Pallas kernels, rnn_backward(): pl.pallas_call(rnn_backward_kernel, out_shape=(jax.ShapeDtypeStruct((coun...  39 us
    ppermute x6, waiting for transfers between devices, line_scatter(): lax.ppermute(going.astype(BF16), axis, [(i, i + 1) for i in range(step)])  36.1 us
    ppermute x6, waiting for transfers between devices, line_gather(): left = lax.ppermute(left, axis, [(i + 1, i) for i in range(size - step)])  35.1 us
    pallas_call x2, Pallas kernels, rnn_forward(): pl.pallas_call(rnn_forward_kernel, out_shape=(jax.ShapeDtypeStruct((count...  34.7 us
    ppermute x4, waiting for transfers between devices, square_scatter(): far = lax.ppermute(pick(chip ^ 3), axis, cross(size)).astype(F32)  30.7 us
  transfers between devices with their start and end apart: 75, of which 24 were waited for; matrix products, arithmetic and copies ran while one was open for 13% of the time, Pallas kernels for 0%

profile of v2, /device:TPU:0, one launch (start us, length us, event | category | flops | bytes accessed | tf_op | source)
XLA Modules:
  0.0 882.9 jit_solution(13466445759271672795)
XLA Ops:
  43.5 10.0 %collective-permute-done.4 = bf16[512,512]{1,0:T(8,128)(2,1)S(1)} collective-permute-done((bf16[512,512]{1,0:T(8,128)(2,1)}, bf16[512,512]{1,0:T(8,128)(2,1)S(1)}, u32[]{:S(2)}, u32[]{:S(2)}) %collective-permute-start.4) | collective-permute-done | bytes 524320 | tf_op jit(solution)/shard_map/ppermute | solution.py:67
  60.5 8.8 collective-permute-done.5
  104.0 10.6 %collective-permute-done.21 = bf16[512,512]{1,0:T(8,128)(2,1)S(1)} collective-permute-done((bf16[512,512]{1,0:T(8,128)(2,1)S(1)}, bf16[512,512]{1,0:T(8,128)(2,1)S(1)}, u32[]{:S(2)}, u32[]{:S(2)}) %collective-permute-start.21) | collective-permute-done | bytes 524320 | tf_op jit(solution)/shard_map/ppermute | solution.py:67
  116.3 6.9 fusion.76.both_ref
  124.7 17.3 %rnn_forward.2 = (bf16[512,640]{1,0:T(8,128)(2,1)}, f32[512,640]{1,0:T(8,128)}, f32[512,640]{1,0:T(8,128)}, f32[512,640]{1,0:T(8,128)}, f32[512,640]{1,0:T(8,128)}, /*index=5*/f32[8,640]{1,0:T(8,128)}) custom-call(f32[512,1280]{1,0:T(8,128)} %copy-done.20, f32[8,640]{1,0:T(8,128)} %broadcast_in_dim.81.halo_ref.start_ref.back_ref.tail_ref, ...), custom_call_target="tpu_custom_call" | custom-call | flops 1677721600 | bytes 9830400 | tf_op jit(solution)/shard_map/rnn_forward/pallas_call | solution.py:290
  143.2 7.0 fusion.77.both_ref
  150.2 17.3 %rnn_forward.3 = (bf16[512,640]{1,0:T(8,128)(2,1)}, f32[512,640]{1,0:T(8,128)}, f32[512,640]{1,0:T(8,128)}, f32[512,640]{1,0:T(8,128)}, f32[512,640]{1,0:T(8,128)}, /*index=5*/f32[8,640]{1,0:T(8,128)}) custom-call(f32[512,1280]{1,0:T(8,128)} %fusion.77.both_ref, f32[8,640]{1,0:T(8,128)} %slice.114.halo_ref, f32[8,640]{1,0:T(8,128)} %get-tuple-element.44.start_ref, ...), custom_call_target="tpu_custom_call" | custom-call | flops 1677721600 | bytes 9830400 | tf_op jit(solution)/shard_map/rnn_forward/pallas_call | solution.py:290
  169.9 349.2 %middle.1 = (bf16[1024,512]{1,0:T(8,128)(2,1)}, f32[1024,640]{1,0:T(8,128)}, bf16[1024,2048]{1,0:T(8,128)(2,1)}, f32[1024,512]{1,0:T(8,128)}, bf16[1024,1536]{1,...) custom-call(bf16[1024,640]{1,0:T(8,128)(2,1)} %copy-done.18, ...), custom_call_target="tpu_custom_call" | custom-call | tf_op jit(solution)/shard_map/middle/pallas_call | solution.py:1016
  522.8 19.2 %rnn_backward.2 = (bf16[512,1280]{1,0:T(8,128)(2,1)}, bf16[512,1280]{1,0:T(8,128)(2,1)}, f32[8,640]{1,0:T(8,128)}, f32[8,640]{1,0:T(8,128)}, f32[8,640]{1,0:T(8,128)}) custom-call(f32[512,640]{1,0:T(8,128)} %get-tuple-element.137.gm_ref, f32[512,1280]{1,0:T(8,128)} %fusion.77.both_ref, f32[8,640]{1,0:T(8,128)} %slice.114.halo_ref, ...), custom_call_target="tpu_custom_call" | custom-call | flops 838860800 | bytes 11796480 | tf_op jit(solution)/shard_map/rnn_backward/pallas_call | solution.py:435
  547.9 19.8 %rnn_backward.3 = (bf16[512,1280]{1,0:T(8,128)(2,1)}, bf16[512,1280]{1,0:T(8,128)(2,1)}, f32[8,640]{1,0:T(8,128)}, f32[8,640]{1,0:T(8,128)}, f32[8,640]{1,0:T(8,128)}) custom-call(f32[512,640]{1,0:T(8,128)} %get-tuple-element.136.gm_ref, f32[512,1280]{1,0:T(8,128)} %copy-done.20, f32[8,640]{1,0:T(8,128)} %broadcast_in_dim.81.halo_ref.start_ref.back_ref.tail_ref, ...), custom_call_target="tpu_custom_call" | custom-call | flops 838860800 | bytes 11796480 | tf_op jit(solution)/shard_map/rnn_backward/pallas_call | solution.py:435
  567.8 9.2 %convolution_convert_fusion.2 = bf16[2048,1280]{1,0:T(8,128)(2,1)} fusion(bf16[512,2048]{1,0:T(8,128)(2,1)S(1)} %copy-done.24, bf16[512,2048]{1,0:T(8,128)(2,1)S(1)} %copy-done.26, bf16[512,1280]{1,0:T(8,128)(2,1)} %get-tuple-element.61, bf16[512,1280]{1,0:T(8,128)(2,1)} %get-tuple-element.60), kind=kOutput, calls=%fused_computation.4 | convolution fusion | flops 5384962048 | bytes 12058624 | tf_op jit(solution)/shard_map/dot_general | solution.py:27
  577.1 7.3 multiply_reduce_fusion
  599.4 15.6 %convolution_convert_fusion = bf16[2048,3072]{1,0:T(8,128)(2,1)S(1)} fusion(bf16[1024,2048]{1,0:T(8,128)(2,1)S(1)} %copy-done.44, bf16[1024,3072]{1,0:T(8,128)(2,1)} %get-tuple-element.68), kind=kOutput, calls=%fused_computation.2 | convolution fusion | flops 12891193344 | bytes 23068672 | tf_op jit(solution)/shard_map/dot_general | solution.py:27
  627.5 7.5 convolution_convert_fusion.1
  671.2 7.4 collective-permute-done.37
  685.1 10.2 %collective-permute-done.30 = bf16[512,512]{1,0:T(8,128)(2,1)S(1)} collective-permute-done((bf16[512,512]{1,0:T(8,128)(2,1)S(1)}, bf16[512,512]{1,0:T(8,128)(2,1)S(1)}, u32[]{:S(2)}, u32[]{:S(2)}) %collective-permute-start.30) | collective-permute-done | bytes 524320 | tf_op jit(solution)/shard_map/ppermute | solution.py:90
  708.0 16.1 %collective-permute-start.31 = (bf16[512,512]{1,0:T(8,128)(2,1)S(1)}, bf16[512,512]{1,0:T(8,128)(2,1)S(1)}, u32[]{:S(2)}, u32[]{:S(2)}) collective-permute-start(bf16[512,512]{1,0:T(8,128)(2,1)S(1)} %get-tuple-element.138), channel_id=1, source_target_pairs={{0,1},{1,2},{2,3},{4,5},{5,6},{6,7},{8,9},{9,10},{10,11},{12,13},{... | collective-permute-start | bytes 1572872 | tf_op jit(solution)/shard_map/ppermute | solution.py:90
  737.7 8.3 collective-permute-done.39
  748.7 6.7 collective-permute-done.69
  769.6 7.4 fusion
  784.5 20.1 %collective-permute-done.57 = bf16[256,1280]{1,0:T(8,128)(2,1)S(1)} collective-permute-done((bf16[256,1280]{1,0:T(8,128)(2,1)S(1)}, bf16[256,1280]{1,0:T(8,128)(2,1)S(1)}, u32[]{:S(2)}, u32[]{:S(2)}) %collective-permute-start.57) | collective-permute-done | bytes 655392 | tf_op jit(solution)/shard_map/ppermute | solution.py:176
  810.1 10.7 %collective-permute-done.72 = bf16[256,1536]{0,1:T(8,128)(2,1)S(1)} collective-permute-done((bf16[256,1536]{0,1:T(8,128)(2,1)S(1)}, bf16[256,1536]{0,1:T(8,128)(2,1)S(1)}, u32[]{:S(2)}, u32[]{:S(2)}) %collective-permute-start.72) | collective-permute-done | bytes 786464 | tf_op jit(solution)/shard_map/ppermute | solution.py:176
  822.6 12.3 %collective-permute-done.59 = bf16[256,1280]{1,0:T(8,128)(2,1)S(1)} collective-permute-done((bf16[256,1280]{1,0:T(8,128)(2,1)S(1)}, bf16[256,1280]{1,0:T(8,128)(2,1)S(1)}, u32[]{:S(2)}, u32[]{:S(2)}) %collective-permute-start.59) | collective-permute-done | bytes 655392 | tf_op jit(solution)/shard_map/ppermute | solution.py:181
  837.6 40.1 %collective-permute-done.74 = bf16[256,1536]{0,1:T(8,128)(2,1)S(1)} collective-permute-done((bf16[256,1536]{0,1:T(8,128)(2,1)S(1)}, bf16[256,1536]{0,1:T(8,128)(2,1)S(1)}, u32[]{:S(2)}, u32[]{:S(2)}) %collective-permute-start.74) | collective-permute-done | bytes 786464 | tf_op jit(solution)/shard_map/ppermute | solution.py:181
  (395 shorter events, 235.8 us)
Async XLA Ops:
  3.0 30.6 %collective-permute-start = (bf16[512,512]{1,0:T(8,128)(2,1)}, bf16[512,512]{1,0:T(8,128)(2,1)}, u32[]{:S(2)}, u32[]{:S(2)}) collective-permute-start(bf16[512,512]{1,0:T(8,128)(2,1)} %get-tuple-element.152), channel_id=1, source_target_pairs={{1,0},{2,1},{3,2},{5,4},{6,5},{7,6},{9,8},{10,9},{11,10},{13,12},{... | collective-permute-start | bytes 1572872 | tf_op jit(solution)/shard_map/ppermute | solution.py:67
  4.4 29.8 %collective-permute-start.1 = (bf16[512,512]{1,0:T(8,128)(2,1)}, bf16[512,512]{1,0:T(8,128)(2,1)}, u32[]{:S(2)}, u32[]{:S(2)}) collective-permute-start(bf16[512,512]{1,0:T(8,128)(2,1)} %get-tuple-element.152), channel_id=1, source_target_pairs={{0,1},{1,2},{2,3},{4,5},{5,6},{6,7},{8,9},{9,10},{10,11},{12,13},{... | collective-permute-start | bytes 1572872 | tf_op jit(solution)/shard_map/ppermute | solution.py:66
  14.2 22.9 %collective-permute-start.7 = (bf16[256,1280]{1,0:T(8,128)(2,1)}, bf16[256,1280]{1,0:T(8,128)(2,1)}, u32[]{:S(2)}, u32[]{:S(2)}) collective-permute-start(bf16[256,1280]{1,0:T(8,128)(2,1)} %constant_dynamic-update-slice_fusion.18), channel_id=1, source_target_pairs={{0,16},{4,20},{8,24},{12,28},{16,0},{20,4},{24,8},{28,12},{1,17},{... | collective-permute-start | bytes 1966088 | tf_op jit(solution)/shard_map/ppermute | solution.py:149
  33.5 22.8 %collective-permute-start.9 = (bf16[256,1280]{1,0:T(8,128)(2,1)}, bf16[256,1280]{1,0:T(8,128)(2,1)S(1)}, u32[]{:S(2)}, u32[]{:S(2)}) collective-permute-start(bf16[256,1280]{1,0:T(8,128)(2,1)} %constant_dynamic-update-slice_fusion.18), channel_id=1, source_target_pairs={{0,4},{4,0},{8,12},{12,8},{16,20},{20,16},{24,28},{28,24},{1,5},{5... | collective-permute-start | bytes 1966088 | tf_op jit(solution)/shard_map/ppermute | solution.py:154
  586.8 83.0 %collective-permute-start.29 = (bf16[512,512]{1,0:T(8,128)(2,1)}, bf16[512,512]{1,0:T(8,128)(2,1)}, u32[]{:S(2)}, u32[]{:S(2)}) collective-permute-start(bf16[512,512]{1,0:T(8,128)(2,1)} %get-tuple-element.140), channel_id=1, source_target_pairs={{0,1},{4,5},{8,9},{12,13},{16,17},{20,21},{24,25},{28,29}} | collective-permute-start | bytes 1572872 | tf_op jit(solution)/shard_map/ppermute | solution.py:90
  589.0 49.5 %collective-permute-start.35 = (f32[8,64]{1,0:T(8,128)S(1)}, f32[8,64]{1,0:T(8,128)S(1)}, u32[]{:S(2)}, u32[]{:S(2)}) collective-permute-start(f32[8,64]{1,0:T(8,128)S(1)} %reshape.208), channel_id=1, source_target_pairs={{0,1},{1,0},{2,3},{3,2},{4,5},{5,4},{6,7},{7,6},{8,9},{9,8},{10,11... | collective-permute-start | bytes 6152 | tf_op jit(solution)/shard_map/ppermute | solution.py:103
  589.1 59.1 %collective-permute-start.43 = (f32[8,64]{1,0:T(8,128)S(1)}, f32[8,64]{1,0:T(8,128)S(1)}, u32[]{:S(2)}, u32[]{:S(2)}) collective-permute-start(f32[8,64]{1,0:T(8,128)S(1)} %reshape.210), channel_id=1, source_target_pairs={{0,1},{1,0},{2,3},{3,2},{4,5},{5,4},{6,7},{7,6},{8,9},{9,8},{10,11... | collective-permute-start | bytes 6152 | tf_op jit(solution)/shard_map/ppermute | solution.py:103
  591.1 63.9 %collective-permute-start.50 = (f32[8,256]{1,0:T(8,128)S(1)}, f32[8,256]{1,0:T(8,128)S(1)}, u32[]{:S(2)}, u32[]{:S(2)}) collective-permute-start(f32[8,256]{1,0:T(8,128)S(1)} %reshape.212), channel_id=1, source_target_pairs={{0,4},{4,0},{8,12},{12,8},{16,20},{20,16},{24,28},{28,24},{1,5},{5... | collective-permute-start | bytes 24584 | tf_op jit(solution)/shard_map/ppermute | solution.py:103
  591.2 62.4 %collective-permute-start.45 = (f32[8,256]{1,0:T(8,128)S(1)}, f32[8,256]{1,0:T(8,128)S(1)}, u32[]{:S(2)}, u32[]{:S(2)}) collective-permute-start(f32[8,256]{1,0:T(8,128)S(1)} %add.480), channel_id=1, source_target_pairs={{0,4},{4,0},{8,12},{12,8},{16,20},{20,16},{24,28},{28,24},{1,5},{5... | collective-permute-start | bytes 24584 | tf_op jit(solution)/shard_map/ppermute | solution.py:103
  658.7 110.8 %collective-permute-start.63 = (bf16[4,256,3072]{2,1,0:T(8,128)(2,1)}, bf16[4,256,3072]{2,1,0:T(8,128)(2,1)}, u32[]{:S(2)}, u32[]{:S(2)}) collective-permute-start(bf16[4,256,3072]{2,1,0:T(8,128)(2,1)} %dynamic-slice_bitcast_fusion), channel_id=1, source_target_pairs={{0,4},{4,0},{8,12},{12,8},{16,20},{20,16},{24,28},{28,24},{1,5},{5... | collective-permute-start | bytes 18874376 | tf_op jit(solution)/shard_map/ppermute | solution.py:169
  669.1 28.6 %collective-permute-start.40 = (bf16[512,512]{1,0:T(8,128)(2,1)}, bf16[512,512]{1,0:T(8,128)(2,1)S(1)}, u32[]{:S(2)}, u32[]{:S(2)}) collective-permute-start(bf16[512,512]{1,0:T(8,128)(2,1)} %get-tuple-element.145), channel_id=1, source_target_pairs={{3,2},{7,6},{11,10},{15,14},{19,18},{23,22},{27,26},{31,30}} | collective-permute-start | bytes 1572872 | tf_op jit(solution)/shard_map/ppermute | solution.py:94
  669.8 33.2 %collective-permute-start.67 = (bf16[4,256,640]{2,1,0:T(8,128)(2,1)}, bf16[4,256,640]{2,1,0:T(8,128)(2,1)S(1)}, u32[]{:S(2)}, u32[]{:S(2)}) collective-permute-start(bf16[4,256,640]{2,1,0:T(8,128)(2,1)} %dynamic-slice_bitcast_fusion.3), channel_id=1, source_target_pairs={{0,4},{4,0},{8,12},{12,8},{16,20},{20,16},{24,28},{28,24},{1,5},{5... | collective-permute-start | bytes 3932168 | tf_op jit(solution)/shard_map/ppermute | solution.py:169
  704.2 61.4 %collective-permute-start.56 = (bf16[4,256,1280]{2,1,0:T(8,128)(2,1)}, bf16[4,256,1280]{2,1,0:T(8,128)(2,1)}, u32[]{:S(2)}, u32[]{:S(2)}) collective-permute-start(bf16[4,256,1280]{2,1,0:T(8,128)(2,1)} %dynamic-slice_bitcast_fusion.1), channel_id=1, source_target_pairs={{0,4},{4,0},{8,12},{12,8},{16,20},{20,16},{24,28},{28,24},{1,5},{5... | collective-permute-start | bytes 7864328 | tf_op jit(solution)/shard_map/ppermute | solution.py:169
  708.0 28.4 %collective-permute-start.31 = (bf16[512,512]{1,0:T(8,128)(2,1)S(1)}, bf16[512,512]{1,0:T(8,128)(2,1)S(1)}, u32[]{:S(2)}, u32[]{:S(2)}) collective-permute-start(bf16[512,512]{1,0:T(8,128)(2,1)S(1)} %get-tuple-element.138), channel_id=1, source_target_pairs={{0,1},{1,2},{2,3},{4,5},{5,6},{6,7},{8,9},{9,10},{10,11},{12,13},{... | collective-permute-start | bytes 1572872 | tf_op jit(solution)/shard_map/ppermute | solution.py:90
  755.4 25.0 %collective-permute-start.71 = (bf16[4,256,1536]{1,2,0:T(8,128)(2,1)}, bf16[4,256,1536]{1,2,0:T(8,128)(2,1)}, u32[]{:S(2)}, u32[]{:S(2)}) collective-permute-start(bf16[4,256,1536]{1,2,0:T(8,128)(2,1)} %bitcast.34), channel_id=1, source_target_pairs={{0,4},{4,0},{8,12},{12,8},{16,20},{20,16},{24,28},{28,24},{1,5},{5... | collective-permute-start | bytes 9437192 | tf_op jit(solution)/shard_map/ppermute | solution.py:169
  777.1 29.9 %collective-permute-start.64 = (bf16[256,3072]{1,0:T(8,128)(2,1)S(1)}, bf16[256,3072]{1,0:T(8,128)(2,1)S(1)}, u32[]{:S(2)}, u32[]{:S(2)}) collective-permute-start(bf16[256,3072]{1,0:T(8,128)(2,1)S(1)} %dynamic-slice_bitcast_fusion.2), channel_id=1, source_target_pairs={{0,16},{4,12},{8,24},{12,4},{16,0},{20,28},{24,8},{28,20},{1,17},{... | collective-permute-start | bytes 4718600 | tf_op jit(solution)/shard_map/ppermute | solution.py:176
  779.5 25.1 %collective-permute-start.57 = (bf16[256,1280]{1,0:T(8,128)(2,1)S(1)}, bf16[256,1280]{1,0:T(8,128)(2,1)S(1)}, u32[]{:S(2)}, u32[]{:S(2)}) collective-permute-start(bf16[256,1280]{1,0:T(8,128)(2,1)S(1)} %dynamic-slice_bitcast_fusion.5), channel_id=1, source_target_pairs={{0,16},{4,12},{8,24},{12,4},{16,0},{20,28},{24,8},{28,20},{1,17},{... | collective-permute-start | bytes 1966088 | tf_op jit(solution)/shard_map/ppermute | solution.py:176
  783.2 37.6 %collective-permute-start.72 = (bf16[256,1536]{0,1:T(8,128)(2,1)S(1)}, bf16[256,1536]{0,1:T(8,128)(2,1)S(1)}, u32[]{:S(2)}, u32[]{:S(2)}) collective-permute-start(bf16[256,1536]{0,1:T(8,128)(2,1)S(1)} %dynamic-slice_bitcast_fusion.4), channel_id=1, source_target_pairs={{0,16},{4,12},{8,24},{12,4},{16,0},{20,28},{24,8},{28,20},{1,17},{... | collective-permute-start | bytes 2359304 | tf_op jit(solution)/shard_map/ppermute | solution.py:176
  805.0 29.9 %collective-permute-start.59 = (bf16[256,1280]{1,0:T(8,128)(2,1)S(1)}, bf16[256,1280]{1,0:T(8,128)(2,1)S(1)}, u32[]{:S(2)}, u32[]{:S(2)}) collective-permute-start(bf16[256,1280]{1,0:T(8,128)(2,1)S(1)} %get-tuple-element.131), channel_id=1, source_target_pairs={{0,16},{4,20},{8,24},{12,28},{16,0},{20,4},{24,8},{28,12},{1,17},{... | collective-permute-start | bytes 1966088 | tf_op jit(solution)/shard_map/ppermute | solution.py:181
  806.3 30.0 %collective-permute-start.58 = (bf16[256,1280]{1,0:T(8,128)(2,1)S(1)}, bf16[256,1280]{1,0:T(8,128)(2,1)S(1)}, u32[]{:S(2)}, u32[]{:S(2)}) collective-permute-start(bf16[256,1280]{1,0:T(8,128)(2,1)S(1)} %get-tuple-element.130), channel_id=1, source_target_pairs={{0,8},{4,12},{8,0},{12,4},{16,24},{20,28},{24,16},{28,20},{1,9},{5... | collective-permute-start | bytes 1966088 | tf_op jit(solution)/shard_map/ppermute | solution.py:180
  808.0 71.0 %collective-permute-start.66 = (bf16[256,3072]{1,0:T(8,128)(2,1)S(1)}, bf16[256,3072]{1,0:T(8,128)(2,1)S(1)}, u32[]{:S(2)}, u32[]{:S(2)}) collective-permute-start(bf16[256,3072]{1,0:T(8,128)(2,1)S(1)} %get-tuple-element.125), channel_id=1, source_target_pairs={{0,16},{4,20},{8,24},{12,28},{16,0},{20,4},{24,8},{28,12},{1,17},{... | collective-permute-start | bytes 4718600 | tf_op jit(solution)/shard_map/ppermute | solution.py:181
  809.5 69.6 %collective-permute-start.65 = (bf16[256,3072]{1,0:T(8,128)(2,1)S(1)}, bf16[256,3072]{1,0:T(8,128)(2,1)S(1)}, u32[]{:S(2)}, u32[]{:S(2)}) collective-permute-start(bf16[256,3072]{1,0:T(8,128)(2,1)S(1)} %get-tuple-element.124), channel_id=1, source_target_pairs={{0,8},{4,12},{8,0},{12,4},{16,24},{20,28},{24,16},{28,20},{1,9},{5... | collective-permute-start | bytes 4718600 | tf_op jit(solution)/shard_map/ppermute | solution.py:180
  821.3 56.3 %collective-permute-start.74 = (bf16[256,1536]{0,1:T(8,128)(2,1)S(1)}, bf16[256,1536]{0,1:T(8,128)(2,1)S(1)}, u32[]{:S(2)}, u32[]{:S(2)}) collective-permute-start(bf16[256,1536]{0,1:T(8,128)(2,1)S(1)} %get-tuple-element.129), channel_id=1, source_target_pairs={{0,16},{4,20},{8,24},{12,28},{16,0},{20,4},{24,8},{28,12},{1,17},{... | collective-permute-start | bytes 2359304 | tf_op jit(solution)/shard_map/ppermute | solution.py:181
  834.9 42.8 %collective-permute-start.73 = (bf16[256,1536]{0,1:T(8,128)(2,1)S(1)}, bf16[256,1536]{0,1:T(8,128)(2,1)S(1)}, u32[]{:S(2)}, u32[]{:S(2)}) collective-permute-start(bf16[256,1536]{0,1:T(8,128)(2,1)S(1)} %get-tuple-element.128), channel_id=1, source_target_pairs={{0,8},{4,12},{8,0},{12,4},{16,24},{20,28},{24,16},{28,20},{1,9},{5... | collective-permute-start | bytes 2359304 | tf_op jit(solution)/shard_map/ppermute | solution.py:180
  (104 other events, 1187.0 us)

commit v3 on v2

--- a/solution.py
+++ b/solution.py
@@ -12,7 +12,7 @@
 ROOT_FLOOR = 0.0001
 TAPS = 4
 LANES = 8
-CHUNKS = 2
+CHUNKS = 1
 TILE = 32
 F32 = jnp.float32
 BF16 = jnp.bfloat16
@@ -313,7 +313,7 @@
 def rnn_backward_kernel(
     gm_ref, both_ref, halo_ref, start_ref, conv_ref, r_ref, i_ref, state_ref, mask_ref,
     gates_ref, params_ref, back_ref, tail_ref,
-    grads_ref, rates_ref, dparams_ref, back_out_ref, tail_out_ref,
+    grads_ref, rates_ref, dparams_ref, back_out_ref, tail_out_ref, dots_ref,
     padded, before, decay, adjoint, coef, dconv, sums,
 ):
     count, width = conv_ref.shape
@@ -418,6 +418,11 @@
             out = out + params_ref[k : k + 1, :] * kept[k : k + TILE, :]
             sums[k] += fold(kept[0:TILE, :] * source[8 - k : 8 - k + TILE, :])
         grads_ref[rows, 0:width] = out.astype(BF16)
+        dot = jnp.sum(
+            out * source[8:, :] + grads_ref[rows, width:].astype(F32) * both_ref[rows, width:],
+            axis=1, keepdims=True,
+        )
+        dots_ref[rows, :] = jnp.broadcast_to(dot, (TILE, 128))
 
     tile_loop(tiles, unconvolve)
     for k in range(8):
@@ -440,6 +445,7 @@
             jax.ShapeDtypeStruct((8, width), F32),
             jax.ShapeDtypeStruct((8, width), F32),
             jax.ShapeDtypeStruct((8, width), F32),
+            jax.ShapeDtypeStruct((count, 128), F32),
         ),
         scratch_shapes=[
             pltpu.VMEM((count + 8, width), F32),
@@ -676,6 +682,240 @@
     def drain(self):
         for k in range(7):
             self.copy(self.shard, self.d, self.by_core, k, 0).wait_send()
+
+
+def head_kernel(dp, mp, names, *refs):
+    ref = dict(zip(names, refs))
+    blocks, w_in, norm, both = ref["blocks"], ref["w_in_here"], ref["norm"], ref["both_here"]
+    chunks, _, step, part = blocks.shape
+    features, width = part * mp, ref["mixed_here"].shape[2]
+    z, d = lax.axis_index("mp"), lax.axis_index("dp")
+    square = dp == 8
+    gather = Spread(z, mp, blocks, ref["spread_sent"], ref["spread_came"])
+
+    barrier = pltpu.get_barrier_semaphore()
+
+    @pl.when(z > 0)
+    def _():
+        pl.semaphore_signal(barrier, inc=1, device_id={"mp": z - 1}, device_id_type=MESH)
+
+    @pl.when(z < mp - 1)
+    def _():
+        pl.semaphore_signal(barrier, inc=1, device_id={"mp": z + 1}, device_id_type=MESH)
+
+    count = jnp.where((z > 0) & (z < mp - 1), 2, 1)
+    if square:
+        for other in partners(d)[1:]:
+            pl.semaphore_signal(barrier, inc=1, device_id={"dp": other}, device_id_type=MESH)
+        count = count + 3
+
+    def chunk_rows(c):
+        return pl.ds(c * step, step)
+
+    def own_block(c):
+        return pltpu.make_async_copy(
+            ref["x"].at[chunk_rows(c), :], blocks.at[c, z], ref["load_sem"].at[c]
+        )
+
+    for c in range(chunks):
+        own_block(c).start()
+    pl.semaphore_wait(barrier, count)
+
+    wholes = (("gates_shard", ref["gates_here"]), ("in_shard", w_in), ("out_shard", ref["w_out"]))
+    if square:
+        squares = [
+            Square(
+                d, ref[name], whole, ref["square_sent"].at[k], ref["square_came"].at[k],
+                ref["square_own"].at[k],
+            )
+            for k, (name, whole) in enumerate(wholes)
+        ]
+        for item in squares:
+            item.start()
+    else:
+        loads = [
+            pltpu.make_async_copy(ref[name], whole, ref["square_own"].at[k])
+            for k, (name, whole) in enumerate(wholes)
+        ]
+        for item in loads:
+            item.start()
+
+    def begin(c):
+        own_block(c).wait()
+        gather.step(c, 0)
+
+    begin(0)
+    if chunks > 1:
+        begin(1)
+
+    def expand():
+        span = ref["gates_flat"].shape[0]
+        rows = span // 8
+        for k in range(8):
+            ref["gates_flat"][k * rows : (k + 1) * rows, :] = ref["gates_here"][
+                k * 32 : k * 32 + 32, :
+            ].astype(F32)[0:rows, :]
+        column = lax.broadcasted_iota(jnp.int32, (span, 2 * width), 1)
+        column = jnp.where(column >= width, column - width, column)
+        for b in range(width // span):
+            inside = (column >= b * span) & (column < (b + 1) * span)
+            ref["dense_here"][b * span : (b + 1) * span, :] = jnp.where(
+                inside, ref["gates_flat"][...], 0.0
+            ).astype(BF16)
+
+    stores = (
+        ("norm", "norm"), ("both", "both_here"), ("conv", "conv_here"), ("r", "r_here"),
+        ("i", "i_here"), ("state", "state_here"), ("mixed", "mixed_here"), ("s1", "s1_here"),
+    )
+
+    def store_all(c):
+        return [
+            pltpu.make_async_copy(
+                ref[near].at[c % 2], ref[far + "_out"].at[chunk_rows(c), :],
+                ref["store_sem"].at[c % 2, k],
+            )
+            for k, (far, near) in enumerate(stores)
+        ]
+
+    ref["halo"][...] = jnp.zeros_like(ref["halo"])
+    ref["start"][...] = jnp.zeros_like(ref["start"])
+
+    def compute(c):
+        slot = c % 2
+        if c > 1:
+            for copy in store_all(c - 2):
+                copy.wait()
+
+        def body(t):
+            rows = rows_at(t, TILE)
+            values = [blocks[c, j, rows, :].astype(F32) for j in range(mp)]
+            total = sum(jnp.sum(v * v, axis=1, keepdims=True) for v in values)
+            s1 = lax.rsqrt(total / features + EPS)
+            for j in range(mp):
+                cols = slice(j * part, (j + 1) * part)
+                norm[slot, rows, cols] = (values[j] * s1 * ref["gains"][0:1, cols]).astype(BF16)
+            ref["s1_here"][slot, rows, :] = jnp.broadcast_to(s1, (TILE, 128))
+
+        tile_loop(step // TILE, body)
+        for k in range(2):
+            cols = slice(k * width, (k + 1) * width)
+            both[slot, :, cols] = matmul(norm[slot], w_in[:, cols])
+        rnn_forward_kernel(
+            both.at[slot], ref["halo"], ref["start"], ref["mask"].at[chunk_rows(c), :],
+            ref["dense_here"], ref["params"],
+            ref["mixed_here"].at[slot], ref["conv_here"].at[slot], ref["r_here"].at[slot],
+            ref["i_here"].at[slot], ref["state_here"].at[slot], ref["end"],
+            ref["padded"], ref["high"], ref["low"], ref["decay"], ref["drive"],
+        )
+        ref["halo"][...] = both[slot, step - 8 :, 0:width]
+        ref["start"][...] = ref["end"][...]
+        for copy in store_all(c):
+            copy.start()
+
+    for s in range(1, mp - 1):
+        gather.step(0, s)
+        if s == 1 and chunks > 2:
+            begin(2)
+    if square:
+        for item in squares[:2]:
+            item.step_one()
+        for item in squares[:2]:
+            item.step_two()
+    gather.finish(0)
+    for c in range(chunks):
+        if c + 1 < chunks:
+            gather.step(c + 1, 1)
+        if c == 0:
+            if square:
+                for item in squares[:2]:
+                    item.finish()
+                squares[2].step_one()
+            else:
+                for item in loads:
+                    item.wait()
+            expand()
+            pass_on = [
+                pltpu.make_async_copy(w_in, ref["w_in"], ref["pass_sem"].at[0]),
+                pltpu.make_async_copy(ref["dense_here"], ref["dense"], ref["pass_sem"].at[1]),
+            ]
+            for copy in pass_on:
+                copy.start()
+        if c == 1 and square:
+            squares[2].step_two()
+        compute(c)
+        if c + 3 < chunks:
+            begin(c + 3)
+        if c + 1 < chunks:
+            for s in range(2, mp - 1):
+                gather.step(c + 1, s)
+            gather.finish(c + 1)
+    if square:
+        squares[2].finish()
+        for item in squares:
+            item.drain()
+    for copy in pass_on:
+        copy.wait()
+    for c in range(max(0, chunks - 2), chunks):
+        for copy in store_all(c):
+            copy.wait()
+    for c in range(chunks):
+        gather.drain(c)
+
+
+def head(dp, mp, chunks, x, gains, params, mask, in_shard, out_shard, gates_shard, span):
+    count, part = x.shape
+    features, width = part * mp, params.shape[1]
+    step = count // chunks
+    dma = pltpu.SemaphoreType.DMA
+    any_, vmem = pl.BlockSpec(memory_space=pl.ANY), pl.BlockSpec(memory_space=pltpu.VMEM)
+    ins = [
+        ("x", x, any_), ("gains", gains, vmem), ("params", params, vmem), ("mask", mask, vmem),
+        ("in_shard", in_shard, any_), ("out_shard", out_shard, any_),
+        ("gates_shard", gates_shard, any_),
+    ]
+    shape = jax.ShapeDtypeStruct
+    outs = [
+        ("w_in", shape((features, 2 * width), BF16)), ("w_out", shape((features, width), BF16)),
+        ("dense", shape((width, 2 * width), BF16)), ("norm_out", shape((count, features), BF16)),
+        ("both_out", shape((count, 2 * width), F32)), ("conv_out", shape((count, width), F32)),
+        ("r_out", shape((count, width), F32)), ("i_out", shape((count, width), F32)),
+        ("state_out", shape((count, width), F32)), ("mixed_out", shape((count, width), BF16)),
+        ("s1_out", shape((count, 128), F32)),
+    ]
+    wide = pltpu.VMEM((2, step, width), F32)
+    columns = pltpu.VMEM((width // 128, step, 128), F32)
+    scratch = [
+        ("blocks", pltpu.VMEM((chunks, mp, step, part), BF16)),
+        ("w_in_here", pltpu.VMEM((features, 2 * width), BF16)),
+        ("gates_here", pltpu.VMEM((256, 2 * width), BF16)),
+        ("gates_flat", pltpu.VMEM((span, 2 * width), F32)),
+        ("dense_here", pltpu.VMEM((width, 2 * width), BF16)),
+        ("norm", pltpu.VMEM((2, step, features), BF16)),
+        ("both_here", pltpu.VMEM((2, step, 2 * width), F32)),
+        ("conv_here", wide), ("r_here", wide), ("i_here", wide), ("state_here", wide),
+        ("mixed_here", pltpu.VMEM((2, step, width), BF16)),
+        ("s1_here", pltpu.VMEM((2, step, 128), F32)),
+        ("halo", pltpu.VMEM((8, width), F32)), ("start", pltpu.VMEM((8, width), F32)),
+        ("end", pltpu.VMEM((8, width), F32)),
+        ("padded", pltpu.VMEM((step + 8, width), F32)),
+        ("high", pltpu.VMEM((step, width), BF16)), ("low", pltpu.VMEM((step, width), BF16)),
+        ("decay", columns), ("drive", columns),
+        ("spread_sent", dma((chunks, 2 * mp))), ("spread_came", dma((chunks, mp))),
+        ("square_sent", dma((3, 8))), ("square_came", dma((3, 8))), ("square_own", dma((3,))),
+        ("load_sem", dma((chunks,))), ("store_sem", dma((2, 8))), ("pass_sem", dma((2,))),
+    ]
+    names = [i[0] for i in ins] + [o[0] for o in outs] + [k[0] for k in scratch]
+    return pl.pallas_call(
+        functools.partial(head_kernel, dp, mp, tuple(names)),
+        in_specs=[i[2] for i in ins],
+        out_specs=[any_] * len(outs),
+        out_shape=[o[1] for o in outs],
+        scratch_shapes=[k[1] for k in scratch],
+        compiler_params=pltpu.CompilerParams(
+            collective_id=2, has_side_effects=True, vmem_limit_bytes=60 * 1024 * 1024
+        ),
+        name="head",
+    )(*[i[1] for i in ins])
 
 
 def middle_kernel(dp, mp, chunks, *refs):
@@ -1064,6 +1304,440 @@
     )(mixed, inputs, cotangent, live, gains, mine, w_out, up, down)
 
 
+class Scatter:
+    def __init__(self, d, count, compute, held, far, first, second, sent, came):
+        self.d, self.count, self.compute = d, count, compute
+        self.held, self.far_in, self.first_in, self.second_in = held, far, first, second
+        self.sent, self.came = sent, came
+        self.core, self.by_core, by_x, by_y = partners(d)
+        even = self.core == 0
+        self.first = jnp.where(even, by_y, by_x)
+        self.second = jnp.where(even, by_x, by_y)
+        self.first_at, self.second_at = 2 - self.core, 1 + self.core
+        other = partners(self.by_core)
+        self.away = (self.by_core, other[2], other[3], partners(other[2])[3])
+        self.distant = partners(by_x)[3]
+
+    def copy(self, src, dst, target, sent, came):
+        return pltpu.make_async_remote_copy(
+            src_ref=src, dst_ref=dst, send_sem=self.sent.at[sent], recv_sem=self.came.at[came],
+            device_id={"dp": target}, device_id_type=MESH,
+        )
+
+    def to_core(self, buffer, k):
+        return self.copy(buffer, self.held.at[k], self.by_core, k, k)
+
+    def to_far(self):
+        return self.copy(self.held.at[3], self.far_in, self.first, 4, 4)
+
+    def to_first(self):
+        return self.copy(self.held.at[self.first_at], self.first_in, self.first, 5, 5)
+
+    def to_second(self):
+        return self.copy(self.held.at[self.second_at], self.second_in, self.second, 6, 6)
+
+    def add_block(self, k, owner):
+        self.copy(self.held.at[k], self.held.at[k], self.by_core, k, k).wait_recv()
+        self.compute(owner, self.held.at[k], True)
+
+    def near_core(self):
+        self.add_block(3, self.distant)
+        self.to_far().start()
+        self.add_block(self.first_at, self.first)
+        self.to_first().start()
+        self.add_block(0, self.d)
+        self.add_block(self.second_at, self.second)
+
+    def onward(self):
+        self.to_far().wait_recv()
+        at = self.second_at
+
+        def body(t):
+            rows = rows_at(t, 16)
+            self.held[at, rows, :] = (
+                self.held[at, rows, :].astype(F32) + self.far_in[rows, :].astype(F32)
+            ).astype(BF16)
+
+        tile_loop(self.count // 16, body)
+        self.to_second().start()
+
+    def finish(self, target):
+        self.to_first().wait_recv()
+        self.to_second().wait_recv()
+
+        def body(t):
+            rows = rows_at(t, 16)
+            target[rows, :] = (
+                self.held[0, rows, :].astype(F32)
+                + self.first_in[rows, :].astype(F32)
+                + self.second_in[rows, :].astype(F32)
+            )
+
+        tile_loop(self.count // 16, body)
+
+    def drain(self):
+        self.to_far().wait_send()
+        self.to_first().wait_send()
+        self.to_second().wait_send()
+
+
+def tail_kernel(mp, tasks, names, *refs):
+    ref = dict(zip(names, refs))
+    pull, w_in, norm1 = ref["pull"], ref["w_in"], ref["norm1"]
+    count, part = ref["x"].shape
+    features = part * mp
+    halves = ref["parts"].shape[0]
+    step = count // halves
+    own = features // 8
+    z, d = lax.axis_index("mp"), lax.axis_index("dp")
+    core, by_core, by_x, by_y = partners(d)
+    fold = Fold(
+        z, mp, ref["parts"], ref["rights"], ref["lefts"], ref["fold_sent"], ref["fold_right"],
+        ref["fold_left"],
+    )
+    fold.clear()
+    near = z + 1 - 2 * lax.rem(z, 2)
+    apart = z + 2 - 4 * lax.div(z, 2)
+
+    barrier = pltpu.get_barrier_semaphore()
+
+    @pl.when(z > 0)
+    def _():
+        pl.semaphore_signal(barrier, inc=1, device_id={"mp": z - 1}, device_id_type=MESH)
+
+    @pl.when(z < mp - 1)
+    def _():
+        pl.semaphore_signal(barrier, inc=1, device_id={"mp": z + 1}, device_id_type=MESH)
+
+    pl.semaphore_signal(barrier, inc=1, device_id={"mp": apart}, device_id_type=MESH)
+    for other in (by_core, by_x, by_y):
+        pl.semaphore_signal(barrier, inc=1, device_id={"dp": other}, device_id_type=MESH)
+    pl.semaphore_wait(barrier, jnp.where((z > 0) & (z < mp - 1), 6, 5))
+
+    rhs, lhs, sends = ref["rhs"], ref["lhs"], ref["sends"]
+    load_sem, lhs_sem, store_sem = ref["load_sem"], ref["lhs_sem"], ref["store_sem"]
+    loaded = [k for k, t in enumerate(tasks) if t[2] not in ("pull", "gates")]
+
+    def load(k):
+        _, _, right, first, width, _ = tasks[k]
+        slot = loaded.index(k) % 2
+        return pltpu.make_async_copy(
+            ref[right].at[:, pl.ds(first, width)], rhs.at[slot, :, pl.ds(0, width)],
+            load_sem.at[slot],
+        )
+
+    load(loaded[0]).start()
+    load(loaded[1]).start()
+
+    other = partners(by_core)
+    far_here, far_there = partners(by_x)[3], partners(other[2])[3]
+    first_dev = jnp.where(core == 0, by_y, by_x)
+    second_dev = jnp.where(core == 0, by_x, by_y)
+    order = (
+        far_there, other[2], other[3], by_core, far_here, first_dev, d, second_dev,
+    )
+    plan = [
+        (k, owner) for k, t in enumerate(tasks) if t[1] not in (None, "norm1") for owner in order
+    ]
+    turn = [0]
+
+    def lhs_copy(index):
+        k, owner = plan[index]
+        cols = pl.ds(pl.multiple_of(owner * own, own), own)
+        return pltpu.make_async_copy(
+            ref[tasks[k][1]].at[:, cols], lhs.at[index % 2], lhs_sem.at[index % 2]
+        )
+
+    lhs_copy(0).start()
+
+    def build(k):
+        _, left, right, first, width, _ = tasks[k]
+
+        def compute(owner, target, add):
+            if left is None:
+                rows = pl.ds(pl.multiple_of(owner * 32, 32), 32)
+                value = ref["gates"][rows, first : first + width].astype(F32)
+            else:
+                if left == "norm1":
+                    source = norm1.at[:, pl.ds(pl.multiple_of(owner * own, own), own)]
+                else:
+                    index = turn[0]
+                    turn[0] += 1
+                    if index + 1 < len(plan):
+                        lhs_copy(index + 1).start()
+                    lhs_copy(index).wait()
+                    source = lhs.at[index % 2]
+                if right == "pull":
+                    operand = pull[:, first : first + width]
+                else:
+                    operand = rhs[loaded.index(k) % 2, :, 0:width]
+                value = inner_rows(source[...], operand)
+            if add:
+                value = value + target[...].astype(F32)
+            target[...] = value.astype(BF16)
+
+        return Scatter(
+            d, 32 if left is None else own, compute, ref["held%d" % k], ref["far%d" % k],
+            ref["first%d" % k], ref["second%d" % k], ref["task_sent"].at[k],
+            ref["task_came"].at[k],
+        )
+
+    scatters = [build(k) for k in range(len(tasks))]
+    sending = [None, None]
+
+    def far_core(k):
+        scatter = scatters[k]
+        width = tasks[k][4]
+        for i, rel in enumerate((3, 1, 2, 0)):
+            slot = i % 2
+            buffer = sends.at[slot, pl.ds(0, scatter.count), pl.ds(0, width)]
+            if sending[slot] is not None:
+                sending[slot].wait_send()
+            scatter.compute(scatter.away[rel], buffer, False)
+            copy = scatter.to_core(buffer, rel)
+            copy.start()
+            sending[slot] = copy
+
+    stage, stage_wait = ref["stage"], [None, None]
+
+    def finish(k):
+        scatter = scatters[k]
+        name, width, column = tasks[k][0], tasks[k][4], tasks[k][5]
+        slot = k % 2
+        if stage_wait[slot] is not None:
+            stage_wait[slot].wait()
+        view = stage.at[slot, pl.ds(0, scatter.count), pl.ds(0, width)]
+        scatter.finish(view)
+        target = ref["grad_" + name].at[:, pl.ds(column, width)]
+        copy = pltpu.make_async_copy(view, target, store_sem.at[slot])
+        copy.start()
+        stage_wait[slot] = copy
+
+    dots, dots_in = ref["dots_row"], ref["dots_in"]
+    for q in range(count // 128):
+        turned = jnp.transpose(ref["dots"][q * 128 : (q + 1) * 128, :])
+        dots[:, q * 128 : (q + 1) * 128] = turned[0:8, :]
+
+    def dots_copy(k):
+        return pltpu.make_async_remote_copy(
+            src_ref=dots, dst_ref=dots_in.at[k], send_sem=ref["dots_sent"].at[k],
+            recv_sem=ref["dots_came"].at[k], device_id={"mp": near if k == 0 else apart},
+            device_id_type=MESH,
+        )
+
+    def dots_add(k):
+        dots_copy(k).wait()
+        dots[...] += dots_in[k]
+
+    dots_copy(0).start()
+    gain = ref["gain"]
+    gain[...] = jnp.zeros_like(gain)
+    for c in range(halves):
+
+        def body(j, c=c):
+            rows = pl.ds(pl.multiple_of(j * part, part), part)
+            for q in range(step // 256):
+                tokens = pl.ds(c * step + q * 256, 256)
+                value = inner_cols(pull[tokens, :], w_in[rows, :])
+                fold.parts[c, j, q * 256 : (q + 1) * 256, :] = value.astype(BF16)
+                gain[:, rows] += jnp.sum(
+                    (value * norm1[tokens, rows].astype(F32)).reshape(-1, 8, part), axis=0
+                )
+
+        tile_loop(mp, body)
+        if c == 0:
+            dots_add(0)
+            dots_copy(1).start()
+        fold.start(c)
+
+    small, small_in = ref["small"], ref["small_in"]
+    small[...] = ref["small_start"][...]
+    small[0:1, :] = jnp.sum(gain[...], axis=0, keepdims=True) / ref["gains"][0:1, :]
+    targets = (
+        {"dp": by_core}, {"dp": by_x}, {"dp": by_y}, {"mp": near}, {"mp": apart},
+    )
+
+    def small_copy(k):
+        rows = pl.ds(0, 16 if k < 3 else 8)
+        return pltpu.make_async_remote_copy(
+            src_ref=small.at[rows, :], dst_ref=small_in.at[k, rows, :],
+            send_sem=ref["small_sent"].at[k], recv_sem=ref["small_came"].at[k],
+            device_id=targets[k], device_id_type=MESH,
+        )
+
+    def small_add(k):
+        rows = 16 if k < 3 else 8
+        small_copy(k).wait()
+        small[0:rows, :] += small_in[k, 0:rows, :]
+
+    def local_copy(c):
+        return pltpu.make_async_copy(
+            ref["local"].at[pl.ds(c * step, step), :], ref["near_local"], ref["local_sem"]
+        )
+
+    local_copy(0).start()
+
+    def input_grad(c):
+        fold.finish(c)
+        local_copy(c).wait()
+
+        def body(t):
+            rows = rows_at(t, TILE)
+            base = pl.ds(pl.multiple_of(c * step + t * TILE, TILE), TILE)
+            s1 = ref["s1"][base, :][:, 0:1]
+            dot = ref["dots_col"][base, :][:, 0:1]
+            grad = (
+                ref["near_local"][rows, :]
+                + s1 * (fold.total(c, rows) * ref["mine"][0:1, :])
+                - ref["x"][base, :].astype(F32) * (s1 * s1 * dot * (1.0 / features))
+            )
+            ref["grad_x"][base, :] = grad.astype(BF16)
+
+        tile_loop(step // TILE, body)
+        if c + 1 < halves:
+            local_copy(c + 1).start()
+
+    def dots_back():
+        for q in range(count // 128):
+            wide = jnp.broadcast_to(dots[0:1, q * 128 : (q + 1) * 128], (128, 128))
+            ref["dots_col"][q * 128 : (q + 1) * 128, :] = jnp.transpose(wide)
+
+    small_copy(0).start()
+    last = len(tasks) - 1
+    for k in range(len(tasks)):
+        if k in loaded:
+            load(k).wait()
+        far_core(k)
+        if k == 0:
+            for i in range(3):
+                small_add(i)
+                if i < 2:
+                    small_copy(i + 1).start()
+        scatters[k].near_core()
+        if k in loaded and loaded.index(k) + 2 < len(loaded):
+            load(loaded[loaded.index(k) + 2]).start()
+        if k == 0:
+            dots_add(1)
+            dots_back()
+        if k == 1:
+            fold.step(0, 1)
+        if k == 2:
+            fold.step(0, 2)
+        if k == 3:
+            input_grad(0)
+        if k == 4:
+            fold.step(1, 1)
+        if k == 6:
+            fold.step(1, 2)
+        if k == 8:
+            input_grad(1)
+            small_copy(3).start()
+        if k > 0:
+            scatters[k - 1].onward()
+        if k > 5:
+            finish(k - 6)
+    scatters[last].onward()
+    small_add(3)
+    small_copy(4).start()
+    for k in range(last - 5, last + 1):
+        finish(k)
+    small_add(4)
+    for copy in stage_wait:
+        copy.wait()
+    for copy in sending:
+        copy.wait_send()
+    for scatter in scatters:
+        scatter.drain()
+    for c in range(halves):
+        fold.drain(c)
+
+
+def tail(mp, pull, w_in, norm1, norm2, pulled, grady, hidden, gbo, mixed, gates, dots, s1, x,
+         local, gains, mine, small):
+    count, part = x.shape
+    features = part * mp
+    own = features // 8
+    halves = 2
+    step = count // halves
+    widths = {
+        "gate": hidden.shape[1], "up": hidden.shape[1], "down": hidden.shape[1],
+        "in": pull.shape[1], "out": mixed.shape[1], "block": pull.shape[1],
+    }
+    heights = {name: 32 if name == "block" else own for name in widths}
+    operands = {
+        "gate": ("norm2", "pulled", 0), "up": ("norm2", "pulled", hidden.shape[1]),
+        "down": ("grady", "hidden", 0), "in": ("norm1", "pull", 0), "out": ("gbo", "mixed", 0),
+        "block": (None, "gates", 0),
+    }
+    tasks = []
+    for name, width in widths.items():
+        left, right, first = operands[name]
+        pieces = 1 if name == "out" else 2
+        for piece in range(pieces):
+            column = piece * (width // pieces)
+            tasks.append((name, left, right, first + column, width // pieces, column))
+    widest = max(t[4] for t in tasks)
+    dma = pltpu.SemaphoreType.DMA
+    any_, vmem = pl.BlockSpec(memory_space=pl.ANY), pl.BlockSpec(memory_space=pltpu.VMEM)
+    ins = [
+        ("pull", pull, vmem), ("w_in", w_in, vmem), ("norm1", norm1, vmem),
+        ("norm2", norm2, any_), ("pulled", pulled, any_), ("grady", grady, any_),
+        ("hidden", hidden, any_), ("gbo", gbo, any_), ("mixed", mixed, any_),
+        ("gates", gates, vmem), ("dots", dots, vmem), ("s1", s1, vmem), ("x", x, vmem),
+        ("local", local, any_), ("gains", gains, vmem), ("mine", mine, vmem),
+        ("small_start", small, vmem),
+    ]
+    outs = [("grad_x", jax.ShapeDtypeStruct((count, part), BF16), vmem)]
+    for name, width in widths.items():
+        outs.append(("grad_" + name, jax.ShapeDtypeStruct((heights[name], width), F32), any_))
+    outs.append(("small", jax.ShapeDtypeStruct((16, features), F32), vmem))
+    scratch = [
+        ("parts", pltpu.VMEM((halves, mp, step, part), BF16)),
+        ("rights", pltpu.VMEM((halves, mp - 1, step, part), BF16)),
+        ("lefts", pltpu.VMEM((halves, mp - 1, step, part), BF16)),
+        ("rhs", pltpu.VMEM((2, count, widest), BF16)),
+        ("lhs", pltpu.VMEM((2, count, own), BF16)),
+        ("sends", pltpu.VMEM((2, own, widest), BF16)),
+        ("stage", pltpu.VMEM((2, own, widest), F32)),
+        ("near_local", pltpu.VMEM((step, part), F32)),
+        ("local_sem", dma),
+        ("gain", pltpu.VMEM((8, features), F32)),
+        ("dots_row", pltpu.VMEM((8, count), F32)),
+        ("dots_in", pltpu.VMEM((2, 8, count), F32)),
+        ("dots_col", pltpu.VMEM((count, 128), F32)),
+        ("small_in", pltpu.VMEM((5, 16, features), F32)),
+        ("fold_sent", dma((halves, mp))),
+        ("fold_right", dma((halves, mp))),
+        ("fold_left", dma((halves, mp))),
+        ("task_sent", dma((len(tasks), 8))),
+        ("task_came", dma((len(tasks), 8))),
+        ("load_sem", dma((2,))),
+        ("lhs_sem", dma((2,))),
+        ("store_sem", dma((2,))),
+        ("dots_sent", dma((2,))),
+        ("dots_came", dma((2,))),
+        ("small_sent", dma((5,))),
+        ("small_came", dma((5,))),
+    ]
+    for k, (name, _, _, _, width, _) in enumerate(tasks):
+        tall = heights[name]
+        scratch.append(("held%d" % k, pltpu.VMEM((4, tall, width), BF16)))
+        for kind in ("far", "first", "second"):
+            scratch.append(("%s%d" % (kind, k), pltpu.VMEM((tall, width), BF16)))
+    names = [i[0] for i in ins] + [o[0] for o in outs] + [k[0] for k in scratch]
+    return pl.pallas_call(
+        functools.partial(tail_kernel, mp, tuple(tasks), tuple(names)),
+        in_specs=[i[2] for i in ins],
+        out_specs=[o[2] for o in outs],
+        out_shape=[o[1] for o in outs],
+        scratch_shapes=[k[1] for k in scratch],
+        compiler_params=pltpu.CompilerParams(
+            collective_id=1, has_side_effects=True, vmem_limit_bytes=63 * 1024 * 1024
+        ),
+        name="tail",
+    )(*[i[1] for i in ins])
+
+
 def make_masks(row_lengths, count):
     ends = jnp.cumsum(row_lengths)
     places = jnp.arange(-TAPS, count, dtype=jnp.int32)
@@ -1113,108 +1787,103 @@
     def mine(values):
         return lax.dynamic_slice_in_dim(values, spot, part, values.ndim - 1)
 
-    gates = pair_gather(jnp.concatenate([recur_gate, input_gate], axis=1), "dp", dp)
-    w_in = square_gather(jnp.concatenate([rnn_in, branch_gate], axis=1), "dp", dp)
-    w_out = square_gather(after(rnn_out.T, w_in), "dp", dp)
+    in_shard = jnp.concatenate([rnn_in, branch_gate], axis=1)
+    out_shard = rnn_out.T
+    gates_shard = jnp.concatenate([recur_gate, input_gate], axis=1)
     up = jnp.concatenate([mlp_gate, mlp_up], axis=1)
     down = mlp_down.T
-    if dp != 8:
+    if dp == 8:
+        gates_shard = jnp.pad(gates_shard, ((0, 32 - span // 8), (0, 0)))
+    else:
+        in_shard, out_shard = square_gather(in_shard, "dp", dp), square_gather(out_shard, "dp", dp)
         up, down = square_gather(up, "dp", dp), square_gather(down, "dp", dp)
-
-    in_parts = cut(inputs)
-    wholes = []
-    for c in range(CHUNKS):
-        source = in_parts[c] if c == 0 else after(in_parts[c], wholes[-1])
-        wholes.append(line_gather(source, "mp", mp))
+        gates_shard = pair_gather(gates_shard, "dp", dp).reshape(8, span // 8, 2 * width)
+        gates_shard = jnp.pad(gates_shard, ((0, 0), (0, 32 - span // 8), (0, 0)))
+        gates_shard = gates_shard.reshape(256, 2 * width)
+
     mask, live = make_masks(lengths[0], count)
-    masks = cut(mask)
     mask_tail = jnp.concatenate([mask, jnp.zeros((8, LANES), F32)], axis=0)
     tail_masks = [mask_tail[c * step : (c + 1) * step + 8] for c in range(CHUNKS)]
     live = jnp.broadcast_to(live[:, None], (count, LANES)).astype(F32)
-    dense = dense_gates(gates, width)
-
-    blank = jnp.zeros((8, width), F32)
-    halo, start = blank, blank
-    halos, starts, boths, saves, mixes, norms, scales1 = [], [], [], [], [], [], []
-    for c in range(CHUNKS):
-        values = wholes[c].astype(F32)
-        s1 = lax.rsqrt(jnp.mean(values * values, axis=1, keepdims=True) + EPS)
-        normed = (values * s1 * gains[0]).astype(BF16)
-        both = matmul(normed, w_in)
-        mixed, conv, r, i, state, end = rnn_forward(
-            both, halo, start, masks[c], dense, rnn_params
-        )
-        halos.append(halo)
-        starts.append(start)
-        halo, start = both[-8:, :width], end
-        boths.append(both)
-        saves.append((conv, r, i, state))
-        mixes.append(mixed)
-        norms.append(normed)
-        scales1.append(s1)
-
+    w_in, w_out, dense, normed, both, conv, r, i, state, mixed, s1 = head(
+        dp, mp, 4, inputs, gains, rnn_params, mask, in_shard, out_shard, gates_shard, span
+    )
     output, gm, gbo, local, hidden, pulled, normed2, grad_y, gain2 = middle(
-        dp, mp, 4, jnp.concatenate(mixes), inputs, cotangent, live, gains, mine(gains), w_out,
+        dp, mp, 4, mixed, inputs, cotangent, live, gains, mine(gains), w_out,
         up, down,
     )
-    gms, locals_ = cut(gm), cut(local)
-
-    grad_up = square_scatter(
-        inner_rows(normed2, pulled).astype(BF16), "dp", dp
-    )
-    grad_down = square_scatter(
-        inner_rows(grad_y, hidden).astype(BF16), "dp", dp
-    )
-    grad_out = square_scatter(
-        inner_rows(gbo, jnp.concatenate(mixes)).astype(BF16), "dp", dp
-    )
-
-    back, tail = blank, blank
-    pulls, rates, grads_in = [None] * CHUNKS, [None] * CHUNKS, [None] * CHUNKS
-    gain1_total, params_total = 0.0, 0.0
+    blank = jnp.zeros((8, width), F32)
+    back, tail_rows = blank, blank
+    pulls, rates, dots = [None] * CHUNKS, [None] * CHUNKS, [None] * CHUNKS
+    params_total = 0.0
+    gms, boths = cut(gm), cut(both)
+    saves = list(zip(cut(conv), cut(r), cut(i), cut(state)))
     for c in reversed(range(CHUNKS)):
-        pull, rate, dparams, back, tail = rnn_backward(
-            gms[c], boths[c], halos[c], starts[c], saves[c], tail_masks[c], dense, rnn_params,
-            back, tail,
+        low = c * step
+        halo = blank if c == 0 else both[low - 8 : low, :width]
+        start = blank if c == 0 else state[low - 8 : low]
+        pull, rate, dparams, back, tail_rows, dot = rnn_backward(
+            gms[c], boths[c], halo, start, saves[c], tail_masks[c], dense, rnn_params,
+            back, tail_rows,
         )
         params_total = params_total + dparams
-        pulls[c], rates[c] = pull, rate
-        gn1_part = inner_cols(pull, w_in).astype(BF16)
-        values = wholes[c].astype(F32)
-        scaled = gn1_part.astype(F32) * values
-        gain1_total = gain1_total + jnp.sum(scaled * scales1[c], axis=0)
-        dots = jnp.sum(scaled * gains[0], axis=1).reshape(8, -1)
-        mean = (line_sum(dots, "mp", mp) / features).reshape(-1, 1)
-        gn1_mine = line_scatter(gn1_part, "mp", mp)
-        s1 = scales1[c]
-        grad = (
-            locals_[c]
-            + s1 * (gn1_mine * mine(gains[0]))
-            - in_parts[c].astype(F32) * (s1 * s1 * s1 * mean)
-        )
-        grads_in[c] = grad.astype(BF16)
-
-    grad_in = square_scatter(
-        inner_rows(jnp.concatenate(norms), jnp.concatenate(pulls)).astype(BF16), "dp", dp
-    )
-    convs = jnp.concatenate([s[0] for s in saves]).astype(BF16)
-    grad_gates = pair_scatter(
-        diagonal_blocks(inner_rows(convs, jnp.concatenate(rates)), span), "dp", dp
-    )
-    grad_params = line_sum(params_total, "dp", dp)
-    grad_gain1 = line_sum(line_sum(gain1_total.reshape(8, -1), "dp", dp), "mp", mp)
-    grad_gain2 = line_sum(jnp.sum(gain2, axis=0).reshape(8, -1), "dp", dp)
+        pulls[c], rates[c], dots[c] = pull, rate, dot
+    pull = jnp.concatenate(pulls)
+    dots = jnp.concatenate(dots)
+    grad_gates = diagonal_blocks(inner_rows(conv.astype(BF16), jnp.concatenate(rates)), span)
+    gain2 = jnp.sum(gain2, axis=0, keepdims=True)
+
+    if dp == 8:
+        rows = span // dp
+        padded = jnp.pad(
+            grad_gates.astype(BF16).reshape(dp, rows, 2 * width), ((0, 0), (0, 32 - rows), (0, 0))
+        ).reshape(dp * 32, 2 * width)
+        small = jnp.concatenate(
+            [
+                jnp.zeros((1, features), F32), gain2 / mp, jnp.zeros((6, features), F32),
+                jnp.pad(params_total, ((0, 0), (0, features - width))),
+            ]
+        )
+        input_grad, grad_gate, grad_up, grad_down, grad_in, grad_out, grad_gates, small = tail(
+            mp, pull, w_in, normed, normed2, pulled, grad_y, hidden, gbo, mixed, padded, dots,
+            s1, inputs, local, gains, mine(gains), small,
+        )
+        grad_gates = grad_gates[:rows]
+        grad_gains, grad_params = small[0:2], small[8:16, :width]
+    else:
+        parts = []
+        gain1 = 0.0
+        norms, s1 = cut(normed), s1[:, 0:1]
+        for c in range(CHUNKS):
+            gn1_part = inner_cols(pulls[c], w_in).astype(BF16)
+            gain1 = gain1 + jnp.sum(gn1_part.astype(F32) * norms[c].astype(F32), axis=0)
+            parts.append(line_scatter(gn1_part, "mp", mp))
+        dot = line_sum(dots[:, 0].reshape(8, -1), "mp", mp).reshape(-1, 1)
+        input_grad = (
+            local + s1 * (jnp.concatenate(parts) * mine(gains[0]))
+            - inputs.astype(F32) * (s1 * s1 * dot / features)
+        ).astype(BF16)
+        grad_both = square_scatter(inner_rows(normed2, pulled).astype(BF16), "dp", dp)
+        grad_gate, grad_up = grad_both[:, :hidden_width], grad_both[:, hidden_width:]
+        grad_down = square_scatter(inner_rows(grad_y, hidden).astype(BF16), "dp", dp)
+        grad_out = square_scatter(inner_rows(gbo, mixed).astype(BF16), "dp", dp)
+        grad_in = square_scatter(inner_rows(normed, pull).astype(BF16), "dp", dp)
+        grad_gates = pair_scatter(grad_gates, "dp", dp)
+        grad_params = line_sum(params_total, "dp", dp)
+        both_gains = jnp.concatenate([(gain1 / gains[0])[None], gain2])
+        both_gains = line_sum(both_gains, "dp", dp)
+        grad_gains = jnp.concatenate([line_sum(both_gains[:1], "mp", mp), both_gains[1:]])
     return (
         output,
-        jnp.concatenate(grads_in),
-        jnp.stack([grad_gain1.reshape(-1), grad_gain2.reshape(-1)]),
+        input_grad,
+        grad_gains,
         grad_params,
         grad_in[:, :width],
         grad_in[:, width:],
         grad_gates[:, :width],
         grad_gates[:, width:],
-        grad_up[:, :hidden_width],
-        grad_up[:, hidden_width:],
+        grad_gate,
+        grad_up,
         grad_out.T,
         grad_down.T,
     )

time: 890 us -> 683 us (0.77)
  Pallas kernels: 423 us -> 639 us
  waiting for transfers between devices: 186 us -> 0 us
  starting transfers between devices: 97.3 us -> 0 us
  matrix products: 68.7 us -> 3.68 us
  local copies, waits for them, and re-layouts: 63.6 us -> 21.9 us
  other arithmetic: 42.4 us -> 6.81 us
    pallas_call x2, Pallas kernels: 34.7 us -> 243 us  [the longest x1 147 us: tail(): pl.pallas_call(functools.partial(tail_kernel, mp, tuple(tasks), tuple(nam...]
    ppermute x75 -> x0, waiting for transfers between devices: 186 us -> none  [the longest x4 52.3 us: square_scatter(): by_y = lax.ppermute(to_y.astype(BF16), axis, swap(size, 4))]
    ppermute x75 -> x0, starting transfers between devices: 97.3 us -> none  [the longest x6 29.1 us: line_scatter(): lax.ppermute(going.astype(BF16), axis, [(i, i + 1) for i in range(step)])]
    dot_general x5 -> x1, matrix products: 41.6 us -> 3.68 us  [inner_rows(): lax.dot_general(left, right, (((0,), (0,)), ((), ())), preferred_element_...]
    dot_general x4 -> x0, matrix products: 27.1 us -> none  [the longest x2 13.8 us: matmul(): return jnp.dot(left, right, preferred_element_type=F32)]
    convert_element_type x19 -> x1, other arithmetic: 25.1 us -> 0.22 us  [per_device(): grad_gates.astype(BF16).reshape(dp, rows, 2 * width)]
    dynamic_slice x4 -> x0, local copies, waits for them, and re-layouts: 9.12 us -> none  [the longest x1 4.71 us: square_scatter(): going = lax.dynamic_index_in_dim(split, 1 - core, 1, keepdims=False)]
    unnamed x116 -> x38, local copies, waits for them, and re-layouts: 20.3 us -> 11.5 us
  transfers between devices with their start and end apart: 75 -> 0, of which waited for: 24 -> 0; matrix products, arithmetic and copies ran while one was open for 13% -> 0% of each run, Pallas kernels for 0% -> 0%
where the time goes in v3:
time: 683 us; the launch traced here: 673 us
  Pallas kernels  639 us (94%)
  local copies, waits for them, and re-layouts  21.9 us (3%)
    pallas_call x1, Pallas kernels, middle(): pl.pallas_call(functools.partial(middle_kernel, dp, mp, chunks), in_specs...  357 us
    pallas_call x1, Pallas kernels, tail(): pl.pallas_call(functools.partial(tail_kernel, mp, tuple(tasks), tuple(nam...  147 us
    pallas_call x1, Pallas kernels, head(): pl.pallas_call(functools.partial(head_kernel, dp, mp, tuple(names)), in_s...  96.3 us
    pallas_call x1, Pallas kernels, rnn_backward(): pl.pallas_call(rnn_backward_kernel, out_shape=(jax.ShapeDtypeStruct((coun...  39.4 us

profile of v3, /device:TPU:0, one launch (start us, length us, event | category | flops | bytes accessed | tf_op | source)
XLA Modules:
  0.0 673.0 jit_solution(16354289915208805477)
XLA Ops:
  1.7 1.0 copy.44.refs_3_
  2.7 2.1 pad_maximum_fusion.1.refs_4_
  4.8 1.9 copy.43
  7.3 96.3 %head.1 = (bf16[2048,1280]{1,0:T(8,128)(2,1)}, bf16[2048,640]{1,0:T(8,128)(2,1)}, bf16[640,1280]{1,0:T(8,128)(2,1)}, bf16[1024,2048]{1,0:T(8,128)(2,1)}, f32[102...) custom-call(bf16[1024,512]{1,0:T(8,128)(2,1)} %refs_12_.1, ...), custom_call_target="tpu_custom_call" | custom-call | tf_op jit(solution)/shard_map/head/pallas_call | solution.py:908
  103.7 1.3 constant_dynamic-slice_fusion.refs_5_.refs_15_
  105.0 1.0 broadcast_in_dim.54.refs_3_
  106.0 1.3 pad_maximum_fusion.refs_7_
  107.3 1.2 copy.45
  108.5 357.0 %middle.1 = (bf16[1024,512]{1,0:T(8,128)(2,1)}, f32[1024,640]{1,0:T(8,128)}, bf16[1024,2048]{1,0:T(8,128)(2,1)}, f32[1024,512]{1,0:T(8,128)}, bf16[1024,1536]{1,...) custom-call(bf16[1024,640]{1,0:T(8,128)(2,1)} %get-tuple-element.44., ...), custom_call_target="tpu_custom_call" | custom-call | tf_op jit(solution)/shard_map/middle/pallas_call | solution.py:1256
  465.5 0.8 concatenate.18.mask_ref
  467.0 39.4 %rnn_backward.1 = (bf16[1024,1280]{1,0:T(8,128)(2,1)}, bf16[1024,1280]{1,0:T(8,128)(2,1)}, f32[8,640]{1,0:T(8,128)}, f32[8,640]{1,0:T(8,128)}, f32[8,640]{1,0:T(8,128)}, /*index=5*/f32[1024,128]{1,0:T(8,128)}) custom-call(f32[1024,640]{1,0:T(8,128)} %get-tuple-element.47.gm_ref, f32[1024,1280]{1,0:T(8,128)} %get-tuple-element.48.both_ref, ...), custom_call_target="tpu_custom_call" | custom-call | flops 1677721600 | bytes 23592960 | tf_op jit(solution)/shard_map/rnn_backward/pallas_call | solution.py:440
  506.5 1.5 select_maximum_fusion.refs_16_
  507.9 3.7 fusion
  512.0 0.9 pad.14
  512.9 146.6 %tail.1 = (bf16[1024,512]{1,0:T(8,128)(2,1)}, f32[256,1536]{1,0:T(8,128)}, f32[256,1536]{1,0:T(8,128)}, f32[256,1536]{1,0:T(8,128)}, f32[256,1280]{1,0:T(8,128)}...) custom-call(bf16[1024,1280]{1,0:T(8,128)(2,1)} %get-tuple-element.54.refs_0_, ...), custom_call_target="tpu_custom_call" | custom-call | tf_op jit(solution)/shard_map/tail/pallas_call | solution.py:1728
  659.5 3.2 copy.48
  662.7 1.1 fusion.16
  663.8 1.1 copy.47
  665.5 1.3 slice.54
  666.9 1.4 slice.53
  668.3 1.0 copy.53
  669.3 1.0 copy.54
  670.3 1.1 copy.55
  671.4 1.1 copy.56
  (49 shorter events, 3.5 us)
Async XLA Ops:
  0.6 6.0 copy-start.14
  0.7 6.0 copy-start.13
  2.7 103.2 %copy-start.8 = (bf16[256,1536]{1,0:T(8,128)(2,1)S(1)}, bf16[256,1536]{1,0:T(8,128)(2,1)}, u32[]{:S(2)}) copy-start(bf16[256,1536]{1,0:T(8,128)(2,1)} %param.23) | copy-start | bytes 2359300
  2.7 103.2 %copy-start.9 = (bf16[256,1536]{1,0:T(8,128)(2,1)S(1)}, bf16[256,1536]{1,0:T(8,128)(2,1)}, u32[]{:S(2)}) copy-start(bf16[256,1536]{1,0:T(8,128)(2,1)} %param.22) | copy-start | bytes 2359300
  7.3 100.0 %copy-start.7 = (bf16[1536,256]{1,0:T(8,128)(2,1)S(1)}, bf16[1536,256]{1,0:T(8,128)(2,1)}, u32[]{:S(2)}) copy-start(bf16[1536,256]{1,0:T(8,128)(2,1)} %param.25) | copy-start | bytes 2359300
  108.5 357.1 %copy-start.1 = (f32[1024,8]{1,0:T(8,128)S(1)}, f32[1024,8]{1,0:T(8,128)}, u32[]{:S(2)}) copy-start(f32[1024,8]{1,0:T(8,128)} %copy.44.refs_3_) | copy-start | bytes 98308
  467.0 39.4 %copy-start.12 = (f32[8,2048]{1,0:T(8,128)S(1)}, f32[8,2048]{1,0:T(8,128)}, u32[]{:S(2)}) copy-start(f32[8,2048]{1,0:T(8,128)} %get-tuple-element.66) | copy-start | bytes 196612
  467.0 41.0 %copy-start = (f32[1024,640]{1,0:T(8,128)S(1)}, f32[1024,640]{1,0:T(8,128)}, u32[]{:S(2)}) copy-start(f32[1024,640]{1,0:T(8,128)} %get-tuple-element.49.conv_ref) | copy-start | bytes 7864324
  659.5 3.2 copy-start.4
  659.5 4.3 copy-start.10
  662.7 2.2 copy-start.11
  662.7 5.7 copy-start.5
  663.8 6.5 copy-start.3
  664.9 4.4 copy-start.6
  669.3 2.1 copy-start.2

commit v4 on v3

--- a/solution.py
+++ b/solution.py
@@ -684,6 +684,98 @@
             self.copy(self.shard, self.d, self.by_core, k, 0).wait_send()
 
 
+class Scatter:
+    def __init__(self, d, count, compute, held, far, first, second, sent, came):
+        self.d, self.count, self.compute = d, count, compute
+        self.held, self.far_in, self.first_in, self.second_in = held, far, first, second
+        self.sent, self.came = sent, came
+        self.core, self.by_core, by_x, by_y = partners(d)
+        even = self.core == 0
+        self.first = jnp.where(even, by_y, by_x)
+        self.second = jnp.where(even, by_x, by_y)
+        self.first_at, self.second_at = 2 - self.core, 1 + self.core
+        other = partners(self.by_core)
+        self.away = (self.by_core, other[2], other[3], partners(other[2])[3])
+        self.distant = partners(by_x)[3]
+
+    def owners(self):
+        return [self.away[k] for k in (3, 1, 2, 0)] + [
+            self.distant, self.first, self.d, self.second
+        ]
+
+    def copy(self, src, dst, target, sent, came):
+        return pltpu.make_async_remote_copy(
+            src_ref=src, dst_ref=dst, send_sem=self.sent.at[sent], recv_sem=self.came.at[came],
+            device_id={"dp": target}, device_id_type=MESH,
+        )
+
+    def to_core(self, buffer, k):
+        return self.copy(buffer, self.held(k), self.by_core, k, k)
+
+    def to_far(self):
+        return self.copy(self.held(3), self.far_in, self.first, 4, 4)
+
+    def to_first(self):
+        return self.copy(self.held(self.first_at), self.first_in, self.first, 5, 5)
+
+    def to_second(self):
+        return self.copy(self.held(self.second_at), self.second_in, self.second, 6, 6)
+
+    def far_core(self, buffers, sending):
+        for slot, k in enumerate((3, 1, 2, 0)):
+            if sending[slot] is not None:
+                sending[slot].wait_send()
+            self.compute(self.away[k], buffers[slot], False)
+            copy = self.to_core(buffers[slot], k)
+            copy.start()
+            sending[slot] = copy
+
+    def add_block(self, k, came, owner):
+        self.copy(self.held(k), self.held(k), self.by_core, k, came).wait_recv()
+        self.compute(owner, self.held(k), True)
+
+    def near_core(self):
+        self.add_block(3, 3, self.distant)
+        self.to_far().start()
+        self.add_block(self.first_at, self.first_at, self.first)
+        self.to_first().start()
+        self.add_block(0, 0, self.d)
+        self.add_block(self.second_at, self.second_at, self.second)
+
+    def onward(self):
+        self.to_far().wait_recv()
+        held = self.held(self.second_at)
+
+        def body(t):
+            rows = rows_at(t, 16)
+            held[rows, :] = (
+                held[rows, :].astype(F32) + self.far_in[rows, :].astype(F32)
+            ).astype(BF16)
+
+        tile_loop(self.count // 16, body)
+        self.to_second().start()
+
+    def finish(self, target):
+        self.to_first().wait_recv()
+        self.to_second().wait_recv()
+        held = self.held(0)
+
+        def body(t):
+            rows = rows_at(t, 16)
+            target[rows, :] = (
+                held[rows, :].astype(F32)
+                + self.first_in[rows, :].astype(F32)
+                + self.second_in[rows, :].astype(F32)
+            )
+
+        tile_loop(self.count // 16, body)
+
+    def drain(self):
+        self.to_far().wait_send()
+        self.to_first().wait_send()
+        self.to_second().wait_send()
+
+
 def head_kernel(dp, mp, names, *refs):
     ref = dict(zip(names, refs))
     blocks, w_in, norm, both = ref["blocks"], ref["w_in_here"], ref["norm"], ref["both_here"]
@@ -721,7 +813,10 @@
         own_block(c).start()
     pl.semaphore_wait(barrier, count)
 
-    wholes = (("gates_shard", ref["gates_here"]), ("in_shard", w_in), ("out_shard", ref["w_out"]))
+    wholes = (
+        ("gates_shard", ref["gates_here"]), ("in_shard", w_in), ("out_shard", ref["w_out"]),
+        ("gate_shard", ref["w_gate"]),
+    )
     if square:
         squares = [
             Square(
@@ -730,7 +825,7 @@
             )
             for k, (name, whole) in enumerate(wholes)
         ]
-        for item in squares:
+        for item in squares[:2]:
             item.start()
     else:
         loads = [
@@ -819,6 +914,7 @@
     if square:
         for item in squares[:2]:
             item.step_one()
+        squares[2].start()
         for item in squares[:2]:
             item.step_two()
     gather.finish(0)
@@ -829,7 +925,6 @@
             if square:
                 for item in squares[:2]:
                     item.finish()
-                squares[2].step_one()
             else:
                 for item in loads:
                     item.wait()
@@ -840,9 +935,14 @@
             ]
             for copy in pass_on:
                 copy.start()
+        if c == 3 and square:
+            squares[3].step_one()
+        compute(c)
+        if c == 0 and square:
+            squares[2].step_one()
+            squares[3].start()
         if c == 1 and square:
             squares[2].step_two()
-        compute(c)
         if c + 3 < chunks:
             begin(c + 3)
         if c + 1 < chunks:
@@ -850,7 +950,9 @@
                 gather.step(c + 1, s)
             gather.finish(c + 1)
     if square:
+        squares[3].step_two()
         squares[2].finish()
+        squares[3].finish()
         for item in squares:
             item.drain()
     for copy in pass_on:
@@ -862,7 +964,9 @@
         gather.drain(c)
 
 
-def head(dp, mp, chunks, x, gains, params, mask, in_shard, out_shard, gates_shard, span):
+def head(
+    dp, mp, chunks, x, gains, params, mask, in_shard, out_shard, gate_shard, gates_shard, span
+):
     count, part = x.shape
     features, width = part * mp, params.shape[1]
     step = count // chunks
@@ -871,12 +975,13 @@
     ins = [
         ("x", x, any_), ("gains", gains, vmem), ("params", params, vmem), ("mask", mask, vmem),
         ("in_shard", in_shard, any_), ("out_shard", out_shard, any_),
-        ("gates_shard", gates_shard, any_),
+        ("gate_shard", gate_shard, any_), ("gates_shard", gates_shard, any_),
     ]
+    gate_width = gate_shard.shape[1]
     shape = jax.ShapeDtypeStruct
     outs = [
         ("w_in", shape((features, 2 * width), BF16)), ("w_out", shape((features, width), BF16)),
-        ("dense", shape((width, 2 * width), BF16)), ("norm_out", shape((count, features), BF16)),
+        ("w_gate", shape((features, gate_width), BF16)), ("dense", shape((width, 2 * width), BF16)), ("norm_out", shape((count, features), BF16)),
         ("both_out", shape((count, 2 * width), F32)), ("conv_out", shape((count, width), F32)),
         ("r_out", shape((count, width), F32)), ("i_out", shape((count, width), F32)),
         ("state_out", shape((count, width), F32)), ("mixed_out", shape((count, width), BF16)),
@@ -901,7 +1006,7 @@
         ("high", pltpu.VMEM((step, width), BF16)), ("low", pltpu.VMEM((step, width), BF16)),
         ("decay", columns), ("drive", columns),
         ("spread_sent", dma((chunks, 2 * mp))), ("spread_came", dma((chunks, mp))),
-        ("square_sent", dma((3, 8))), ("square_came", dma((3, 8))), ("square_own", dma((3,))),
+        ("square_sent", dma((4, 8))), ("square_came", dma((4, 8))), ("square_own", dma((4,))),
         ("load_sem", dma((chunks,))), ("store_sem", dma((2, 8))), ("pass_sem", dma((2,))),
     ]
     names = [i[0] for i in ins] + [o[0] for o in outs] + [k[0] for k in scratch]
@@ -918,22 +1023,46 @@
     )(*[i[1] for i in ins])
 
 
+MIDDLE_ORDER = (
+    ("d", 0, 0), ("A", 0, 0), ("d", 0, 1), ("d", 0, 2), ("a", 1, 0), ("d", 1, 0), ("a", 2, 0),
+    ("d", 0, 3), ("J", 0, 0), ("d", 2, 0), ("e", 0, 0), ("A", 0, 1), ("e", 1, 0), ("e", 2, 0),
+    ("a", 1, 1), ("d", 1, 2), ("e", 3, 0), ("A", 0, 2), ("S", 1, 0), ("a", 2, 1), ("d", 1, 1),
+    ("S", 2, 0), ("d", 2, 2), ("J", 0, 1), ("d", 3, 0), ("a", 1, 2), ("e", 0, 1), ("S", 3, 0),
+    ("H", 0, 0), ("a", 2, 2), ("d", 1, 3), ("d", 2, 1), ("G", 0, 0), ("d", 3, 2), ("c", 1, 0),
+    ("e", 1, 1), ("J", 0, 2), ("e", 0, 2), ("d", 3, 1), ("e", 2, 1), ("O", 0, 0), ("e", 3, 1),
+    ("b", 1, 0), ("c", 2, 0), ("A", 0, 3), ("e", 1, 2), ("K", 0, 0), ("a", 1, 3), ("b", 2, 0),
+    ("e", 2, 2), ("H", 0, 1), ("d", 2, 3), ("G", 0, 1), ("e", 3, 2), ("O", 0, 1), ("f", 1, 0),
+    ("c", 1, 1), ("a", 2, 3), ("c", 2, 1), ("Y", 0, 0), ("f", 2, 0), ("b", 1, 1), ("J", 0, 3),
+    ("K", 0, 1), ("H", 0, 2), ("e", 0, 3), ("B", 0, 0), ("f", 1, 1), ("G", 0, 2), ("e", 1, 3),
+    ("f", 2, 1), ("c", 1, 2), ("b", 2, 1), ("c", 2, 2), ("B", 0, 1), ("e", 2, 3), ("Y", 0, 1),
+    ("K", 0, 2), ("O", 0, 2), ("e", 3, 3), ("f", 1, 2), ("d", 3, 3), ("H", 0, 3), ("f", 2, 2),
+    ("G", 0, 3), ("b", 1, 2), ("B", 0, 2), ("O", 0, 3), ("D", 0, 0), ("c", 1, 3), ("W", 0, 0),
+    ("D", 0, 1), ("c", 2, 3), ("D", 0, 2), ("K", 0, 3), ("W", 0, 1), ("b", 2, 2), ("D", 0, 3),
+    ("W", 0, 2), ("D", 0, 4), ("Z", 0, 0), ("W", 0, 3), ("f", 1, 3), ("D", 0, 5), ("b", 1, 3),
+    ("f", 2, 3), ("Z", 0, 1), ("b", 2, 3), ("W", 0, 4), ("B", 0, 3), ("W", 0, 5), ("Y", 0, 2),
+    ("Z", 0, 2), ("Y", 0, 3), ("Z", 0, 3), ("Z", 0, 4), ("Z", 0, 5),
+)
+
+
 def middle_kernel(dp, mp, chunks, *refs):
     (
-        mixed_ref, x_ref, cot_ref, live_ref, gains_ref, mine_ref, wout_ref, up_ref, down_ref,
+        mixed_ref, x_ref, cot_ref, live_ref, gains_ref, mine_ref, wout_ref, gate_ref, up_ref,
+        down_ref,
         output_ref, gm_ref, gbo_ref, local_ref, hidden_ref, pulled_ref, norm_ref, grady_ref,
-        gain_ref,
+        grad_gate_ref, grad_up_ref, gain_ref,
         w_up, w_down, cots, mids, gn2s, mid_mine, gn2_mine,
         parts1, rights1, lefts1, parts2, rights2, lefts2, parts3, rights3, lefts3,
         norm, hidden, pulled, gbo, gm, local, out,
         spread_sent, spread_came, fold_sent, fold_right, fold_left,
         square_sent, square_came, square_own, load_sem, store_sem,
+        stage, free_sem, task_sent, task_came, left_sem, right_sem, stage_sem,
     ) = refs
     step, part = x_ref.shape[0] // chunks, x_ref.shape[1]
     features = part * mp
     hidden_width = w_down.shape[1]
     z, d = lax.axis_index("mp"), lax.axis_index("dp")
     square = dp == 8
+    up_half = w_up.at[:, pl.ds(hidden_width, hidden_width)]
 
     folds = [
         Fold(z, mp, p, r, l, fold_sent.at[k], fold_right.at[k], fold_left.at[k])
@@ -968,18 +1097,24 @@
 
     if square:
         squares = [
-            Square(d, up_ref, w_up, square_sent.at[0], square_came.at[0], square_own.at[0]),
-            Square(d, down_ref, w_down, square_sent.at[1], square_came.at[1], square_own.at[1]),
+            Square(
+                d, shard, whole, square_sent.at[k], square_came.at[k], square_own.at[k]
+            )
+            for k, (shard, whole) in enumerate(((up_ref, up_half), (down_ref, w_down)))
         ]
         for item in squares:
             item.start()
     else:
         loads = [
-            pltpu.make_async_copy(up_ref, w_up, square_own.at[0]),
+            pltpu.make_async_copy(up_ref, up_half, square_own.at[0]),
             pltpu.make_async_copy(down_ref, w_down, square_own.at[1]),
         ]
         for item in loads:
             item.start()
+    load_gate = pltpu.make_async_copy(
+        gate_ref, w_up.at[:, pl.ds(0, hidden_width)], square_own.at[2]
+    )
+    load_gate.start()
 
     def chunk_rows(c):
         return pl.ds(c * step, step)
@@ -1004,9 +1139,14 @@
         tile_loop(mp, body)
 
     def branch(c):
+        if c > 1:
+            rs1.drain(c % 2)
         fill(rs1, c % 2, mixed_ref[chunk_rows(c), :], wout_ref)
+        rs1.start(c % 2)
 
     def join(c):
+        rs1.finish(c % 2)
+
         def body(t):
             rows = rows_at(t, TILE)
             base = pl.ds(pl.multiple_of(c * step + t * TILE, TILE), TILE)
@@ -1054,6 +1194,12 @@
             store(pulled, pulled_ref, c, 2).wait()
             for copy in grad_y_copies(c - 1):
                 copy.wait()
+        if c == 0:
+            load_gate.wait()
+            for item in squares if square else ():
+                item.finish()
+            for item in () if square else loads:
+                item.wait()
         ag2.drain(c)
         normalise(c)
         store(norm, norm_ref, c, 0).start()
@@ -1084,27 +1230,37 @@
             rs3.drain(slot)
         fill(rs3, slot, pulled[...], w_up)
         rs3.start(slot)
+        if square and c == chunks - 1:
+            for item in squares:
+                item.drain()
+            for k, other in enumerate(partners(d)[1:]):
+                pl.semaphore_signal(
+                    free_sem.at[k], inc=1, device_id={"dp": other}, device_id_type=MESH
+                )
 
     def mlp_third(c):
         slot = c % 2
         if c > 1:
             rs2.drain(slot)
         fill(rs2, slot, hidden[...], w_down)
+        rs2.start(slot)
 
     def gather_grad(c):
         slot = c % 2
+        rs3.finish(slot)
 
         def body(t):
             rows = rows_at(t, TILE)
             total = rs3.total(slot, rows)
             gn2_mine[slot, rows, :] = total
-            gn2s[slot, z, rows, :] = total.astype(BF16)
+            gn2s[c, z, rows, :] = total.astype(BF16)
 
         tile_loop(tiles, body)
-        ag4.step(slot, 0)
+        ag4.step(c, 0)
 
     def norm_back(c):
         slot = c % 2
+        ag4.finish(c)
         if c > 0:
             store(gbo, gbo_ref, c, 3).wait()
             store(local, local_ref, c, 4).wait()
@@ -1113,7 +1269,7 @@
         def body(t):
             rows = rows_at(t, TILE)
             blocks, s2 = stats(c, rows)
-            grads = [gn2s[slot, j, rows, :].astype(F32) for j in range(mp)]
+            grads = [gn2s[c, j, rows, :].astype(F32) for j in range(mp)]
             scaled = [grads[j] * gains_ref[1:2, block_cols(j)] for j in range(mp)]
             mean = (
                 sum(jnp.sum(scaled[j] * blocks[j], axis=1, keepdims=True) for j in range(mp))
@@ -1141,6 +1297,7 @@
         store(gm, gm_ref, c, 5).start()
 
     def make_output(c):
+        rs2.finish(c % 2)
         if c > 0:
             store(out, output_ref, c, 6).wait()
 
@@ -1151,73 +1308,121 @@
         tile_loop(tiles, body)
         store(out, output_ref, c, 6).start()
 
-    def has(c):
-        return 0 <= c < chunks
-
-    for r in range(chunks + 3):
-        if has(r):
-            if r > 1:
-                rs1.drain(r % 2)
-            branch(r)
-            rs1.start(r % 2)
-            own_cot(r).wait()
-        if has(r - 1):
-            ag3.step(r - 1, 0)
-        if has(r):
-            ag2.step(r, 0)
-        if has(r - 3):
-            gather_grad(r - 3)
-            rs2.start((r - 3) % 2)
-        if r == 0 and square:
-            squares[0].step_one()
-        if r == 1 and square:
-            squares[1].step_one()
-        if r == 2:
-            if square:
+    own = features // 8
+    count_tasks = 2 * hidden_width // part
+    scatters, sending = [], [None] * 4
+    buffers = [rights1.at[i // 2, i % 2] for i in range(4)]
+    staged = [None]
+
+    def left_block(i):
+        return (cots if i < 2 else mids).at[i % 2]
+
+    def left_copies():
+        return [
+            pltpu.make_async_copy(
+                norm_ref.at[chunk_rows(i), pl.ds(j * part, part)], left_block(i).at[j],
+                left_sem.at[i, j],
+            )
+            for i in range(chunks)
+            for j in range(mp)
+        ]
+
+    def right_copies(k):
+        return [
+            pltpu.make_async_copy(
+                pulled_ref.at[chunk_rows(i), pl.ds(k * part, part)], parts1.at[k % 2, i],
+                right_sem.at[k % 2, i],
+            )
+            for i in range(chunks)
+        ]
+
+    def make_scatter(k):
+        def compute(owner, target, add):
+            j = lax.div(owner, 2)
+            near = pl.ds(pl.multiple_of(lax.rem(owner, 2) * own, own), own)
+            value = sum(
+                inner_rows(left_block(i)[j, :, near], parts1[k % 2, i]) for i in range(chunks)
+            )
+            if add:
+                value = value + target[...].astype(F32)
+            target[...] = value.astype(BF16)
+
+        cols = pl.ds(k * part, part)
+
+        def place(first):
+            return w_up.at[pl.ds(first, own), cols]
+
+        def held(i):
+            return w_up.at[pl.ds(pl.multiple_of(i * own, own), own), cols]
+
+        return Scatter(
+            d, own, compute, held, place(4 * own), place(5 * own), place(6 * own),
+            task_sent.at[k], task_came.at[k],
+        )
+
+    def weight_first(k):
+        if not square:
+            return
+        if k == 0:
+            store(norm, norm_ref, chunks - 1, 0).wait()
+            store(pulled, pulled_ref, chunks - 1, 2).wait()
+            for slot in range(2):
+                rs1.drain(slot)
+            for c in range(2):
+                ag3.drain(c)
+            scatters.extend(make_scatter(i) for i in range(count_tasks))
+            for copy in right_copies(0) + left_copies():
+                copy.start()
+            for i in range(3):
+                pl.semaphore_wait(free_sem.at[i], 1)
+        if k + 1 < count_tasks:
+            for copy in right_copies(k + 1):
+                copy.start()
+        for copy in right_copies(k) + (left_copies() if k == 0 else []):
+            copy.wait()
+        scatters[k].far_core(buffers, sending)
+        scatters[k].near_core()
+
+    def weight_second(k):
+        if square:
+            scatters[k].onward()
+
+    def weight_third(k):
+        if not square:
+            return
+        if staged[0] is not None:
+            staged[0].wait()
+        scatters[k].finish(stage)
+        half = count_tasks // 2
+        target = grad_gate_ref if k < half else grad_up_ref
+        staged[0] = pltpu.make_async_copy(
+            stage, target.at[:, pl.ds((k % half) * part, part)], stage_sem
+        )
+        staged[0].start()
+
+    steps = {
+        "A": branch, "J": join, "H": mlp_first, "G": mlp_second, "O": mlp_third,
+        "K": gather_grad, "B": norm_back, "Y": make_output, "D": weight_first,
+        "W": weight_second, "Z": weight_third,
+    }
+    moves = {"a": (rs1, 2), "b": (rs2, 2), "c": (rs3, 2), "d": (ag2, 0), "e": (ag3, 0), "f": (ag4, 0)}
+    for name, s, c in MIDDLE_ORDER:
+        if name == "S":
+            if square and s < 3:
+                squares[s - 1].step_one()
+            if square and s == 3:
                 squares[0].step_two()
                 squares[1].step_two()
-                for item in squares:
-                    item.finish()
-            else:
-                for item in loads:
-                    item.wait()
-        if has(r - 2):
-            mlp_first(r - 2)
-        for s in range(1, mp - 1):
-            if has(r):
-                rs1.step(r % 2, s)
-            if has(r - 1):
-                ag3.step(r - 1, s)
-            if has(r - 3):
-                ag4.step((r - 3) % 2, s)
-            if has(r):
-                ag2.step(r, s)
-            if has(r - 3):
-                rs2.step((r - 3) % 2, s)
-            if s == 1 and has(r - 2):
-                mlp_second(r - 2)
-        if has(r):
-            rs1.finish(r % 2)
-            join(r)
-        if has(r - 1):
-            ag3.finish(r - 1)
-        if has(r):
-            ag2.finish(r)
-        if has(r - 2):
-            rs3.step((r - 2) % 2, 1)
-            mlp_third(r - 2)
-        if has(r - 3):
-            ag4.finish((r - 3) % 2)
-            norm_back(r - 3)
-            ag4.drain((r - 3) % 2)
-        if has(r - 2):
-            for s in range(2, mp - 1):
-                rs3.step((r - 2) % 2, s)
-        if has(r - 3):
-            rs2.finish((r - 3) % 2)
-            make_output(r - 3)
-        if has(r - 2):
-            rs3.finish((r - 2) % 2)
+        elif name in steps:
+            steps[name](c)
+        else:
+            line, parity = moves[name]
+            if s == mp - 1:
+                line.finish(c)
+                continue
+            if name == "d" and s == 0:
+                own_cot(c).wait()
+            line.step(c % parity if parity else c, s)
 
     last = chunks - 1
     for k, (buffer, target) in enumerate(
@@ -1226,20 +1431,26 @@
             (local, local_ref), (gm, gm_ref), (out, output_ref),
         )
     ):
-        store(buffer, target, last, k).wait()
+        if not (square and k in (0, 2)):
+            store(buffer, target, last, k).wait()
     for copy in grad_y_copies(last):
         copy.wait()
     for c in range(chunks):
-        ag3.drain(c)
+        if c > 1 or not square:
+            ag3.drain(c)
+        ag4.drain(c)
     for slot in range(2):
-        for fold in folds:
+        for fold in folds[1:] if square else folds:
             fold.drain(slot)
     if square:
-        for item in squares:
-            item.drain()
-
-
-def middle(dp, mp, chunks, mixed, inputs, cotangent, live, gains, mine, w_out, up, down):
+        staged[0].wait()
+        for copy in sending:
+            copy.wait_send()
+        for scatter in scatters:
+            scatter.drain()
+
+
+def middle(dp, mp, chunks, mixed, inputs, cotangent, live, gains, mine, w_out, gate, up, down):
     count, part = inputs.shape
     width, hidden_width = mixed.shape[1], down.shape[1]
     step, features = count // chunks, part * mp
@@ -1255,8 +1466,8 @@
     any_, vmem = pl.BlockSpec(memory_space=pl.ANY), pl.BlockSpec(memory_space=pltpu.VMEM)
     return pl.pallas_call(
         functools.partial(middle_kernel, dp, mp, chunks),
-        in_specs=[vmem, vmem, any_, vmem, vmem, vmem, vmem, any_, any_],
-        out_specs=[any_] * 8 + [vmem],
+        in_specs=[vmem, vmem, any_, vmem, vmem, vmem, vmem, any_, any_, any_],
+        out_specs=[any_] * 10 + [vmem],
         out_shape=(
             jax.ShapeDtypeStruct((count, part), BF16),
             jax.ShapeDtypeStruct((count, width), F32),
@@ -1266,6 +1477,8 @@
             jax.ShapeDtypeStruct((count, 2 * hidden_width), BF16),
             jax.ShapeDtypeStruct((count, features), BF16),
             jax.ShapeDtypeStruct((count, features), BF16),
+            jax.ShapeDtypeStruct((features // 8, hidden_width), F32),
+            jax.ShapeDtypeStruct((features // 8, hidden_width), F32),
             jax.ShapeDtypeStruct((8, features), F32),
         ),
         scratch_shapes=[
@@ -1273,7 +1486,7 @@
             pltpu.VMEM((features, hidden_width), BF16),
             pltpu.VMEM((chunks, mp, step, part), BF16),
             pltpu.VMEM((chunks, mp, step, part), BF16),
-            pltpu.VMEM((2, mp, step, part), BF16),
+            pltpu.VMEM((chunks, mp, step, part), BF16),
             pltpu.VMEM((chunks, step, part), F32),
             pltpu.VMEM((2, step, part), F32),
         ]
@@ -1293,97 +1506,27 @@
             dma((3, 2, mp)),
             dma((2, 8)),
             dma((2, 8)),
-            dma((2,)),
+            dma((3,)),
             dma((chunks,)),
             dma((12,)),
+            pltpu.VMEM((features // 8, part), F32),
+            pltpu.SemaphoreType.REGULAR((3,)),
+            dma((2 * hidden_width // part, 8)),
+            dma((2 * hidden_width // part, 8)),
+            dma((chunks, mp)),
+            dma((2, chunks)),
+            dma,
         ],
         compiler_params=pltpu.CompilerParams(
             collective_id=0, has_side_effects=True, vmem_limit_bytes=62 * 1024 * 1024
         ),
         name="middle",
-    )(mixed, inputs, cotangent, live, gains, mine, w_out, up, down)
-
-
-class Scatter:
-    def __init__(self, d, count, compute, held, far, first, second, sent, came):
-        self.d, self.count, self.compute = d, count, compute
-        self.held, self.far_in, self.first_in, self.second_in = held, far, first, second
-        self.sent, self.came = sent, came
-        self.core, self.by_core, by_x, by_y = partners(d)
-        even = self.core == 0
-        self.first = jnp.where(even, by_y, by_x)
-        self.second = jnp.where(even, by_x, by_y)
-        self.first_at, self.second_at = 2 - self.core, 1 + self.core
-        other = partners(self.by_core)
-        self.away = (self.by_core, other[2], other[3], partners(other[2])[3])
-        self.distant = partners(by_x)[3]
-
-    def copy(self, src, dst, target, sent, came):
-        return pltpu.make_async_remote_copy(
-            src_ref=src, dst_ref=dst, send_sem=self.sent.at[sent], recv_sem=self.came.at[came],
-            device_id={"dp": target}, device_id_type=MESH,
-        )
-
-    def to_core(self, buffer, k):
-        return self.copy(buffer, self.held.at[k], self.by_core, k, k)
-
-    def to_far(self):
-        return self.copy(self.held.at[3], self.far_in, self.first, 4, 4)
-
-    def to_first(self):
-        return self.copy(self.held.at[self.first_at], self.first_in, self.first, 5, 5)
-
-    def to_second(self):
-        return self.copy(self.held.at[self.second_at], self.second_in, self.second, 6, 6)
-
-    def add_block(self, k, owner):
-        self.copy(self.held.at[k], self.held.at[k], self.by_core, k, k).wait_recv()
-        self.compute(owner, self.held.at[k], True)
-
-    def near_core(self):
-        self.add_block(3, self.distant)
-        self.to_far().start()
-        self.add_block(self.first_at, self.first)
-        self.to_first().start()
-        self.add_block(0, self.d)
-        self.add_block(self.second_at, self.second)
-
-    def onward(self):
-        self.to_far().wait_recv()
-        at = self.second_at
-
-        def body(t):
-            rows = rows_at(t, 16)
-            self.held[at, rows, :] = (
-                self.held[at, rows, :].astype(F32) + self.far_in[rows, :].astype(F32)
-            ).astype(BF16)
-
-        tile_loop(self.count // 16, body)
-        self.to_second().start()
-
-    def finish(self, target):
-        self.to_first().wait_recv()
-        self.to_second().wait_recv()
-
-        def body(t):
-            rows = rows_at(t, 16)
-            target[rows, :] = (
-                self.held[0, rows, :].astype(F32)
-                + self.first_in[rows, :].astype(F32)
-                + self.second_in[rows, :].astype(F32)
-            )
-
-        tile_loop(self.count // 16, body)
-
-    def drain(self):
-        self.to_far().wait_send()
-        self.to_first().wait_send()
-        self.to_second().wait_send()
-
-
-def tail_kernel(mp, tasks, names, *refs):
+    )(mixed, inputs, cotangent, live, gains, mine, w_out, gate, up, down)
+
+
+def tail_kernel(mp, tasks, loaded, names, *refs):
     ref = dict(zip(names, refs))
-    pull, w_in, norm1 = ref["pull"], ref["w_in"], ref["norm1"]
+    pull, w_in, norm1 = ref["pull"], ref["w_in"], ref["norm1_here"]
     count, part = ref["x"].shape
     features = part * mp
     halves = ref["parts"].shape[0]
@@ -1414,41 +1557,20 @@
         pl.semaphore_signal(barrier, inc=1, device_id={"dp": other}, device_id_type=MESH)
     pl.semaphore_wait(barrier, jnp.where((z > 0) & (z < mp - 1), 6, 5))
 
-    rhs, lhs, sends = ref["rhs"], ref["lhs"], ref["sends"]
-    load_sem, lhs_sem, store_sem = ref["load_sem"], ref["lhs_sem"], ref["store_sem"]
-    loaded = [k for k, t in enumerate(tasks) if t[2] not in ("pull", "gates")]
-
-    def load(k):
-        _, _, right, first, width, _ = tasks[k]
-        slot = loaded.index(k) % 2
-        return pltpu.make_async_copy(
-            ref[right].at[:, pl.ds(first, width)], rhs.at[slot, :, pl.ds(0, width)],
-            load_sem.at[slot],
-        )
-
-    load(loaded[0]).start()
-    load(loaded[1]).start()
-
-    other = partners(by_core)
-    far_here, far_there = partners(by_x)[3], partners(other[2])[3]
-    first_dev = jnp.where(core == 0, by_y, by_x)
-    second_dev = jnp.where(core == 0, by_x, by_y)
-    order = (
-        far_there, other[2], other[3], by_core, far_here, first_dev, d, second_dev,
-    )
-    plan = [
-        (k, owner) for k, t in enumerate(tasks) if t[1] not in (None, "norm1") for owner in order
-    ]
-    turn = [0]
-
-    def lhs_copy(index):
-        k, owner = plan[index]
-        cols = pl.ds(pl.multiple_of(owner * own, own), own)
-        return pltpu.make_async_copy(
-            ref[tasks[k][1]].at[:, cols], lhs.at[index % 2], lhs_sem.at[index % 2]
-        )
-
-    lhs_copy(0).start()
+    sends, store_sem = ref["sends"], ref["store_sem"]
+    loads = {
+        name: pltpu.make_async_copy(ref[name], ref[name + "_here"], ref["load_sem"].at[k])
+        for k, name in enumerate(loaded)
+    }
+    for copy in loads.values():
+        copy.start()
+
+    def ready(name):
+        if name in loads:
+            loads.pop(name).wait()
+
+    def operand(name):
+        return ref[name + "_here"] if name in loaded else ref[name]
 
     def build(k):
         _, left, right, first, width, _ = tasks[k]
@@ -1458,45 +1580,28 @@
                 rows = pl.ds(pl.multiple_of(owner * 32, 32), 32)
                 value = ref["gates"][rows, first : first + width].astype(F32)
             else:
-                if left == "norm1":
-                    source = norm1.at[:, pl.ds(pl.multiple_of(owner * own, own), own)]
-                else:
-                    index = turn[0]
-                    turn[0] += 1
-                    if index + 1 < len(plan):
-                        lhs_copy(index + 1).start()
-                    lhs_copy(index).wait()
-                    source = lhs.at[index % 2]
-                if right == "pull":
-                    operand = pull[:, first : first + width]
-                else:
-                    operand = rhs[loaded.index(k) % 2, :, 0:width]
-                value = inner_rows(source[...], operand)
+                cols = pl.ds(pl.multiple_of(owner * own, own), own)
+                value = inner_rows(
+                    operand(left)[:, cols], operand(right)[:, first : first + width]
+                )
             if add:
                 value = value + target[...].astype(F32)
             target[...] = value.astype(BF16)
 
         return Scatter(
-            d, 32 if left is None else own, compute, ref["held%d" % k], ref["far%d" % k],
-            ref["first%d" % k], ref["second%d" % k], ref["task_sent"].at[k],
+            d, 32 if left is None else own, compute, ref["held%d" % k].at.__getitem__,
+            ref["far%d" % k], ref["first%d" % k], ref["second%d" % k], ref["task_sent"].at[k],
             ref["task_came"].at[k],
         )
 
     scatters = [build(k) for k in range(len(tasks))]
-    sending = [None, None]
+    sending = [None] * 4
 
     def far_core(k):
-        scatter = scatters[k]
-        width = tasks[k][4]
-        for i, rel in enumerate((3, 1, 2, 0)):
-            slot = i % 2
-            buffer = sends.at[slot, pl.ds(0, scatter.count), pl.ds(0, width)]
-            if sending[slot] is not None:
-                sending[slot].wait_send()
-            scatter.compute(scatter.away[rel], buffer, False)
-            copy = scatter.to_core(buffer, rel)
-            copy.start()
-            sending[slot] = copy
+        height, width = scatters[k].count, tasks[k][4]
+        scatters[k].far_core(
+            [sends.at[slot, pl.ds(0, height), pl.ds(0, width)] for slot in range(4)], sending
+        )
 
     stage, stage_wait = ref["stage"], [None, None]
 
@@ -1532,6 +1637,7 @@
     dots_copy(0).start()
     gain = ref["gain"]
     gain[...] = jnp.zeros_like(gain)
+    ready("norm1")
     for c in range(halves):
 
         def body(j, c=c):
@@ -1570,6 +1676,9 @@
         small_copy(k).wait()
         small[0:rows, :] += small_in[k, 0:rows, :]
 
+    ready("x")
+    ready("s1")
+
     def local_copy(c):
         return pltpu.make_async_copy(
             ref["local"].at[pl.ds(c * step, step), :], ref["near_local"], ref["local_sem"]
@@ -1584,12 +1693,12 @@
         def body(t):
             rows = rows_at(t, TILE)
             base = pl.ds(pl.multiple_of(c * step + t * TILE, TILE), TILE)
-            s1 = ref["s1"][base, :][:, 0:1]
+            s1 = ref["s1_here"][base, :][:, 0:1]
             dot = ref["dots_col"][base, :][:, 0:1]
             grad = (
                 ref["near_local"][rows, :]
                 + s1 * (fold.total(c, rows) * ref["mine"][0:1, :])
-                - ref["x"][base, :].astype(F32) * (s1 * s1 * dot * (1.0 / features))
+                - ref["x_here"][base, :].astype(F32) * (s1 * s1 * dot * (1.0 / features))
             )
             ref["grad_x"][base, :] = grad.astype(BF16)
 
@@ -1605,8 +1714,8 @@
     small_copy(0).start()
     last = len(tasks) - 1
     for k in range(len(tasks)):
-        if k in loaded:
-            load(k).wait()
+        for name in tasks[k][1:3]:
+            ready(name)
         far_core(k)
         if k == 0:
             for i in range(3):
@@ -1614,33 +1723,28 @@
                 if i < 2:
                     small_copy(i + 1).start()
         scatters[k].near_core()
-        if k in loaded and loaded.index(k) + 2 < len(loaded):
-            load(loaded[loaded.index(k) + 2]).start()
         if k == 0:
             dots_add(1)
             dots_back()
+            fold.step(0, 1)
         if k == 1:
-            fold.step(0, 1)
-        if k == 2:
             fold.step(0, 2)
         if k == 3:
             input_grad(0)
+        if k > 0:
+            scatters[k - 1].onward()
         if k == 4:
             fold.step(1, 1)
-        if k == 6:
-            fold.step(1, 2)
-        if k == 8:
-            input_grad(1)
-            small_copy(3).start()
-        if k > 0:
-            scatters[k - 1].onward()
-        if k > 5:
-            finish(k - 6)
+            finish(0)
     scatters[last].onward()
+    finish(1)
+    fold.step(1, 2)
+    small_copy(3).start()
+    for k in range(2, last + 1):
+        finish(k)
     small_add(3)
     small_copy(4).start()
-    for k in range(last - 5, last + 1):
-        finish(k)
+    input_grad(1)
     small_add(4)
     for copy in stage_wait:
         copy.wait()
@@ -1652,20 +1756,19 @@
         fold.drain(c)
 
 
-def tail(mp, pull, w_in, norm1, norm2, pulled, grady, hidden, gbo, mixed, gates, dots, s1, x,
-         local, gains, mine, small):
+def tail(mp, pull, w_in, norm1, grady, hidden, gbo, mixed, gates, dots, s1, x, local, gains, mine,
+         small):
     count, part = x.shape
     features = part * mp
     own = features // 8
     halves = 2
     step = count // halves
     widths = {
-        "gate": hidden.shape[1], "up": hidden.shape[1], "down": hidden.shape[1],
-        "in": pull.shape[1], "out": mixed.shape[1], "block": pull.shape[1],
+        "down": hidden.shape[1], "in": pull.shape[1], "out": mixed.shape[1],
+        "block": pull.shape[1],
     }
     heights = {name: 32 if name == "block" else own for name in widths}
     operands = {
-        "gate": ("norm2", "pulled", 0), "up": ("norm2", "pulled", hidden.shape[1]),
         "down": ("grady", "hidden", 0), "in": ("norm1", "pull", 0), "out": ("gbo", "mixed", 0),
         "block": (None, "gates", 0),
     }
@@ -1680,10 +1783,10 @@
     dma = pltpu.SemaphoreType.DMA
     any_, vmem = pl.BlockSpec(memory_space=pl.ANY), pl.BlockSpec(memory_space=pltpu.VMEM)
     ins = [
-        ("pull", pull, vmem), ("w_in", w_in, vmem), ("norm1", norm1, vmem),
-        ("norm2", norm2, any_), ("pulled", pulled, any_), ("grady", grady, any_),
+        ("pull", pull, vmem), ("w_in", w_in, vmem), ("norm1", norm1, any_),
+        ("grady", grady, any_),
         ("hidden", hidden, any_), ("gbo", gbo, any_), ("mixed", mixed, any_),
-        ("gates", gates, vmem), ("dots", dots, vmem), ("s1", s1, vmem), ("x", x, vmem),
+        ("gates", gates, vmem), ("dots", dots, vmem), ("s1", s1, any_), ("x", x, any_),
         ("local", local, any_), ("gains", gains, vmem), ("mine", mine, vmem),
         ("small_start", small, vmem),
     ]
@@ -1695,9 +1798,7 @@
         ("parts", pltpu.VMEM((halves, mp, step, part), BF16)),
         ("rights", pltpu.VMEM((halves, mp - 1, step, part), BF16)),
         ("lefts", pltpu.VMEM((halves, mp - 1, step, part), BF16)),
-        ("rhs", pltpu.VMEM((2, count, widest), BF16)),
-        ("lhs", pltpu.VMEM((2, count, own), BF16)),
-        ("sends", pltpu.VMEM((2, own, widest), BF16)),
+        ("sends", pltpu.VMEM((4, own, widest), BF16)),
         ("stage", pltpu.VMEM((2, own, widest), F32)),
         ("near_local", pltpu.VMEM((step, part), F32)),
         ("local_sem", dma),
@@ -1711,14 +1812,17 @@
         ("fold_left", dma((halves, mp))),
         ("task_sent", dma((len(tasks), 8))),
         ("task_came", dma((len(tasks), 8))),
-        ("load_sem", dma((2,))),
-        ("lhs_sem", dma((2,))),
+        ("load_sem", dma((8,))),
         ("store_sem", dma((2,))),
         ("dots_sent", dma((2,))),
         ("dots_came", dma((2,))),
         ("small_sent", dma((5,))),
         ("small_came", dma((5,))),
     ]
+    loaded = ("norm1", "grady", "hidden", "x", "s1", "gbo", "mixed")
+    for name, value, _ in ins:
+        if name in loaded:
+            scratch.append((name + "_here", pltpu.VMEM(value.shape, value.dtype)))
     for k, (name, _, _, _, width, _) in enumerate(tasks):
         tall = heights[name]
         scratch.append(("held%d" % k, pltpu.VMEM((4, tall, width), BF16)))
@@ -1726,7 +1830,7 @@
             scratch.append(("%s%d" % (kind, k), pltpu.VMEM((tall, width), BF16)))
     names = [i[0] for i in ins] + [o[0] for o in outs] + [k[0] for k in scratch]
     return pl.pallas_call(
-        functools.partial(tail_kernel, mp, tuple(tasks), tuple(names)),
+        functools.partial(tail_kernel, mp, tuple(tasks), loaded, tuple(names)),
         in_specs=[i[2] for i in ins],
         out_specs=[o[2] for o in outs],
         out_shape=[o[1] for o in outs],
@@ -1790,13 +1894,12 @@
     in_shard = jnp.concatenate([rnn_in, branch_gate], axis=1)
     out_shard = rnn_out.T
     gates_shard = jnp.concatenate([recur_gate, input_gate], axis=1)
-    up = jnp.concatenate([mlp_gate, mlp_up], axis=1)
-    down = mlp_down.T
+    gate, up, down = mlp_gate, mlp_up, mlp_down.T
     if dp == 8:
         gates_shard = jnp.pad(gates_shard, ((0, 32 - span // 8), (0, 0)))
     else:
         in_shard, out_shard = square_gather(in_shard, "dp", dp), square_gather(out_shard, "dp", dp)
-        up, down = square_gather(up, "dp", dp), square_gather(down, "dp", dp)
+        gate, up, down = [square_gather(w, "dp", dp) for w in (gate, up, down)]
         gates_shard = pair_gather(gates_shard, "dp", dp).reshape(8, span // 8, 2 * width)
         gates_shard = jnp.pad(gates_shard, ((0, 0), (0, 32 - span // 8), (0, 0)))
         gates_shard = gates_shard.reshape(256, 2 * width)
@@ -1805,12 +1908,14 @@
     mask_tail = jnp.concatenate([mask, jnp.zeros((8, LANES), F32)], axis=0)
     tail_masks = [mask_tail[c * step : (c + 1) * step + 8] for c in range(CHUNKS)]
     live = jnp.broadcast_to(live[:, None], (count, LANES)).astype(F32)
-    w_in, w_out, dense, normed, both, conv, r, i, state, mixed, s1 = head(
-        dp, mp, 4, inputs, gains, rnn_params, mask, in_shard, out_shard, gates_shard, span
+    w_in, w_out, w_gate, dense, normed, both, conv, r, i, state, mixed, s1 = head(
+        dp, mp, 4, inputs, gains, rnn_params, mask, in_shard, out_shard, gate, gates_shard, span
     )
-    output, gm, gbo, local, hidden, pulled, normed2, grad_y, gain2 = middle(
+    (
+        output, gm, gbo, local, hidden, pulled, normed2, grad_y, grad_gate, grad_up, gain2,
+    ) = middle(
         dp, mp, 4, mixed, inputs, cotangent, live, gains, mine(gains), w_out,
-        up, down,
+        w_gate, up, down,
     )
     blank = jnp.zeros((8, width), F32)
     back, tail_rows = blank, blank
@@ -1844,8 +1949,8 @@
                 jnp.pad(params_total, ((0, 0), (0, features - width))),
             ]
         )
-        input_grad, grad_gate, grad_up, grad_down, grad_in, grad_out, grad_gates, small = tail(
-            mp, pull, w_in, normed, normed2, pulled, grad_y, hidden, gbo, mixed, padded, dots,
+        input_grad, grad_down, grad_in, grad_out, grad_gates, small = tail(
+            mp, pull, w_in, normed, grad_y, hidden, gbo, mixed, padded, dots,
             s1, inputs, local, gains, mine(gains), small,
         )
         grad_gates = grad_gates[:rows]

time: 683 us -> 608 us (0.89)
  Pallas kernels: 639 us -> 566 us
    pallas_call x1, Pallas kernels: 147 us -> 105 us  [tail(): pl.pallas_call(functools.partial(tail_kernel, mp, tuple(tasks), loaded, t...]
    pallas_call x1, Pallas kernels: 357 us -> 324 us  [middle(): pl.pallas_call(functools.partial(middle_kernel, dp, mp, chunks), in_specs...]
where the time goes in v4:
time: 608 us; the launch traced here: 598 us
  Pallas kernels  566 us (93%)
  local copies, waits for them, and re-layouts  22 us (4%)
    pallas_call x1, Pallas kernels, middle(): pl.pallas_call(functools.partial(middle_kernel, dp, mp, chunks), in_specs...  324 us
    pallas_call x1, Pallas kernels, tail(): pl.pallas_call(functools.partial(tail_kernel, mp, tuple(tasks), loaded, t...  105 us
    pallas_call x1, Pallas kernels, head(): pl.pallas_call(functools.partial(head_kernel, dp, mp, tuple(names)), in_s...  97.6 us
    pallas_call x1, Pallas kernels, rnn_backward(): pl.pallas_call(rnn_backward_kernel, out_shape=(jax.ShapeDtypeStruct((coun...  39.4 us

profile of v4, /device:TPU:0, one launch (start us, length us, event | category | flops | bytes accessed | tf_op | source)
XLA Modules:
  0.0 598.2 jit_solution(4893709328614993646)
XLA Ops:
  0.7 0.8 reduce-window.8
  1.7 1.0 copy.44.refs_3_
  2.7 2.0 pad_maximum_fusion.refs_4_
  4.7 1.9 copy.43
  7.3 97.6 %head.1 = (bf16[2048,1280]{1,0:T(8,128)(2,1)}, bf16[2048,640]{1,0:T(8,128)(2,1)}, bf16[2048,1536]{1,0:T(8,128)(2,1)}, bf16[640,1280]{1,0:T(8,128)(2,1)}, bf16[10...) custom-call(bf16[1024,512]{1,0:T(8,128)(2,1)} %refs_10_.1, ...), custom_call_target="tpu_custom_call" | custom-call | tf_op jit(solution)/shard_map/head/pallas_call | solution.py:1013
  104.9 1.3 constant_dynamic-slice_fusion.refs_5_.refs_13_
  106.2 1.0 broadcast_in_dim.54.refs_3_
  107.2 1.2 copy.45
  108.3 323.8 %middle.1 = (bf16[1024,512]{1,0:T(8,128)(2,1)}, f32[1024,640]{1,0:T(8,128)}, bf16[1024,2048]{1,0:T(8,128)(2,1)}, f32[1024,512]{1,0:T(8,128)}, bf16[1024,1536]{1,...) custom-call(bf16[1024,640]{1,0:T(8,128)(2,1)} %get-tuple-element.43., ...), custom_call_target="tpu_custom_call" | custom-call | tf_op jit(solution)/shard_map/middle/pallas_call | solution.py:1467
  432.1 0.8 concatenate.14.mask_ref
  433.5 39.4 %rnn_backward.1 = (bf16[1024,1280]{1,0:T(8,128)(2,1)}, bf16[1024,1280]{1,0:T(8,128)(2,1)}, f32[8,640]{1,0:T(8,128)}, f32[8,640]{1,0:T(8,128)}, f32[8,640]{1,0:T(8,128)}, /*index=5*/f32[1024,128]{1,0:T(8,128)}) custom-call(f32[1024,640]{1,0:T(8,128)} %get-tuple-element.47.gm_ref, f32[1024,1280]{1,0:T(8,128)} %get-tuple-element.48.both_ref, ...), custom_call_target="tpu_custom_call" | custom-call | flops 1677721600 | bytes 23592960 | tf_op jit(solution)/shard_map/rnn_backward/pallas_call | solution.py:440
  473.0 1.5 select_maximum_fusion.refs_14_
  474.5 3.7 fusion
  478.6 0.9 pad.14
  479.5 105.4 %tail.1 = (bf16[1024,512]{1,0:T(8,128)(2,1)}, f32[256,1536]{1,0:T(8,128)}, f32[256,1280]{1,0:T(8,128)}, f32[256,640]{1,0:T(8,128)}, f32[32,1280]{1,0:T(8,128)}, /*index=5*/f32[16,2048]{1,0:T(8,128)}) custom-call(bf16[1024,1280]{1,0:T(8,128)(2,1)} %get-tuple-element.54.refs_0_, bf16[2048,1280]{1,0:T(8,128)(2,1)} %get-tuple-element.55.refs_1_, ...), custom_call_target="tpu_custom_call" | custom-call | tf_op jit(solution)/shard_map/tail/pallas_call | solution.py:1832
  584.9 3.2 copy.48
  588.1 1.1 fusion.16
  589.2 1.1 copy.47
  591.0 1.3 slice.54
  592.3 1.4 slice.53
  593.7 1.0 copy.53
  594.7 1.0 copy.54
  595.7 1.1 copy.55
  596.8 1.1 copy.56
  (44 shorter events, 2.6 us)
Async XLA Ops:
  0.6 6.0 %copy-start.12 = (bf16[20,640]{1,0:T(8,128)(2,1)S(1)}, bf16[20,640]{1,0:T(8,128)(2,1)}, u32[]{:S(2)}) copy-start(bf16[20,640]{1,0:T(8,128)(2,1)} %param.20) | copy-start | bytes 76804
  0.7 6.0 %copy-start.11 = (bf16[20,640]{1,0:T(8,128)(2,1)S(1)}, bf16[20,640]{1,0:T(8,128)(2,1)}, u32[]{:S(2)}) copy-start(bf16[20,640]{1,0:T(8,128)(2,1)} %param.21) | copy-start | bytes 76804
  4.7 102.5 %copy-start.7 = (bf16[1536,256]{1,0:T(8,128)(2,1)S(1)}, bf16[1536,256]{1,0:T(8,128)(2,1)}, u32[]{:S(2)}) copy-start(bf16[1536,256]{1,0:T(8,128)(2,1)} %param.25) | copy-start | bytes 2359300
  108.3 323.8 %copy-start.1 = (f32[1024,8]{1,0:T(8,128)S(1)}, f32[1024,8]{1,0:T(8,128)}, u32[]{:S(2)}) copy-start(f32[1024,8]{1,0:T(8,128)} %copy.44.refs_3_) | copy-start | bytes 98308
  433.5 39.4 %copy-start.10 = (f32[8,2048]{1,0:T(8,128)S(1)}, f32[8,2048]{1,0:T(8,128)}, u32[]{:S(2)}) copy-start(f32[8,2048]{1,0:T(8,128)} %get-tuple-element.64) | copy-start | bytes 196612
  433.5 41.0 %copy-start = (f32[1024,640]{1,0:T(8,128)S(1)}, f32[1024,640]{1,0:T(8,128)}, u32[]{:S(2)}) copy-start(f32[1024,640]{1,0:T(8,128)} %get-tuple-element.49.conv_ref) | copy-start | bytes 7864324
  584.9 3.2 copy-start.4
  584.9 4.3 copy-start.8
  588.1 2.2 copy-start.9
  588.1 5.7 copy-start.5
  589.2 6.5 %copy-start.3 = (f32[256,1536]{1,0:T(8,128)S(1)}, f32[256,1536]{1,0:T(8,128)}, u32[]{:S(2)}) copy-start(f32[256,1536]{1,0:T(8,128)} %get-tuple-element.154) | copy-start | bytes 4718596
  590.3 4.4 copy-start.6
  594.7 2.1 copy-start.2

commit v5 on v4

--- a/solution.py
+++ b/solution.py
@@ -1524,24 +1524,81 @@
     )(mixed, inputs, cotangent, live, gains, mine, w_out, gate, up, down)
 
 
-def tail_kernel(mp, tasks, loaded, names, *refs):
+def tail_kernel(mp, tasks, names, *refs):
     ref = dict(zip(names, refs))
-    pull, w_in, norm1 = ref["pull"], ref["w_in"], ref["norm1_here"]
-    count, part = ref["x"].shape
-    features = part * mp
-    halves = ref["parts"].shape[0]
-    step = count // halves
-    own = features // 8
+    pull, w_in, params = ref["pull"], ref["w_in_here"], ref["params"]
+    chunks, _, step, part = ref["parts"].shape
+    count, features = chunks * step, part * mp
+    own, width = features // 8, params.shape[1]
     z, d = lax.axis_index("mp"), lax.axis_index("dp")
-    core, by_core, by_x, by_y = partners(d)
+    _, by_core, by_x, by_y = partners(d)
     fold = Fold(
         z, mp, ref["parts"], ref["rights"], ref["lefts"], ref["fold_sent"], ref["fold_right"],
         ref["fold_left"],
     )
-    fold.clear()
     near = z + 1 - 2 * lax.rem(z, 2)
     apart = z + 2 - 4 * lax.div(z, 2)
 
+    def chunk_rows(c):
+        return pl.ds(c * step, step)
+
+    def recurrence_copies(c):
+        copies = [
+            pltpu.make_async_copy(
+                ref[name].at[chunk_rows(c), :], ref[name + "_here"], ref["chunk_sem"].at[k]
+            )
+            for k, name in enumerate(("gm", "both", "conv", "r", "i", "state"))
+        ]
+        if c > 0:
+            rows = pl.ds(c * step - 8, 8)
+            copies += [
+                pltpu.make_async_copy(
+                    ref["both"].at[rows, pl.ds(0, width)], ref["halo"], ref["chunk_sem"].at[6]
+                ),
+                pltpu.make_async_copy(
+                    ref["state"].at[rows, :], ref["start"], ref["chunk_sem"].at[7]
+                ),
+            ]
+        return copies
+
+    def norm_copy(c):
+        return pltpu.make_async_copy(
+            ref["norm1"].at[chunk_rows(c), :], ref["norm_here"], ref["norm_sem"]
+        )
+
+    def left_copy(name):
+        return pltpu.make_async_copy(ref[name], ref["lhs"], ref["left_sem"])
+
+    def right_copy(name, first, columns, slot):
+        return pltpu.make_async_copy(
+            ref[name].at[:, pl.ds(first, columns)], ref["rhs"].at[slot, :, pl.ds(0, columns)],
+            ref["right_sem"].at[slot],
+        )
+
+    def end_copies(c):
+        return [
+            pltpu.make_async_copy(
+                ref[name].at[chunk_rows(c), :], ref[name + "_here"], ref["end_sem"].at[k]
+            )
+            for k, name in enumerate(("local", "x", "s1"))
+        ]
+
+    whole_copies = [
+        pltpu.make_async_copy(ref[name], ref[name + "_here"], ref["whole_sem"].at[k])
+        for k, name in enumerate(("dense", "w_in"))
+    ]
+    last = chunks - 1
+    for copy in recurrence_copies(last) + whole_copies:
+        copy.start()
+    norm_copy(last).start()
+    left_copy("grady").start()
+    first_rights = [
+        right_copy(t[2], t[3], t[4], k) for k, t in enumerate(tasks[:2])
+    ]
+    for copy in first_rights + end_copies(last):
+        copy.start()
+
+    fold.clear()
     barrier = pltpu.get_barrier_semaphore()
 
     @pl.when(z > 0)
@@ -1555,35 +1612,114 @@
     pl.semaphore_signal(barrier, inc=1, device_id={"mp": apart}, device_id_type=MESH)
     for other in (by_core, by_x, by_y):
         pl.semaphore_signal(barrier, inc=1, device_id={"dp": other}, device_id_type=MESH)
-    pl.semaphore_wait(barrier, jnp.where((z > 0) & (z < mp - 1), 6, 5))
+
+    for name in ("back", "after", "gain", "dense_sum", "params_sum"):
+        ref[name][...] = jnp.zeros_like(ref[name])
+    gain = ref["gain"]
+
+    def recur(c):
+        for copy in recurrence_copies(c):
+            copy.wait()
+        if c == 0:
+            ref["halo"][...] = jnp.zeros_like(ref["halo"])
+            ref["start"][...] = jnp.zeros_like(ref["start"])
+        if c == last:
+            for copy in whole_copies:
+                copy.wait()
+        rnn_backward_kernel(
+            ref["gm_here"], ref["both_here"], ref["halo"], ref["start"], ref["conv_here"],
+            ref["r_here"], ref["i_here"], ref["state_here"],
+            ref["mask"].at[pl.ds(c * step, step + 8), :], ref["dense_here"], params,
+            ref["back"], ref["after"],
+            pull.at[chunk_rows(c), :], ref["rates"], ref["dparams"], ref["back"], ref["after"],
+            ref["dots"],
+            ref["padded"], ref["before"], ref["decay"], ref["adjoint"], ref["coef"],
+            ref["dconv"], ref["sums"],
+        )
+        ref["params_sum"][...] += ref["dparams"][...]
+        ref["dense_sum"][...] += inner_rows(ref["conv_here"][...].astype(BF16), ref["rates"][...])
+        if c > 0:
+            for copy in recurrence_copies(c - 1):
+                copy.start()
+        for q in range(step // 128):
+            turned = jnp.transpose(ref["dots"][q * 128 : (q + 1) * 128, :])
+            ref["dots_row"][c, :, q * 128 : (q + 1) * 128] = turned[0:8, :]
+        if c == last:
+            pl.semaphore_wait(barrier, jnp.where((z > 0) & (z < mp - 1), 6, 5))
+        dots_copy(c, 0).start()
+        norm_copy(c).wait()
+
+        def body(j):
+            rows = pl.ds(pl.multiple_of(j * part, part), part)
+            value = inner_cols(pull[chunk_rows(c), :], w_in[rows, :])
+            fold.parts[c, j] = value.astype(BF16)
+            gain[:, rows] += jnp.sum(
+                (value * ref["norm_here"][:, rows].astype(F32)).reshape(-1, 8, part), axis=0
+            )
+
+        tile_loop(mp, body)
+        fold.start(c)
+        if c > 0:
+            norm_copy(c - 1).start()
+
+    def dots_copy(c, k):
+        return pltpu.make_async_remote_copy(
+            src_ref=ref["dots_row"].at[c], dst_ref=ref["dots_in"].at[c, k],
+            send_sem=ref["dots_sent"].at[c, k], recv_sem=ref["dots_came"].at[c, k],
+            device_id={"mp": near if k == 0 else apart}, device_id_type=MESH,
+        )
+
+    def dots_add(c, k):
+        dots_copy(c, k).wait()
+        ref["dots_row"][c] += ref["dots_in"][c, k]
+        if k == 0:
+            dots_copy(c, 1).start()
+
+    def input_grad(c):
+        dots_add(c, 1)
+        for q in range(step // 128):
+            row = ref["dots_row"][c, 0:1, q * 128 : (q + 1) * 128]
+            ref["dots_col"][q * 128 : (q + 1) * 128, :] = jnp.transpose(
+                jnp.broadcast_to(row, (128, 128))
+            )
+        fold.finish(c)
+        for copy in end_copies(c):
+            copy.wait()
+
+        def body(t):
+            rows = rows_at(t, TILE)
+            base = pl.ds(pl.multiple_of(c * step + t * TILE, TILE), TILE)
+            s1 = ref["s1_here"][rows, :][:, 0:1]
+            dot = ref["dots_col"][rows, :][:, 0:1]
+            grad = (
+                ref["local_here"][rows, :]
+                + s1 * (fold.total(c, rows) * ref["mine"][0:1, :])
+                - ref["x_here"][rows, :].astype(F32) * (s1 * s1 * dot * (1.0 / features))
+            )
+            ref["grad_x"][base, :] = grad.astype(BF16)
+
+        tile_loop(step // TILE, body)
+        if c > 0:
+            for copy in end_copies(c - 1):
+                copy.start()
 
     sends, store_sem = ref["sends"], ref["store_sem"]
-    loads = {
-        name: pltpu.make_async_copy(ref[name], ref[name + "_here"], ref["load_sem"].at[k])
-        for k, name in enumerate(loaded)
-    }
-    for copy in loads.values():
-        copy.start()
-
-    def ready(name):
-        if name in loads:
-            loads.pop(name).wait()
-
-    def operand(name):
-        return ref[name + "_here"] if name in loaded else ref[name]
+    slots = {k: k % 2 for k, t in enumerate(tasks) if t[2] in ("hidden", "mixed")}
 
     def build(k):
-        _, left, right, first, width, _ = tasks[k]
+        _, left, right, first, columns, _ = tasks[k]
 
         def compute(owner, target, add):
             if left is None:
                 rows = pl.ds(pl.multiple_of(owner * 32, 32), 32)
-                value = ref["gates"][rows, first : first + width].astype(F32)
+                value = ref["gates"][rows, first : first + columns].astype(F32)
             else:
-                cols = pl.ds(pl.multiple_of(owner * own, own), own)
-                value = inner_rows(
-                    operand(left)[:, cols], operand(right)[:, first : first + width]
-                )
+                near = pl.ds(pl.multiple_of(owner * own, own), own)
+                if right == "pull":
+                    operand = pull[:, first : first + columns]
+                else:
+                    operand = ref["rhs"][slots[k], :, 0:columns]
+                value = inner_rows(ref["lhs"][:, near], operand)
             if add:
                 value = value + target[...].astype(F32)
             target[...] = value.astype(BF16)
@@ -1598,67 +1734,27 @@
     sending = [None] * 4
 
     def far_core(k):
-        height, width = scatters[k].count, tasks[k][4]
+        height, columns = scatters[k].count, tasks[k][4]
         scatters[k].far_core(
-            [sends.at[slot, pl.ds(0, height), pl.ds(0, width)] for slot in range(4)], sending
+            [sends.at[slot, pl.ds(0, height), pl.ds(0, columns)] for slot in range(4)], sending
         )
 
     stage, stage_wait = ref["stage"], [None, None]
 
     def finish(k):
         scatter = scatters[k]
-        name, width, column = tasks[k][0], tasks[k][4], tasks[k][5]
+        name, columns, column = tasks[k][0], tasks[k][4], tasks[k][5]
         slot = k % 2
         if stage_wait[slot] is not None:
             stage_wait[slot].wait()
-        view = stage.at[slot, pl.ds(0, scatter.count), pl.ds(0, width)]
+        view = stage.at[slot, pl.ds(0, scatter.count), pl.ds(0, columns)]
         scatter.finish(view)
-        target = ref["grad_" + name].at[:, pl.ds(column, width)]
+        target = ref["grad_" + name].at[:, pl.ds(column, columns)]
         copy = pltpu.make_async_copy(view, target, store_sem.at[slot])
         copy.start()
         stage_wait[slot] = copy
 
-    dots, dots_in = ref["dots_row"], ref["dots_in"]
-    for q in range(count // 128):
-        turned = jnp.transpose(ref["dots"][q * 128 : (q + 1) * 128, :])
-        dots[:, q * 128 : (q + 1) * 128] = turned[0:8, :]
-
-    def dots_copy(k):
-        return pltpu.make_async_remote_copy(
-            src_ref=dots, dst_ref=dots_in.at[k], send_sem=ref["dots_sent"].at[k],
-            recv_sem=ref["dots_came"].at[k], device_id={"mp": near if k == 0 else apart},
-            device_id_type=MESH,
-        )
-
-    def dots_add(k):
-        dots_copy(k).wait()
-        dots[...] += dots_in[k]
-
-    dots_copy(0).start()
-    gain = ref["gain"]
-    gain[...] = jnp.zeros_like(gain)
-    ready("norm1")
-    for c in range(halves):
-
-        def body(j, c=c):
-            rows = pl.ds(pl.multiple_of(j * part, part), part)
-            for q in range(step // 256):
-                tokens = pl.ds(c * step + q * 256, 256)
-                value = inner_cols(pull[tokens, :], w_in[rows, :])
-                fold.parts[c, j, q * 256 : (q + 1) * 256, :] = value.astype(BF16)
-                gain[:, rows] += jnp.sum(
-                    (value * norm1[tokens, rows].astype(F32)).reshape(-1, 8, part), axis=0
-                )
-
-        tile_loop(mp, body)
-        if c == 0:
-            dots_add(0)
-            dots_copy(1).start()
-        fold.start(c)
-
     small, small_in = ref["small"], ref["small_in"]
-    small[...] = ref["small_start"][...]
-    small[0:1, :] = jnp.sum(gain[...], axis=0, keepdims=True) / ref["gains"][0:1, :]
     targets = (
         {"dp": by_core}, {"dp": by_x}, {"dp": by_y}, {"mp": near}, {"mp": apart},
     )
@@ -1671,166 +1767,196 @@
             device_id=targets[k], device_id_type=MESH,
         )
 
-    def small_add(k):
+    def small_first():
+        small[...] = jnp.zeros_like(small)
+        small[0:1, :] = jnp.sum(gain[...], axis=0, keepdims=True) / ref["gains"][0:1, :]
+        small[1:2, :] = ref["gain2"][...] * (1.0 / mp)
+        small[8:16, 0:width] = ref["params_sum"][...]
+        small_copy(0).start()
+
+    def small_next(k):
         rows = 16 if k < 3 else 8
         small_copy(k).wait()
         small[0:rows, :] += small_in[k, 0:rows, :]
-
-    ready("x")
-    ready("s1")
-
-    def local_copy(c):
-        return pltpu.make_async_copy(
-            ref["local"].at[pl.ds(c * step, step), :], ref["near_local"], ref["local_sem"]
-        )
-
-    local_copy(0).start()
-
-    def input_grad(c):
-        fold.finish(c)
-        local_copy(c).wait()
-
-        def body(t):
-            rows = rows_at(t, TILE)
-            base = pl.ds(pl.multiple_of(c * step + t * TILE, TILE), TILE)
-            s1 = ref["s1_here"][base, :][:, 0:1]
-            dot = ref["dots_col"][base, :][:, 0:1]
-            grad = (
-                ref["near_local"][rows, :]
-                + s1 * (fold.total(c, rows) * ref["mine"][0:1, :])
-                - ref["x_here"][base, :].astype(F32) * (s1 * s1 * dot * (1.0 / features))
+        if k < 4:
+            small_copy(k + 1).start()
+
+    def gate_blocks():
+        flat, gates = ref["flat"], ref["gates"]
+        span = flat.shape[0] - 16
+        rows = span // 8
+        column = lax.broadcasted_iota(jnp.int32, (span, 2 * width), 1)
+        column = jnp.where(column >= width, column - width, column)
+        total = jnp.zeros((span, 2 * width), F32)
+        for b in range(width // span):
+            inside = (column >= b * span) & (column < (b + 1) * span)
+            total = total + jnp.where(
+                inside, ref["dense_sum"][b * span : (b + 1) * span, :], 0.0
             )
-            ref["grad_x"][base, :] = grad.astype(BF16)
-
-        tile_loop(step // TILE, body)
-        if c + 1 < halves:
-            local_copy(c + 1).start()
-
-    def dots_back():
-        for q in range(count // 128):
-            wide = jnp.broadcast_to(dots[0:1, q * 128 : (q + 1) * 128], (128, 128))
-            ref["dots_col"][q * 128 : (q + 1) * 128, :] = jnp.transpose(wide)
-
-    small_copy(0).start()
-    last = len(tasks) - 1
-    for k in range(len(tasks)):
-        for name in tasks[k][1:3]:
-            ready(name)
+        flat[0:span, :] = total
+        flat[span:, :] = jnp.zeros((16, 2 * width), F32)
+        for k in range(8):
+            gates[k * 32 : (k + 1) * 32, :] = flat[k * rows : k * rows + 32, :].astype(BF16)
+
+    recur(3)
+    for copy in first_rights:
+        copy.wait()
+    left_copy("grady").wait()
+    far_core(0)
+    scatters[0].near_core()
+    fold.step(3, 1)
+    recur(2)
+    fold.step(3, 2)
+    far_core(1)
+    scatters[1].near_core()
+    left_copy("gbo").start()
+    out_right = right_copy("mixed", 0, tasks[2][4], 0)
+    out_right.start()
+    dots_add(3, 0)
+    scatters[0].onward()
+    fold.step(2, 1)
+    recur(1)
+    dots_add(2, 0)
+    fold.step(2, 2)
+    left_copy("gbo").wait()
+    out_right.wait()
+    far_core(2)
+    scatters[2].near_core()
+    left_copy("norm1").start()
+    scatters[1].onward()
+    fold.step(1, 1)
+    input_grad(3)
+    recur(0)
+    small_first()
+    gate_blocks()
+    dots_add(1, 0)
+    fold.step(1, 2)
+    small_next(0)
+    left_copy("norm1").wait()
+    far_core(3)
+    small_next(1)
+    scatters[3].near_core()
+    scatters[2].onward()
+    small_next(2)
+    fold.step(0, 1)
+    input_grad(2)
+    far_core(4)
+    scatters[4].near_core()
+    scatters[3].onward()
+    dots_add(0, 0)
+    fold.step(0, 2)
+    for k in (5, 6):
         far_core(k)
-        if k == 0:
-            for i in range(3):
-                small_add(i)
-                if i < 2:
-                    small_copy(i + 1).start()
         scatters[k].near_core()
-        if k == 0:
-            dots_add(1)
-            dots_back()
-            fold.step(0, 1)
-        if k == 1:
-            fold.step(0, 2)
-        if k == 3:
-            input_grad(0)
-        if k > 0:
-            scatters[k - 1].onward()
-        if k == 4:
-            fold.step(1, 1)
-            finish(0)
-    scatters[last].onward()
+    scatters[4].onward()
+    finish(0)
     finish(1)
-    fold.step(1, 2)
-    small_copy(3).start()
-    for k in range(2, last + 1):
+    input_grad(1)
+    for k in (5, 6):
+        scatters[k].onward()
+    finish(2)
+    small_next(3)
+    finish(3)
+    input_grad(0)
+    for k in (4, 5, 6):
         finish(k)
-    small_add(3)
-    small_copy(4).start()
-    input_grad(1)
-    small_add(4)
+    small_next(4)
     for copy in stage_wait:
         copy.wait()
     for copy in sending:
         copy.wait_send()
     for scatter in scatters:
         scatter.drain()
-    for c in range(halves):
+    for c in range(chunks):
         fold.drain(c)
 
 
-def tail(mp, pull, w_in, norm1, grady, hidden, gbo, mixed, gates, dots, s1, x, local, gains, mine,
-         small):
+def tail(mp, chunks, span, rnn, mask, params, dense, w_in, norm1, grady, hidden, gbo, mixed, s1, x,
+         local, gains, mine, gain2):
+    gm, both, conv, r, i, state = rnn
     count, part = x.shape
-    features = part * mp
-    own = features // 8
-    halves = 2
-    step = count // halves
+    features, width = part * mp, params.shape[1]
+    own, step = features // 8, count // chunks
     widths = {
-        "down": hidden.shape[1], "in": pull.shape[1], "out": mixed.shape[1],
-        "block": pull.shape[1],
+        "down": hidden.shape[1], "out": width, "in": 2 * width, "block": 2 * width,
     }
     heights = {name: 32 if name == "block" else own for name in widths}
     operands = {
-        "down": ("grady", "hidden", 0), "in": ("norm1", "pull", 0), "out": ("gbo", "mixed", 0),
-        "block": (None, "gates", 0),
+        "down": ("grady", "hidden"), "out": ("gbo", "mixed"), "in": ("norm1", "pull"),
+        "block": (None, "gates"),
     }
     tasks = []
-    for name, width in widths.items():
-        left, right, first = operands[name]
+    for name, columns in widths.items():
+        left, right = operands[name]
         pieces = 1 if name == "out" else 2
+        size = columns // pieces
         for piece in range(pieces):
-            column = piece * (width // pieces)
-            tasks.append((name, left, right, first + column, width // pieces, column))
+            tasks.append((name, left, right, piece * size, size, piece * size))
     widest = max(t[4] for t in tasks)
     dma = pltpu.SemaphoreType.DMA
     any_, vmem = pl.BlockSpec(memory_space=pl.ANY), pl.BlockSpec(memory_space=pltpu.VMEM)
     ins = [
-        ("pull", pull, vmem), ("w_in", w_in, vmem), ("norm1", norm1, any_),
-        ("grady", grady, any_),
-        ("hidden", hidden, any_), ("gbo", gbo, any_), ("mixed", mixed, any_),
-        ("gates", gates, vmem), ("dots", dots, vmem), ("s1", s1, any_), ("x", x, any_),
-        ("local", local, any_), ("gains", gains, vmem), ("mine", mine, vmem),
-        ("small_start", small, vmem),
+        ("gm", gm, any_), ("both", both, any_), ("conv", conv, any_), ("r", r, any_),
+        ("i", i, any_), ("state", state, any_), ("mask", mask, vmem), ("params", params, vmem),
+        ("dense", dense, any_), ("w_in", w_in, any_), ("norm1", norm1, any_),
+        ("grady", grady, any_), ("hidden", hidden, any_), ("gbo", gbo, any_),
+        ("mixed", mixed, any_), ("s1", s1, any_), ("x", x, any_), ("local", local, any_),
+        ("gains", gains, vmem), ("mine", mine, vmem), ("gain2", gain2, vmem),
     ]
-    outs = [("grad_x", jax.ShapeDtypeStruct((count, part), BF16), vmem)]
-    for name, width in widths.items():
-        outs.append(("grad_" + name, jax.ShapeDtypeStruct((heights[name], width), F32), any_))
-    outs.append(("small", jax.ShapeDtypeStruct((16, features), F32), vmem))
+    shape = jax.ShapeDtypeStruct
+    outs = [("grad_x", shape((count, part), BF16), vmem)]
+    for name, columns in widths.items():
+        outs.append(("grad_" + name, shape((heights[name], columns), F32), any_))
+    outs.append(("small", shape((16, features), F32), vmem))
+    wide = pltpu.VMEM((step, width), F32)
+    tall = pltpu.VMEM((step + 8, width), F32)
+    eight = pltpu.VMEM((8, width), F32)
+    columns = pltpu.VMEM((width // 128, step, 128), F32)
     scratch = [
-        ("parts", pltpu.VMEM((halves, mp, step, part), BF16)),
-        ("rights", pltpu.VMEM((halves, mp - 1, step, part), BF16)),
-        ("lefts", pltpu.VMEM((halves, mp - 1, step, part), BF16)),
+        ("gm_here", wide), ("both_here", pltpu.VMEM((step, 2 * width), F32)),
+        ("conv_here", wide), ("r_here", wide), ("i_here", wide), ("state_here", wide),
+        ("halo", eight), ("start", eight), ("back", eight), ("after", eight),
+        ("dparams", eight), ("params_sum", eight),
+        ("dense_here", pltpu.VMEM(dense.shape, BF16)), ("w_in_here", pltpu.VMEM(w_in.shape, BF16)),
+        ("pull", pltpu.VMEM((count, 2 * width), BF16)),
+        ("rates", pltpu.VMEM((step, 2 * width), BF16)),
+        ("dots", pltpu.VMEM((step, 128), F32)),
+        ("padded", tall), ("before", tall), ("decay", columns), ("adjoint", columns),
+        ("coef", columns), ("dconv", tall), ("sums", pltpu.VMEM((8, 8, width), F32)),
+        ("dense_sum", pltpu.VMEM((width, 2 * width), F32)),
+        ("flat", pltpu.VMEM((span + 16, 2 * width), F32)),
+        ("gates", pltpu.VMEM((256, 2 * width), BF16)),
+        ("norm_here", pltpu.VMEM((step, features), BF16)),
+        ("lhs", pltpu.VMEM((count, features), BF16)),
+        ("rhs", pltpu.VMEM((2, count, widest), BF16)),
+        ("local_here", pltpu.VMEM((step, part), F32)), ("x_here", pltpu.VMEM((step, part), BF16)),
+        ("s1_here", pltpu.VMEM((step, 128), F32)),
+        ("parts", pltpu.VMEM((chunks, mp, step, part), BF16)),
+        ("rights", pltpu.VMEM((chunks, mp - 1, step, part), BF16)),
+        ("lefts", pltpu.VMEM((chunks, mp - 1, step, part), BF16)),
         ("sends", pltpu.VMEM((4, own, widest), BF16)),
         ("stage", pltpu.VMEM((2, own, widest), F32)),
-        ("near_local", pltpu.VMEM((step, part), F32)),
-        ("local_sem", dma),
         ("gain", pltpu.VMEM((8, features), F32)),
-        ("dots_row", pltpu.VMEM((8, count), F32)),
-        ("dots_in", pltpu.VMEM((2, 8, count), F32)),
-        ("dots_col", pltpu.VMEM((count, 128), F32)),
+        ("dots_row", pltpu.VMEM((chunks, 8, step), F32)),
+        ("dots_in", pltpu.VMEM((chunks, 2, 8, step), F32)),
+        ("dots_col", pltpu.VMEM((step, 128), F32)),
         ("small_in", pltpu.VMEM((5, 16, features), F32)),
-        ("fold_sent", dma((halves, mp))),
-        ("fold_right", dma((halves, mp))),
-        ("fold_left", dma((halves, mp))),
-        ("task_sent", dma((len(tasks), 8))),
-        ("task_came", dma((len(tasks), 8))),
-        ("load_sem", dma((8,))),
-        ("store_sem", dma((2,))),
-        ("dots_sent", dma((2,))),
-        ("dots_came", dma((2,))),
-        ("small_sent", dma((5,))),
-        ("small_came", dma((5,))),
+        ("chunk_sem", dma((8,))), ("norm_sem", dma), ("left_sem", dma), ("right_sem", dma((2,))),
+        ("end_sem", dma((3,))), ("whole_sem", dma((2,))), ("store_sem", dma((2,))),
+        ("fold_sent", dma((chunks, mp))), ("fold_right", dma((chunks, mp))),
+        ("fold_left", dma((chunks, mp))),
+        ("task_sent", dma((len(tasks), 8))), ("task_came", dma((len(tasks), 8))),
+        ("dots_sent", dma((chunks, 2))), ("dots_came", dma((chunks, 2))),
+        ("small_sent", dma((5,))), ("small_came", dma((5,))),
     ]
-    loaded = ("norm1", "grady", "hidden", "x", "s1", "gbo", "mixed")
-    for name, value, _ in ins:
-        if name in loaded:
-            scratch.append((name + "_here", pltpu.VMEM(value.shape, value.dtype)))
-    for k, (name, _, _, _, width, _) in enumerate(tasks):
-        tall = heights[name]
-        scratch.append(("held%d" % k, pltpu.VMEM((4, tall, width), BF16)))
+    for k, (name, _, _, _, size, _) in enumerate(tasks):
+        rows = heights[name]
+        scratch.append(("held%d" % k, pltpu.VMEM((4, rows, size), BF16)))
         for kind in ("far", "first", "second"):
-            scratch.append(("%s%d" % (kind, k), pltpu.VMEM((tall, width), BF16)))
+            scratch.append(("%s%d" % (kind, k), pltpu.VMEM((rows, size), BF16)))
     names = [i[0] for i in ins] + [o[0] for o in outs] + [k[0] for k in scratch]
     return pl.pallas_call(
-        functools.partial(tail_kernel, mp, tuple(tasks), loaded, tuple(names)),
+        functools.partial(tail_kernel, mp, tuple(tasks), tuple(names)),
         in_specs=[i[2] for i in ins],
         out_specs=[o[2] for o in outs],
         out_shape=[o[1] for o in outs],
@@ -1917,45 +2043,36 @@
         dp, mp, 4, mixed, inputs, cotangent, live, gains, mine(gains), w_out,
         w_gate, up, down,
     )
-    blank = jnp.zeros((8, width), F32)
-    back, tail_rows = blank, blank
-    pulls, rates, dots = [None] * CHUNKS, [None] * CHUNKS, [None] * CHUNKS
-    params_total = 0.0
-    gms, boths = cut(gm), cut(both)
-    saves = list(zip(cut(conv), cut(r), cut(i), cut(state)))
-    for c in reversed(range(CHUNKS)):
-        low = c * step
-        halo = blank if c == 0 else both[low - 8 : low, :width]
-        start = blank if c == 0 else state[low - 8 : low]
-        pull, rate, dparams, back, tail_rows, dot = rnn_backward(
-            gms[c], boths[c], halo, start, saves[c], tail_masks[c], dense, rnn_params,
-            back, tail_rows,
-        )
-        params_total = params_total + dparams
-        pulls[c], rates[c], dots[c] = pull, rate, dot
-    pull = jnp.concatenate(pulls)
-    dots = jnp.concatenate(dots)
-    grad_gates = diagonal_blocks(inner_rows(conv.astype(BF16), jnp.concatenate(rates)), span)
     gain2 = jnp.sum(gain2, axis=0, keepdims=True)
-
     if dp == 8:
         rows = span // dp
-        padded = jnp.pad(
-            grad_gates.astype(BF16).reshape(dp, rows, 2 * width), ((0, 0), (0, 32 - rows), (0, 0))
-        ).reshape(dp * 32, 2 * width)
-        small = jnp.concatenate(
-            [
-                jnp.zeros((1, features), F32), gain2 / mp, jnp.zeros((6, features), F32),
-                jnp.pad(params_total, ((0, 0), (0, features - width))),
-            ]
-        )
-        input_grad, grad_down, grad_in, grad_out, grad_gates, small = tail(
-            mp, pull, w_in, normed, grad_y, hidden, gbo, mixed, padded, dots,
-            s1, inputs, local, gains, mine(gains), small,
+        input_grad, grad_down, grad_out, grad_in, grad_gates, small = tail(
+            mp, 4, span, (gm, both, conv, r, i, state), mask_tail, rnn_params, dense, w_in, normed,
+            grad_y, hidden, gbo, mixed, s1, inputs, local, gains, mine(gains), gain2,
         )
         grad_gates = grad_gates[:rows]
         grad_gains, grad_params = small[0:2], small[8:16, :width]
     else:
+        blank = jnp.zeros((8, width), F32)
+        back, tail_rows = blank, blank
+        pulls, rates, dots = [None] * CHUNKS, [None] * CHUNKS, [None] * CHUNKS
+        params_total = 0.0
+        gms, boths = cut(gm), cut(both)
+        saves = list(zip(cut(conv), cut(r), cut(i), cut(state)))
+        for c in reversed(range(CHUNKS)):
+            low = c * step
+            halo = blank if c == 0 else both[low - 8 : low, :width]
+            start = blank if c == 0 else state[low - 8 : low]
+            pull, rate, dparams, back, tail_rows, dot = rnn_backward(
+                gms[c], boths[c], halo, start, saves[c], tail_masks[c], dense, rnn_params,
+                back, tail_rows,
+            )
+            params_total = params_total + dparams
+            pulls[c], rates[c], dots[c] = pull, rate, dot
+        pull = jnp.concatenate(pulls)
+        dots = jnp.concatenate(dots)
+        grad_gates = diagonal_blocks(inner_rows(conv.astype(BF16), jnp.concatenate(rates)), span)
+
         parts = []
         gain1 = 0.0
         norms, s1 = cut(normed), s1[:, 0:1]

time: 608 us -> 569 us (0.936)
  Pallas kernels: 566 us -> 533 us
    pallas_call x2 -> x1, Pallas kernels: 145 us -> 112 us  [tail(): pl.pallas_call(functools.partial(tail_kernel, mp, tuple(tasks), tuple(nam...]
where the time goes in v5:
time: 569 us; the launch traced here: 560 us
  Pallas kernels  533 us (94%)
  local copies, waits for them, and re-layouts  20.3 us (4%)
    pallas_call x1, Pallas kernels, middle(): pl.pallas_call(functools.partial(middle_kernel, dp, mp, chunks), in_specs...  324 us
    pallas_call x1, Pallas kernels, tail(): pl.pallas_call(functools.partial(tail_kernel, mp, tuple(tasks), tuple(nam...  112 us
    pallas_call x1, Pallas kernels, head(): pl.pallas_call(functools.partial(head_kernel, dp, mp, tuple(names)), in_s...  97.6 us
    unnamed x30, local copies, waits for them, and re-layouts  11.6 us

profile of v5, /device:TPU:0, one launch (start us, length us, event | category | flops | bytes accessed | tf_op | source)
XLA Modules:
  0.0 559.9 jit_solution(13462221993741888258)
XLA Ops:
  0.7 0.8 reduce-window.8
  1.5 0.1 convert_reduce_fusion
  1.7 1.0 copy.44.refs_3_
  2.7 2.0 pad_maximum_fusion.refs_4_
  4.7 1.9 copy.43
  6.6 0.6 fusion.2.refs_7_
  7.3 97.6 %head.1 = (bf16[2048,1280]{1,0:T(8,128)(2,1)}, bf16[2048,640]{1,0:T(8,128)(2,1)}, bf16[2048,1536]{1,0:T(8,128)(2,1)}, bf16[640,1280]{1,0:T(8,128)(2,1)}, bf16[10...) custom-call(bf16[1024,512]{1,0:T(8,128)(2,1)} %refs_16_.1, ...), custom_call_target="tpu_custom_call" | custom-call | tf_op jit(solution)/shard_map/head/pallas_call | solution.py:1013
  104.9 1.3 constant_dynamic-slice_fusion.refs_5_.refs_19_
  106.2 1.0 broadcast_in_dim.9.refs_3_
  107.2 1.2 copy.45
  108.3 323.8 %middle.1 = (bf16[1024,512]{1,0:T(8,128)(2,1)}, f32[1024,640]{1,0:T(8,128)}, bf16[1024,2048]{1,0:T(8,128)(2,1)}, f32[1024,512]{1,0:T(8,128)}, bf16[1024,1536]{1,...) custom-call(bf16[1024,640]{1,0:T(8,128)(2,1)} %get-tuple-element.39., ...), custom_call_target="tpu_custom_call" | custom-call | tf_op jit(solution)/shard_map/middle/pallas_call | solution.py:1467
  432.1 1.5 reduce_sum.19
  433.6 0.8 concatenate.11.refs_6_
  434.4 112.0 %tail.1 = (bf16[1024,512]{1,0:T(8,128)(2,1)}, f32[256,1536]{1,0:T(8,128)}, f32[256,640]{1,0:T(8,128)}, f32[256,1280]{1,0:T(8,128)}, f32[32,1280]{1,0:T(8,128)}, /*index=5*/f32[16,2048]{1,0:T(8,128)}) custom-call(f32[1024,640]{1,0:T(8,128)} %get-tuple-element.43.refs_0_, f32[1024,1280]{1,0:T(8,128)} %get-tuple-element.44.refs_1_, ...), custom_call_target="tpu_custom_call" | custom-call | tf_op jit(solution)/shard_map/tail/pallas_call | solution.py:1958
  546.4 3.2 copy.48
  549.6 1.1 fusion.6
  550.7 1.1 copy.47
  551.8 0.7 fusion.7
  552.4 1.3 slice.38
  553.8 1.4 slice.37
  555.2 1.0 copy.53
  556.2 1.0 copy.54
  557.2 1.1 copy.55
  558.3 1.1 copy.56
  (27 shorter events, 0.2 us)
Async XLA Ops:
  0.6 6.0 %copy-start.10 = (bf16[20,640]{1,0:T(8,128)(2,1)S(1)}, bf16[20,640]{1,0:T(8,128)(2,1)}, u32[]{:S(2)}) copy-start(bf16[20,640]{1,0:T(8,128)(2,1)} %param.20) | copy-start | bytes 76804
  0.7 6.0 %copy-start.9 = (bf16[20,640]{1,0:T(8,128)(2,1)S(1)}, bf16[20,640]{1,0:T(8,128)(2,1)}, u32[]{:S(2)}) copy-start(bf16[20,640]{1,0:T(8,128)(2,1)} %param.21) | copy-start | bytes 76804
  4.7 102.5 %copy-start.6 = (bf16[1536,256]{1,0:T(8,128)(2,1)S(1)}, bf16[1536,256]{1,0:T(8,128)(2,1)}, u32[]{:S(2)}) copy-start(bf16[1536,256]{1,0:T(8,128)(2,1)} %param.25) | copy-start | bytes 2359300
  108.3 325.3 %copy-start = (f32[1024,8]{1,0:T(8,128)S(1)}, f32[1024,8]{1,0:T(8,128)}, u32[]{:S(2)}) copy-start(f32[1024,8]{1,0:T(8,128)} %copy.44.refs_3_) | copy-start | bytes 98308
  546.4 3.2 copy-start.3
  546.4 4.3 copy-start.7
  549.6 2.2 copy-start.8
  549.6 5.7 %copy-start.4 = (bf16[1024,512]{1,0:T(8,128)(2,1)S(1)}, bf16[1024,512]{1,0:T(8,128)(2,1)}, u32[]{:S(2)}) copy-start(bf16[1024,512]{1,0:T(8,128)(2,1)} %get-tuple-element.134) | copy-start | bytes 3145732
  550.7 6.5 %copy-start.2 = (f32[256,1536]{1,0:T(8,128)S(1)}, f32[256,1536]{1,0:T(8,128)}, u32[]{:S(2)}) copy-start(f32[256,1536]{1,0:T(8,128)} %get-tuple-element.142) | copy-start | bytes 4718596
  551.8 4.4 copy-start.5
  556.2 2.1 copy-start.1

commit v6 on v5

--- a/solution.py
+++ b/solution.py
@@ -190,22 +190,12 @@
     return pl.ds(pl.multiple_of(index * size, size), size)
 
 
-def put(ref, rows, values):
-    for j in range(ref.shape[0]):
-        ref[j, rows, :] = values[:, j * 128 : (j + 1) * 128]
-
-
-def get(ref, rows):
-    return jnp.concatenate([ref[j, rows, :] for j in range(ref.shape[0])], axis=1)
-
-
 def rnn_forward_kernel(
     both_ref, halo_ref, start_ref, mask_ref, gates_ref, params_ref,
     mixed_ref, conv_ref, r_ref, i_ref, state_ref, end_ref,
-    padded, high, low, decay, drive,
+    padded, high, low,
 ):
     count, width = conv_ref.shape
-    seg = count // 8
     tiles = count // TILE
     padded[0:8, :] = halo_ref[...]
     padded[8:, :] = both_ref[:, 0:width]
@@ -238,7 +228,9 @@
 
     strength = DECAY_SCALE * jax.nn.softplus(-params_ref[TAPS + 3 : TAPS + 4, :])
 
-    def prepare(t):
+    place = lax.broadcasted_iota(jnp.int32, (8, width), 0)
+
+    def advance(t, carry):
         rows = rows_at(t, TILE)
         keep = mask_ref[rows, :][:, 0:1]
         r = jax.nn.sigmoid(r_ref[rows, :] + params_ref[TAPS + 1 : TAPS + 2, :])
@@ -246,42 +238,27 @@
         log_a = -strength * r
         scale = jnp.sqrt(jnp.maximum(one_less_exp(2.0 * log_a), ROOT_FLOOR))
         scale = jnp.where(keep > 0.0, scale, 1.0)
-        put(decay, rows, jnp.exp(log_a) * keep)
-        put(drive, rows, scale * i * conv_ref[rows, :])
+        decay = jnp.exp(log_a) * keep
+        drive = scale * i * conv_ref[rows, :]
         r_ref[rows, :] = r
         i_ref[rows, :] = i
-
-    tile_loop(tiles, prepare)
-
-    def scan(t, carry):
-        held, prod = carry
-        rows = pl.ds(t, 8, stride=seg)
-        a = get(decay, rows)
-        held = a * held + get(drive, rows)
-        prod = a * prod
-        put(drive, rows, held)
-        put(decay, rows, prod)
-        return held, prod
-
-    shape = (8, width)
-    held, prod = lax.fori_loop(0, seg, scan, (jnp.zeros(shape, F32), jnp.ones(shape, F32)))
-    carry = start_ref[0:1, :]
-    carries = []
-    for s in range(8):
-        carries.append(carry)
-        carry = prod[s : s + 1, :] * carry + held[s : s + 1, :]
-    end_ref[...] = jnp.broadcast_to(carry, shape)
-
-    small = min(TILE, seg)
-    for s in range(8):
-
-        def finish(t, s=s):
-            rows = pl.ds(pl.multiple_of(s * seg + t * small, small), small)
-            state = get(drive, rows) + get(decay, rows) * carries[s]
-            state_ref[rows, :] = state
-            mixed_ref[rows, :] = (state * gelu(both_ref[rows, width:])).astype(BF16)
-
-        tile_loop(seg // small, finish)
+        states = []
+        for g in range(0, TILE, 8):
+            a, held = decay[g : g + 8, :], drive[g : g + 8, :]
+            for s in (1, 2, 4):
+                inside = place >= s
+                held = held + a * jnp.where(inside, pltpu.roll(held, s, 0), 0.0)
+                a = a * jnp.where(inside, pltpu.roll(a, s, 0), 1.0)
+            held = held + a * carry
+            carry = jnp.broadcast_to(held[7:8, :], (8, width))
+            states.append(held)
+        state = jnp.concatenate(states, axis=0)
+        state_ref[rows, :] = state
+        mixed_ref[rows, :] = (state * gelu(both_ref[rows, width:])).astype(BF16)
+        return carry
+
+    carry = jnp.broadcast_to(start_ref[0:1, :], (8, width))
+    end_ref[...] = lax.fori_loop(0, tiles, advance, carry)
 
 
 def rnn_forward(both, halo, start, mask, gates, params):
@@ -298,8 +275,6 @@
             pltpu.VMEM((count + 8, width), F32),
             pltpu.VMEM((count, width), BF16),
             pltpu.VMEM((count, width), BF16),
-            pltpu.VMEM((width // 128, count, 128), F32),
-            pltpu.VMEM((width // 128, count, 128), F32),
         ],
         compiler_params=pltpu.CompilerParams(vmem_limit_bytes=VMEM_BYTES),
         cost_estimate=pl.CostEstimate(
@@ -314,10 +289,9 @@
     gm_ref, both_ref, halo_ref, start_ref, conv_ref, r_ref, i_ref, state_ref, mask_ref,
     gates_ref, params_ref, back_ref, tail_ref,
     grads_ref, rates_ref, dparams_ref, back_out_ref, tail_out_ref, dots_ref,
-    padded, before, decay, adjoint, coef, dconv, sums,
+    padded, before, dconv, sums,
 ):
     count, width = conv_ref.shape
-    seg = count // 8
     tiles = count // TILE
     padded[0:8, :] = halo_ref[...]
     padded[8:, :] = both_ref[:, 0:width]
@@ -325,70 +299,61 @@
     before[8:, :] = state_ref[...]
     strength = DECAY_SCALE * jax.nn.softplus(-params_ref[TAPS + 3 : TAPS + 4, :])
 
-    def prepare(t):
-        rows = rows_at(t, TILE)
+    sums[...] = jnp.zeros_like(sums)
+    place = lax.broadcasted_iota(jnp.int32, (8, width), 0)
+
+    def fold(values):
+        return jnp.sum(values.reshape(-1, 8, width), axis=0)
+
+    def chain(t, carry):
+        later, later_decay = carry
+        base = pl.multiple_of((tiles - 1 - t) * TILE, TILE)
+        rows = pl.ds(base, TILE)
         keep = mask_ref[rows, :][:, 0:1]
         gm = gm_ref[rows, :]
         value, slope = gelu_and_slope(both_ref[rows, width:])
-        put(adjoint, rows, gm * value)
         grads_ref[rows, width:] = (gm * state_ref[rows, :] * slope).astype(BF16)
-        put(decay, rows, jnp.exp(-strength * r_ref[rows, :]) * keep)
-
-    tile_loop(tiles, prepare)
-
-    def scan(t, carry):
-        held, prod = carry
-        rows = pl.ds(seg - 1 - t, 8, stride=seg)
-        a = get(decay, rows)
-        total = get(adjoint, rows) + held
-        put(adjoint, rows, total)
-        put(coef, rows, prod)
-        return a * total, a * prod
-
-    shape = (8, width)
-    held, prod = lax.fori_loop(0, seg, scan, (jnp.zeros(shape, F32), jnp.ones(shape, F32)))
-    carry = back_ref[0:1, :]
-    carries = [None] * 8
-    for s in reversed(range(8)):
-        carries[s] = carry
-        carry = prod[s : s + 1, :] * carry + held[s : s + 1, :]
-    back_out_ref[...] = jnp.broadcast_to(carry, shape)
-
-    sums[...] = jnp.zeros_like(sums)
-
-    def fold(values):
-        return jnp.sum(values.reshape(-1, 8, width), axis=0)
-
-    small = min(TILE, seg)
-    for s in range(8):
-
-        def chain(t, s=s):
-            base = pl.multiple_of(s * seg + t * small, small)
-            rows = pl.ds(base, small)
-            keep = mask_ref[rows, :][:, 0:1]
-            a = get(adjoint, rows) + get(coef, rows) * carries[s]
-            r, i, conv = r_ref[rows, :], i_ref[rows, :], conv_ref[rows, :]
-            fall = get(decay, rows)
-            prior = before[pl.ds(base, small + 8), :][7 : 7 + small, :]
-            room = one_less_exp(-2.0 * strength * r)
-            bound = jnp.maximum(room, ROOT_FLOOR)
-            inverse = lax.rsqrt(bound)
-            live = keep > 0.0
-            scale = jnp.where(live, bound * inverse, 1.0)
-            open_ = jnp.where(room > ROOT_FLOOR, inverse, 0.0)
-            driven = a * i
-            dlog = fall * (a * prior - fall * driven * conv * open_)
-            common = a * scale
-            drec = dlog * (-strength) * r * (1.0 - r)
-            dinp = common * conv * i * (1.0 - i)
-            rates_ref[rows, 0:width] = drec.astype(BF16)
-            rates_ref[rows, width:] = dinp.astype(BF16)
-            dconv[rows, :] = common * i
-            sums[5] += fold(drec)
-            sums[6] += fold(dinp)
-            sums[7] += fold(dlog * r)
-
-        tile_loop(seg // small, chain)
+        given = gm * value
+        r, i, conv = r_ref[rows, :], i_ref[rows, :], conv_ref[rows, :]
+        fall = jnp.exp(-strength * r) * keep
+        adjoints = []
+        for g in reversed(range(0, TILE, 8)):
+            a = fall[g : g + 8, :]
+            ahead = jnp.where(place == 7, later_decay, pltpu.roll(a, 7, 0))
+            held = given[g : g + 8, :]
+            for s in (1, 2, 4):
+                inside = place < 8 - s
+                held = held + ahead * jnp.where(inside, pltpu.roll(held, 8 - s, 0), 0.0)
+                ahead = ahead * jnp.where(inside, pltpu.roll(ahead, 8 - s, 0), 1.0)
+            held = held + ahead * later
+            later = jnp.broadcast_to(held[0:1, :], (8, width))
+            later_decay = jnp.broadcast_to(a[0:1, :], (8, width))
+            adjoints.append(held)
+        a = jnp.concatenate(adjoints[::-1], axis=0)
+        prior = before[pl.ds(base, TILE + 8), :][7 : 7 + TILE, :]
+        room = one_less_exp(-2.0 * strength * r)
+        bound = jnp.maximum(room, ROOT_FLOOR)
+        inverse = lax.rsqrt(bound)
+        scale = jnp.where(keep > 0.0, bound * inverse, 1.0)
+        open_ = jnp.where(room > ROOT_FLOOR, inverse, 0.0)
+        driven = a * i
+        dlog = fall * (a * prior - fall * driven * conv * open_)
+        common = a * scale
+        drec = dlog * (-strength) * r * (1.0 - r)
+        dinp = common * conv * i * (1.0 - i)
+        rates_ref[rows, 0:width] = drec.astype(BF16)
+        rates_ref[rows, width:] = dinp.astype(BF16)
+        dconv[rows, :] = common * i
+        sums[5] += fold(drec)
+        sums[6] += fold(dinp)
+        sums[7] += fold(dlog * r)
+        return later, later_decay
+
+    later = jnp.broadcast_to(back_ref[0:1, :], (8, width))
+    later, later_decay = lax.fori_loop(
+        0, tiles, chain, (later, jnp.ones((8, width), F32))
+    )
+    back_out_ref[...] = later * later_decay
 
     block = min(256, count)
 
@@ -450,9 +415,6 @@
         scratch_shapes=[
             pltpu.VMEM((count + 8, width), F32),
             pltpu.VMEM((count + 8, width), F32),
-            pltpu.VMEM((width // 128, count, 128), F32),
-            pltpu.VMEM((width // 128, count, 128), F32),
-            pltpu.VMEM((width // 128, count, 128), F32),
             pltpu.VMEM((count + 8, width), F32),
             pltpu.VMEM((8, 8, width), F32),
         ],
@@ -900,7 +862,7 @@
             ref["dense_here"], ref["params"],
             ref["mixed_here"].at[slot], ref["conv_here"].at[slot], ref["r_here"].at[slot],
             ref["i_here"].at[slot], ref["state_here"].at[slot], ref["end"],
-            ref["padded"], ref["high"], ref["low"], ref["decay"], ref["drive"],
+            ref["padded"], ref["high"], ref["low"],
         )
         ref["halo"][...] = both[slot, step - 8 :, 0:width]
         ref["start"][...] = ref["end"][...]
@@ -914,7 +876,8 @@
     if square:
         for item in squares[:2]:
             item.step_one()
-        squares[2].start()
+        for item in squares[2:]:
+            item.start()
         for item in squares[:2]:
             item.step_two()
     gather.finish(0)
@@ -935,22 +898,21 @@
             ]
             for copy in pass_on:
                 copy.start()
-        if c == 3 and square:
-            squares[3].step_one()
-        compute(c)
-        if c == 0 and square:
-            squares[2].step_one()
-            squares[3].start()
-        if c == 1 and square:
-            squares[2].step_two()
         if c + 3 < chunks:
             begin(c + 3)
+        compute(c)
+        if square and (c + 1) * 4 == chunks:
+            squares[2].step_one()
+        if square and (c + 1) * 2 == chunks:
+            squares[2].step_two()
+            squares[3].step_one()
+        if square and (c + 1) * 4 == 3 * chunks:
+            squares[3].step_two()
         if c + 1 < chunks:
             for s in range(2, mp - 1):
                 gather.step(c + 1, s)
             gather.finish(c + 1)
     if square:
-        squares[3].step_two()
         squares[2].finish()
         squares[3].finish()
         for item in squares:
@@ -988,7 +950,6 @@
         ("s1_out", shape((count, 128), F32)),
     ]
     wide = pltpu.VMEM((2, step, width), F32)
-    columns = pltpu.VMEM((width // 128, step, 128), F32)
     scratch = [
         ("blocks", pltpu.VMEM((chunks, mp, step, part), BF16)),
         ("w_in_here", pltpu.VMEM((features, 2 * width), BF16)),
@@ -1004,7 +965,6 @@
         ("end", pltpu.VMEM((8, width), F32)),
         ("padded", pltpu.VMEM((step + 8, width), F32)),
         ("high", pltpu.VMEM((step, width), BF16)), ("low", pltpu.VMEM((step, width), BF16)),
-        ("decay", columns), ("drive", columns),
         ("spread_sent", dma((chunks, 2 * mp))), ("spread_came", dma((chunks, mp))),
         ("square_sent", dma((4, 8))), ("square_came", dma((4, 8))), ("square_own", dma((4,))),
         ("load_sem", dma((chunks,))), ("store_sem", dma((2, 8))), ("pass_sem", dma((2,))),
@@ -1024,29 +984,29 @@
 
 
 MIDDLE_ORDER = (
-    ("d", 0, 0), ("A", 0, 0), ("d", 0, 1), ("d", 0, 2), ("a", 1, 0), ("d", 1, 0), ("a", 2, 0),
-    ("d", 0, 3), ("J", 0, 0), ("d", 2, 0), ("e", 0, 0), ("A", 0, 1), ("e", 1, 0), ("e", 2, 0),
-    ("a", 1, 1), ("d", 1, 2), ("e", 3, 0), ("A", 0, 2), ("S", 1, 0), ("a", 2, 1), ("d", 1, 1),
-    ("S", 2, 0), ("d", 2, 2), ("J", 0, 1), ("d", 3, 0), ("a", 1, 2), ("e", 0, 1), ("S", 3, 0),
-    ("H", 0, 0), ("a", 2, 2), ("d", 1, 3), ("d", 2, 1), ("G", 0, 0), ("d", 3, 2), ("c", 1, 0),
-    ("e", 1, 1), ("J", 0, 2), ("e", 0, 2), ("d", 3, 1), ("e", 2, 1), ("O", 0, 0), ("e", 3, 1),
-    ("b", 1, 0), ("c", 2, 0), ("A", 0, 3), ("e", 1, 2), ("K", 0, 0), ("a", 1, 3), ("b", 2, 0),
-    ("e", 2, 2), ("H", 0, 1), ("d", 2, 3), ("G", 0, 1), ("e", 3, 2), ("O", 0, 1), ("f", 1, 0),
-    ("c", 1, 1), ("a", 2, 3), ("c", 2, 1), ("Y", 0, 0), ("f", 2, 0), ("b", 1, 1), ("J", 0, 3),
-    ("K", 0, 1), ("H", 0, 2), ("e", 0, 3), ("B", 0, 0), ("f", 1, 1), ("G", 0, 2), ("e", 1, 3),
-    ("f", 2, 1), ("c", 1, 2), ("b", 2, 1), ("c", 2, 2), ("B", 0, 1), ("e", 2, 3), ("Y", 0, 1),
-    ("K", 0, 2), ("O", 0, 2), ("e", 3, 3), ("f", 1, 2), ("d", 3, 3), ("H", 0, 3), ("f", 2, 2),
-    ("G", 0, 3), ("b", 1, 2), ("B", 0, 2), ("O", 0, 3), ("D", 0, 0), ("c", 1, 3), ("W", 0, 0),
-    ("D", 0, 1), ("c", 2, 3), ("D", 0, 2), ("K", 0, 3), ("W", 0, 1), ("b", 2, 2), ("D", 0, 3),
-    ("W", 0, 2), ("D", 0, 4), ("Z", 0, 0), ("W", 0, 3), ("f", 1, 3), ("D", 0, 5), ("b", 1, 3),
-    ("f", 2, 3), ("Z", 0, 1), ("b", 2, 3), ("W", 0, 4), ("B", 0, 3), ("W", 0, 5), ("Y", 0, 2),
-    ("Z", 0, 2), ("Y", 0, 3), ("Z", 0, 3), ("Z", 0, 4), ("Z", 0, 5),
+    ("d", 0, 0), ("A", 0, 0), ("d", 0, 1), ("d", 1, 0), ("a", 1, 0), ("d", 2, 0), ("a", 2, 0),
+    ("d", 0, 2), ("J", 0, 0), ("e", 0, 0), ("A", 0, 1), ("e", 1, 0), ("d", 1, 2), ("e", 2, 0),
+    ("d", 3, 0), ("S", 1, 0), ("a", 1, 1), ("a", 2, 1), ("d", 2, 2), ("d", 1, 1), ("d", 0, 3),
+    ("e", 3, 0), ("S", 2, 0), ("A", 0, 2), ("d", 2, 1), ("S", 3, 0), ("d", 1, 3), ("J", 0, 1),
+    ("e", 0, 1), ("a", 1, 2), ("H", 0, 0), ("a", 2, 2), ("e", 1, 1), ("G", 0, 0), ("O", 0, 0),
+    ("c", 1, 0), ("e", 2, 1), ("J", 0, 2), ("d", 2, 3), ("d", 3, 1), ("d", 3, 2), ("e", 3, 1),
+    ("e", 0, 2), ("b", 1, 0), ("A", 0, 3), ("c", 2, 0), ("H", 0, 1), ("e", 1, 2), ("K", 0, 0),
+    ("G", 0, 1), ("a", 1, 3), ("e", 2, 2), ("b", 2, 0), ("f", 1, 0), ("O", 0, 1), ("e", 3, 2),
+    ("a", 2, 3), ("c", 1, 1), ("H", 0, 2), ("f", 2, 0), ("c", 2, 1), ("b", 1, 1), ("J", 0, 3),
+    ("d", 3, 3), ("Y", 0, 0), ("B", 0, 0), ("e", 0, 3), ("K", 0, 1), ("b", 2, 1), ("G", 0, 2),
+    ("f", 1, 1), ("c", 1, 2), ("e", 1, 3), ("f", 2, 1), ("Y", 0, 1), ("c", 2, 2), ("B", 0, 1),
+    ("e", 2, 3), ("K", 0, 2), ("O", 0, 2), ("f", 1, 2), ("e", 3, 3), ("H", 0, 3), ("f", 2, 2),
+    ("G", 0, 3), ("b", 1, 2), ("B", 0, 2), ("O", 0, 3), ("c", 1, 3), ("D", 0, 0), ("D", 0, 1),
+    ("c", 2, 3), ("W", 0, 0), ("D", 0, 2), ("Z", 0, 0), ("W", 0, 1), ("K", 0, 3), ("D", 0, 3),
+    ("W", 0, 2), ("f", 1, 3), ("Z", 0, 1), ("b", 2, 2), ("b", 1, 3), ("W", 0, 3), ("D", 0, 4),
+    ("f", 2, 3), ("D", 0, 5), ("W", 0, 4), ("Z", 0, 2), ("W", 0, 5), ("b", 2, 3), ("Y", 0, 2),
+    ("Z", 0, 3), ("B", 0, 3), ("Z", 0, 4), ("Y", 0, 3), ("Z", 0, 5),
 )
 
 
 def middle_kernel(dp, mp, chunks, *refs):
     (
-        mixed_ref, x_ref, cot_ref, live_ref, gains_ref, mine_ref, wout_ref, gate_ref, up_ref,
+        mixed_ref, x_ref, cot_ref, live_ref, gains_ref, wout_ref, gate_ref, up_ref,
         down_ref,
         output_ref, gm_ref, gbo_ref, local_ref, hidden_ref, pulled_ref, norm_ref, grady_ref,
         grad_gate_ref, grad_up_ref, gain_ref,
@@ -1063,6 +1023,7 @@
     z, d = lax.axis_index("mp"), lax.axis_index("dp")
     square = dp == 8
     up_half = w_up.at[:, pl.ds(hidden_width, hidden_width)]
+    own_cols = pl.ds(pl.multiple_of(z * part, part), part)
 
     folds = [
         Fold(z, mp, p, r, l, fold_sent.at[k], fold_right.at[k], fold_left.at[k])
@@ -1169,7 +1130,7 @@
             rows = rows_at(t, TILE)
             base = pl.ds(pl.multiple_of(c * step + t * TILE, TILE), TILE)
             blocks, s2 = stats(c, rows)
-            live = live_ref[base, :][:, 0:1]
+            live = live_ref[base, :][:, TAPS : TAPS + 1]
             for j in range(mp):
                 norm[rows, block_cols(j)] = (
                     blocks[j] * s2 * gains_ref[1:2, block_cols(j)]
@@ -1286,7 +1247,7 @@
                 )
             local[rows, :] = (
                 cots[c, z, rows, :].astype(F32)
-                + s2 * (gn2_mine[slot, rows, :] * mine_ref[1:2, :])
+                + s2 * (gn2_mine[slot, rows, :] * gains_ref[1:2, own_cols])
                 - mid_mine[c, rows, :] * fall
             )
 
@@ -1450,7 +1411,7 @@
             scatter.drain()
 
 
-def middle(dp, mp, chunks, mixed, inputs, cotangent, live, gains, mine, w_out, gate, up, down):
+def middle(dp, mp, chunks, mixed, inputs, cotangent, live, gains, w_out, gate, up, down):
     count, part = inputs.shape
     width, hidden_width = mixed.shape[1], down.shape[1]
     step, features = count // chunks, part * mp
@@ -1466,7 +1427,7 @@
     any_, vmem = pl.BlockSpec(memory_space=pl.ANY), pl.BlockSpec(memory_space=pltpu.VMEM)
     return pl.pallas_call(
         functools.partial(middle_kernel, dp, mp, chunks),
-        in_specs=[vmem, vmem, any_, vmem, vmem, vmem, vmem, any_, any_, any_],
+        in_specs=[vmem, vmem, any_, vmem, vmem, vmem, any_, any_, any_],
         out_specs=[any_] * 10 + [vmem],
         out_shape=(
             jax.ShapeDtypeStruct((count, part), BF16),
@@ -1521,7 +1482,19 @@
             collective_id=0, has_side_effects=True, vmem_limit_bytes=62 * 1024 * 1024
         ),
         name="middle",
-    )(mixed, inputs, cotangent, live, gains, mine, w_out, gate, up, down)
+    )(mixed, inputs, cotangent, live, gains, w_out, gate, up, down)
+
+
+TAIL_ORDER = (
+    ("R", 0, 3), ("R", 0, 2), ("D", 0, 0), ("R", 0, 1), ("D", 0, 1), ("a", 0, 3), ("l", 0, 2),
+    ("W", 0, 0), ("s", 1, 3), ("s", 1, 2), ("R", 0, 0), ("W", 0, 1), ("s", 2, 3), ("D", 0, 2),
+    ("s", 2, 2), ("m", 0, 0), ("l", 0, 3), ("s", 1, 1), ("a", 0, 2), ("g", 0, 0), ("W", 0, 2),
+    ("m", 0, 1), ("a", 0, 1), ("a", 0, 0), ("D", 0, 3), ("s", 1, 0), ("D", 0, 4), ("s", 2, 1),
+    ("m", 0, 2), ("D", 0, 5), ("D", 0, 6), ("I", 0, 3), ("W", 0, 3), ("s", 2, 0), ("Z", 0, 0),
+    ("I", 0, 2), ("W", 0, 4), ("W", 0, 5), ("Z", 0, 1), ("I", 0, 1), ("m", 0, 3), ("W", 0, 6),
+    ("Z", 0, 2), ("I", 0, 0), ("m", 0, 4), ("Z", 0, 3), ("Z", 0, 4), ("Z", 0, 5), ("m", 0, 5),
+    ("Z", 0, 6),
+)
 
 
 def tail_kernel(mp, tasks, names, *refs):
@@ -1538,6 +1511,7 @@
     )
     near = z + 1 - 2 * lax.rem(z, 2)
     apart = z + 2 - 4 * lax.div(z, 2)
+    own_cols = pl.ds(pl.multiple_of(z * part, part), part)
 
     def chunk_rows(c):
         return pl.ds(c * step, step)
@@ -1633,8 +1607,7 @@
             ref["back"], ref["after"],
             pull.at[chunk_rows(c), :], ref["rates"], ref["dparams"], ref["back"], ref["after"],
             ref["dots"],
-            ref["padded"], ref["before"], ref["decay"], ref["adjoint"], ref["coef"],
-            ref["dconv"], ref["sums"],
+            ref["padded"], ref["before"], ref["dconv"], ref["sums"],
         )
         ref["params_sum"][...] += ref["dparams"][...]
         ref["dense_sum"][...] += inner_rows(ref["conv_here"][...].astype(BF16), ref["rates"][...])
@@ -1693,7 +1666,7 @@
             dot = ref["dots_col"][rows, :][:, 0:1]
             grad = (
                 ref["local_here"][rows, :]
-                + s1 * (fold.total(c, rows) * ref["mine"][0:1, :])
+                + s1 * (fold.total(c, rows) * ref["gains"][0:1, own_cols])
                 - ref["x_here"][rows, :].astype(F32) * (s1 * s1 * dot * (1.0 / features))
             )
             ref["grad_x"][base, :] = grad.astype(BF16)
@@ -1770,7 +1743,7 @@
     def small_first():
         small[...] = jnp.zeros_like(small)
         small[0:1, :] = jnp.sum(gain[...], axis=0, keepdims=True) / ref["gains"][0:1, :]
-        small[1:2, :] = ref["gain2"][...] * (1.0 / mp)
+        small[1:2, :] = jnp.sum(ref["gain2"][...], axis=0, keepdims=True) * (1.0 / mp)
         small[8:16, 0:width] = ref["params_sum"][...]
         small_copy(0).start()
 
@@ -1798,69 +1771,35 @@
         for k in range(8):
             gates[k * 32 : (k + 1) * 32, :] = flat[k * rows : k * rows + 32, :].astype(BF16)
 
-    recur(3)
-    for copy in first_rights:
-        copy.wait()
-    left_copy("grady").wait()
-    far_core(0)
-    scatters[0].near_core()
-    fold.step(3, 1)
-    recur(2)
-    fold.step(3, 2)
-    far_core(1)
-    scatters[1].near_core()
-    left_copy("gbo").start()
     out_right = right_copy("mixed", 0, tasks[2][4], 0)
-    out_right.start()
-    dots_add(3, 0)
-    scatters[0].onward()
-    fold.step(2, 1)
-    recur(1)
-    dots_add(2, 0)
-    fold.step(2, 2)
-    left_copy("gbo").wait()
-    out_right.wait()
-    far_core(2)
-    scatters[2].near_core()
-    left_copy("norm1").start()
-    scatters[1].onward()
-    fold.step(1, 1)
-    input_grad(3)
-    recur(0)
-    small_first()
-    gate_blocks()
-    dots_add(1, 0)
-    fold.step(1, 2)
-    small_next(0)
-    left_copy("norm1").wait()
-    far_core(3)
-    small_next(1)
-    scatters[3].near_core()
-    scatters[2].onward()
-    small_next(2)
-    fold.step(0, 1)
-    input_grad(2)
-    far_core(4)
-    scatters[4].near_core()
-    scatters[3].onward()
-    dots_add(0, 0)
-    fold.step(0, 2)
-    for k in (5, 6):
+
+    def load_next(k):
+        left_copy("gbo" if k == 2 else "norm1").start()
+        if k == 2:
+            out_right.start()
+
+    def weight(k):
+        if k == 0:
+            for copy in first_rights:
+                copy.wait()
+            left_copy("grady").wait()
+        if k == 2:
+            out_right.wait()
+        if k in (2, 3):
+            left_copy("norm1").wait()
         far_core(k)
         scatters[k].near_core()
-    scatters[4].onward()
-    finish(0)
-    finish(1)
-    input_grad(1)
-    for k in (5, 6):
-        scatters[k].onward()
-    finish(2)
-    small_next(3)
-    finish(3)
-    input_grad(0)
-    for k in (4, 5, 6):
-        finish(k)
-    small_next(4)
+
+    steps = {
+        "R": recur, "I": input_grad, "D": weight, "W": lambda k: scatters[k].onward(),
+        "Z": finish, "l": load_next, "g": lambda k: gate_blocks(), "a": lambda c: dots_add(c, 0),
+        "m": lambda k: small_next(k - 1) if k else small_first(),
+    }
+    for name, s, c in TAIL_ORDER:
+        if name == "s":
+            fold.step(c, s)
+        else:
+            steps[name](c)
     for copy in stage_wait:
         copy.wait()
     for copy in sending:
@@ -1872,7 +1811,7 @@
 
 
 def tail(mp, chunks, span, rnn, mask, params, dense, w_in, norm1, grady, hidden, gbo, mixed, s1, x,
-         local, gains, mine, gain2):
+         local, gains, gain2):
     gm, both, conv, r, i, state = rnn
     count, part = x.shape
     features, width = part * mp, params.shape[1]
@@ -1901,7 +1840,7 @@
         ("dense", dense, any_), ("w_in", w_in, any_), ("norm1", norm1, any_),
         ("grady", grady, any_), ("hidden", hidden, any_), ("gbo", gbo, any_),
         ("mixed", mixed, any_), ("s1", s1, any_), ("x", x, any_), ("local", local, any_),
-        ("gains", gains, vmem), ("mine", mine, vmem), ("gain2", gain2, vmem),
+        ("gains", gains, vmem), ("gain2", gain2, vmem),
     ]
     shape = jax.ShapeDtypeStruct
     outs = [("grad_x", shape((count, part), BF16), vmem)]
@@ -1911,7 +1850,6 @@
     wide = pltpu.VMEM((step, width), F32)
     tall = pltpu.VMEM((step + 8, width), F32)
     eight = pltpu.VMEM((8, width), F32)
-    columns = pltpu.VMEM((width // 128, step, 128), F32)
     scratch = [
         ("gm_here", wide), ("both_here", pltpu.VMEM((step, 2 * width), F32)),
         ("conv_here", wide), ("r_here", wide), ("i_here", wide), ("state_here", wide),
@@ -1921,8 +1859,7 @@
         ("pull", pltpu.VMEM((count, 2 * width), BF16)),
         ("rates", pltpu.VMEM((step, 2 * width), BF16)),
         ("dots", pltpu.VMEM((step, 128), F32)),
-        ("padded", tall), ("before", tall), ("decay", columns), ("adjoint", columns),
-        ("coef", columns), ("dconv", tall), ("sums", pltpu.VMEM((8, 8, width), F32)),
+        ("padded", tall), ("before", tall), ("dconv", tall), ("sums", pltpu.VMEM((8, 8, width), F32)),
         ("dense_sum", pltpu.VMEM((width, 2 * width), F32)),
         ("flat", pltpu.VMEM((span + 16, 2 * width), F32)),
         ("gates", pltpu.VMEM((256, 2 * width), BF16)),
@@ -1976,9 +1913,9 @@
     now = segment[TAPS:]
     same = [(segment[TAPS - k : TAPS - k + count] == now).astype(F32) for k in range(1, TAPS)]
     blank = jnp.zeros((count,), F32)
-    columns = [same[0]] + same + [blank] * (LANES - TAPS)
-    live = now < row_lengths.shape[0]
-    return jnp.stack(columns, axis=1), live
+    live = (now < row_lengths.shape[0]).astype(F32)
+    columns = [same[0]] + same + [live] + [blank] * (LANES - TAPS - 1)
+    return jnp.stack(columns, axis=1)
 
 
 def dense_gates(gates, width):
@@ -2030,25 +1967,23 @@
         gates_shard = jnp.pad(gates_shard, ((0, 0), (0, 32 - span // 8), (0, 0)))
         gates_shard = gates_shard.reshape(256, 2 * width)
 
-    mask, live = make_masks(lengths[0], count)
+    mask = make_masks(lengths[0], count)
     mask_tail = jnp.concatenate([mask, jnp.zeros((8, LANES), F32)], axis=0)
     tail_masks = [mask_tail[c * step : (c + 1) * step + 8] for c in range(CHUNKS)]
-    live = jnp.broadcast_to(live[:, None], (count, LANES)).astype(F32)
     w_in, w_out, w_gate, dense, normed, both, conv, r, i, state, mixed, s1 = head(
         dp, mp, 4, inputs, gains, rnn_params, mask, in_shard, out_shard, gate, gates_shard, span
     )
     (
         output, gm, gbo, local, hidden, pulled, normed2, grad_y, grad_gate, grad_up, gain2,
     ) = middle(
-        dp, mp, 4, mixed, inputs, cotangent, live, gains, mine(gains), w_out,
+        dp, mp, 4, mixed, inputs, cotangent, mask, gains, w_out,
         w_gate, up, down,
     )
-    gain2 = jnp.sum(gain2, axis=0, keepdims=True)
     if dp == 8:
         rows = span // dp
         input_grad, grad_down, grad_out, grad_in, grad_gates, small = tail(
             mp, 4, span, (gm, both, conv, r, i, state), mask_tail, rnn_params, dense, w_in, normed,
-            grad_y, hidden, gbo, mixed, s1, inputs, local, gains, mine(gains), gain2,
+            grad_y, hidden, gbo, mixed, s1, inputs, local, gains, gain2,
         )
         grad_gates = grad_gates[:rows]
         grad_gains, grad_params = small[0:2], small[8:16, :width]
@@ -2092,6 +2027,7 @@
         grad_in = square_scatter(inner_rows(normed, pull).astype(BF16), "dp", dp)
         grad_gates = pair_scatter(grad_gates, "dp", dp)
         grad_params = line_sum(params_total, "dp", dp)
+        gain2 = jnp.sum(gain2, axis=0, keepdims=True)
         both_gains = jnp.concatenate([(gain1 / gains[0])[None], gain2])
         both_gains = line_sum(both_gains, "dp", dp)
         grad_gains = jnp.concatenate([line_sum(both_gains[:1], "mp", mp), both_gains[1:]])

time: 569 us -> 554 us (0.974)
  Pallas kernels: 533 us -> 522 us
where the time goes in v6:
time: 554 us; the launch traced here: 545 us
  Pallas kernels  522 us (94%)
  local copies, waits for them, and re-layouts  18 us (3%)
    pallas_call x1, Pallas kernels, middle(): pl.pallas_call(functools.partial(middle_kernel, dp, mp, chunks), in_specs...  319 us
    pallas_call x1, Pallas kernels, tail(): pl.pallas_call(functools.partial(tail_kernel, mp, tuple(tasks), tuple(nam...  109 us
    pallas_call x1, Pallas kernels, head(): pl.pallas_call(functools.partial(head_kernel, dp, mp, tuple(names)), in_s...  92.9 us
    unnamed x30, local copies, waits for them, and re-layouts  11.5 us

profile of v6, /device:TPU:0, one launch (start us, length us, event | category | flops | bytes accessed | tf_op | source)
XLA Modules:
  0.0 544.5 jit_solution(2476877981411458257)
XLA Ops:
  0.7 0.8 reduce-window.8
  1.5 0.1 convert_reduce_fusion
  1.6 0.1 compare_convert_fusion
  1.7 0.1 stack.40
  1.8 1.0 copy.46.refs_3_
  2.8 2.0 pad_maximum_fusion.refs_4_
  4.8 1.9 copy.45
  6.7 0.0 copy-done.9
  6.7 0.6 fusion.2.refs_7_
  7.3 92.9 %head.1 = (bf16[2048,1280]{1,0:T(8,128)(2,1)}, bf16[2048,640]{1,0:T(8,128)(2,1)}, bf16[2048,1536]{1,0:T(8,128)(2,1)}, bf16[640,1280]{1,0:T(8,128)(2,1)}, bf16[10...) custom-call(bf16[1024,512]{1,0:T(8,128)(2,1)} %refs_16_.1, ...), custom_call_target="tpu_custom_call" | custom-call | tf_op jit(solution)/shard_map/head/pallas_call | solution.py:973
  100.2 1.2 copy.47
  101.4 319.5 %middle.1 = (bf16[1024,512]{1,0:T(8,128)(2,1)}, f32[1024,640]{1,0:T(8,128)}, bf16[1024,2048]{1,0:T(8,128)(2,1)}, f32[1024,512]{1,0:T(8,128)}, bf16[1024,1536]{1,...) custom-call(bf16[1024,640]{1,0:T(8,128)(2,1)} %get-tuple-element.39., ...), custom_call_target="tpu_custom_call" | custom-call | tf_op jit(solution)/shard_map/middle/pallas_call | solution.py:1428
  420.9 0.8 concatenate.11.refs_6_
  421.7 109.3 %tail.1 = (bf16[1024,512]{1,0:T(8,128)(2,1)}, f32[256,1536]{1,0:T(8,128)}, f32[256,640]{1,0:T(8,128)}, f32[256,1280]{1,0:T(8,128)}, f32[32,1280]{1,0:T(8,128)}, /*index=5*/f32[16,2048]{1,0:T(8,128)}) custom-call(f32[1024,640]{1,0:T(8,128)} %get-tuple-element.43.refs_0_, f32[1024,1280]{1,0:T(8,128)} %get-tuple-element.44.refs_1_, ...), custom_call_target="tpu_custom_call" | custom-call | tf_op jit(solution)/shard_map/tail/pallas_call | solution.py:1895
  531.0 3.2 copy.51
  534.2 1.1 fusion.6
  535.3 1.1 copy.50
  536.4 0.7 fusion.7
  537.1 1.3 slice.38
  538.4 1.4 slice.37
  539.8 1.0 copy.56
  540.8 1.0 copy.57
  541.8 1.1 copy.58
  542.9 1.1 copy.59
  (25 shorter events, 0.1 us)
Async XLA Ops:
  0.6 6.0 %copy-start.10 = (bf16[20,640]{1,0:T(8,128)(2,1)S(1)}, bf16[20,640]{1,0:T(8,128)(2,1)}, u32[]{:S(2)}) copy-start(bf16[20,640]{1,0:T(8,128)(2,1)} %param.20) | copy-start | bytes 76804
  0.7 6.0 %copy-start.9 = (bf16[20,640]{1,0:T(8,128)(2,1)S(1)}, bf16[20,640]{1,0:T(8,128)(2,1)}, u32[]{:S(2)}) copy-start(bf16[20,640]{1,0:T(8,128)(2,1)} %param.21) | copy-start | bytes 76804
  2.8 97.5 %copy-start.6 = (bf16[1536,256]{1,0:T(8,128)(2,1)S(1)}, bf16[1536,256]{1,0:T(8,128)(2,1)}, u32[]{:S(2)}) copy-start(bf16[1536,256]{1,0:T(8,128)(2,1)} %param.25) | copy-start | bytes 2359300
  101.4 319.5 %copy-start = (f32[1024,8]{1,0:T(8,128)S(1)}, f32[1024,8]{1,0:T(8,128)}, u32[]{:S(2)}) copy-start(f32[1024,8]{1,0:T(8,128)} %copy.46.refs_3_) | copy-start | bytes 98308
  531.0 3.2 copy-start.3
  531.0 4.3 copy-start.7
  534.2 2.2 copy-start.8
  534.2 5.7 %copy-start.4 = (bf16[1024,512]{1,0:T(8,128)(2,1)S(1)}, bf16[1024,512]{1,0:T(8,128)(2,1)}, u32[]{:S(2)}) copy-start(bf16[1024,512]{1,0:T(8,128)(2,1)} %get-tuple-element.134) | copy-start | bytes 3145732
  535.3 6.5 %copy-start.2 = (f32[256,1536]{1,0:T(8,128)S(1)}, f32[256,1536]{1,0:T(8,128)}, u32[]{:S(2)}) copy-start(f32[256,1536]{1,0:T(8,128)} %get-tuple-element.142) | copy-start | bytes 4718596
  536.4 4.4 copy-start.5
  540.8 2.1 copy-start.1

commit v7 on v6

--- a/solution.py
+++ b/solution.py
@@ -578,14 +578,15 @@
 
 
 class Square:
-    def __init__(self, d, shard, whole, sent, came, own):
-        self.d, self.shard, self.whole = d, shard, whole
+    def __init__(self, d, shard, whole, sent, came, own, axis=0):
+        self.d, self.shard, self.whole, self.axis = d, shard, whole, axis
         self.sent, self.came, self.own = sent, came, own
         self.core, self.by_core, self.by_x, self.by_y = partners(d)
 
     def rows(self, d):
-        count = self.shard.shape[0]
-        return self.whole.at[pl.ds(pl.multiple_of(d * count, count), count), :]
+        count = self.shard.shape[self.axis]
+        window = pl.ds(pl.multiple_of(d * count, count), count)
+        return self.whole.at[:, window] if self.axis else self.whole.at[window, :]
 
     def copy(self, src, origin, target, sent, came):
         return pltpu.make_async_remote_copy(
@@ -776,23 +777,26 @@
     pl.semaphore_wait(barrier, count)
 
     wholes = (
-        ("gates_shard", ref["gates_here"]), ("in_shard", w_in), ("out_shard", ref["w_out"]),
-        ("gate_shard", ref["w_gate"]),
+        ("gates_shard", ref["gates_here"], 0),
+        ("rnn_in", w_in.at[:, pl.ds(0, width)], 0),
+        ("branch_gate", w_in.at[:, pl.ds(width, width)], 0),
+        ("rnn_out", ref["w_out"], 1),
+        ("mlp_gate", ref["w_gate"], 0),
     )
     if square:
         squares = [
             Square(
                 d, ref[name], whole, ref["square_sent"].at[k], ref["square_came"].at[k],
-                ref["square_own"].at[k],
+                ref["square_own"].at[k], axis,
             )
-            for k, (name, whole) in enumerate(wholes)
+            for k, (name, whole, axis) in enumerate(wholes)
         ]
-        for item in squares[:2]:
+        for item in squares[:3]:
             item.start()
     else:
         loads = [
             pltpu.make_async_copy(ref[name], whole, ref["square_own"].at[k])
-            for k, (name, whole) in enumerate(wholes)
+            for k, (name, whole, _) in enumerate(wholes)
         ]
         for item in loads:
             item.start()
@@ -874,11 +878,11 @@
         if s == 1 and chunks > 2:
             begin(2)
     if square:
-        for item in squares[:2]:
+        for item in squares[:3]:
             item.step_one()
-        for item in squares[2:]:
+        for item in squares[3:]:
             item.start()
-        for item in squares[:2]:
+        for item in squares[:3]:
             item.step_two()
     gather.finish(0)
     for c in range(chunks):
@@ -886,7 +890,7 @@
             gather.step(c + 1, 1)
         if c == 0:
             if square:
-                for item in squares[:2]:
+                for item in squares[:3]:
                     item.finish()
             else:
                 for item in loads:
@@ -902,19 +906,19 @@
             begin(c + 3)
         compute(c)
         if square and (c + 1) * 4 == chunks:
-            squares[2].step_one()
+            squares[3].step_one()
         if square and (c + 1) * 2 == chunks:
-            squares[2].step_two()
-            squares[3].step_one()
+            squares[3].step_two()
+            squares[4].step_one()
         if square and (c + 1) * 4 == 3 * chunks:
-            squares[3].step_two()
+            squares[4].step_two()
         if c + 1 < chunks:
             for s in range(2, mp - 1):
                 gather.step(c + 1, s)
             gather.finish(c + 1)
     if square:
-        squares[2].finish()
         squares[3].finish()
+        squares[4].finish()
         for item in squares:
             item.drain()
     for copy in pass_on:
@@ -927,7 +931,8 @@
 
 
 def head(
-    dp, mp, chunks, x, gains, params, mask, in_shard, out_shard, gate_shard, gates_shard, span
+    dp, mp, chunks, x, gains, params, mask, rnn_in, branch_gate, rnn_out, mlp_gate, gates_shard,
+    span,
 ):
     count, part = x.shape
     features, width = part * mp, params.shape[1]
@@ -936,13 +941,13 @@
     any_, vmem = pl.BlockSpec(memory_space=pl.ANY), pl.BlockSpec(memory_space=pltpu.VMEM)
     ins = [
         ("x", x, any_), ("gains", gains, vmem), ("params", params, vmem), ("mask", mask, vmem),
-        ("in_shard", in_shard, any_), ("out_shard", out_shard, any_),
-        ("gate_shard", gate_shard, any_), ("gates_shard", gates_shard, any_),
+        ("rnn_in", rnn_in, any_), ("branch_gate", branch_gate, any_), ("rnn_out", rnn_out, any_),
+        ("mlp_gate", mlp_gate, any_), ("gates_shard", gates_shard, any_),
     ]
-    gate_width = gate_shard.shape[1]
+    gate_width = mlp_gate.shape[1]
     shape = jax.ShapeDtypeStruct
     outs = [
-        ("w_in", shape((features, 2 * width), BF16)), ("w_out", shape((features, width), BF16)),
+        ("w_in", shape((features, 2 * width), BF16)), ("w_out", shape((width, features), BF16)),
         ("w_gate", shape((features, gate_width), BF16)), ("dense", shape((width, 2 * width), BF16)), ("norm_out", shape((count, features), BF16)),
         ("both_out", shape((count, 2 * width), F32)), ("conv_out", shape((count, width), F32)),
         ("r_out", shape((count, width), F32)), ("i_out", shape((count, width), F32)),
@@ -966,7 +971,7 @@
         ("padded", pltpu.VMEM((step + 8, width), F32)),
         ("high", pltpu.VMEM((step, width), BF16)), ("low", pltpu.VMEM((step, width), BF16)),
         ("spread_sent", dma((chunks, 2 * mp))), ("spread_came", dma((chunks, mp))),
-        ("square_sent", dma((4, 8))), ("square_came", dma((4, 8))), ("square_own", dma((4,))),
+        ("square_sent", dma((5, 8))), ("square_came", dma((5, 8))), ("square_own", dma((5,))),
         ("load_sem", dma((chunks,))), ("store_sem", dma((2, 8))), ("pass_sem", dma((2,))),
     ]
     names = [i[0] for i in ins] + [o[0] for o in outs] + [k[0] for k in scratch]
@@ -984,23 +989,23 @@
 
 
 MIDDLE_ORDER = (
-    ("d", 0, 0), ("A", 0, 0), ("d", 0, 1), ("d", 1, 0), ("a", 1, 0), ("d", 2, 0), ("a", 2, 0),
-    ("d", 0, 2), ("J", 0, 0), ("e", 0, 0), ("A", 0, 1), ("e", 1, 0), ("d", 1, 2), ("e", 2, 0),
-    ("d", 3, 0), ("S", 1, 0), ("a", 1, 1), ("a", 2, 1), ("d", 2, 2), ("d", 1, 1), ("d", 0, 3),
-    ("e", 3, 0), ("S", 2, 0), ("A", 0, 2), ("d", 2, 1), ("S", 3, 0), ("d", 1, 3), ("J", 0, 1),
-    ("e", 0, 1), ("a", 1, 2), ("H", 0, 0), ("a", 2, 2), ("e", 1, 1), ("G", 0, 0), ("O", 0, 0),
-    ("c", 1, 0), ("e", 2, 1), ("J", 0, 2), ("d", 2, 3), ("d", 3, 1), ("d", 3, 2), ("e", 3, 1),
-    ("e", 0, 2), ("b", 1, 0), ("A", 0, 3), ("c", 2, 0), ("H", 0, 1), ("e", 1, 2), ("K", 0, 0),
-    ("G", 0, 1), ("a", 1, 3), ("e", 2, 2), ("b", 2, 0), ("f", 1, 0), ("O", 0, 1), ("e", 3, 2),
-    ("a", 2, 3), ("c", 1, 1), ("H", 0, 2), ("f", 2, 0), ("c", 2, 1), ("b", 1, 1), ("J", 0, 3),
-    ("d", 3, 3), ("Y", 0, 0), ("B", 0, 0), ("e", 0, 3), ("K", 0, 1), ("b", 2, 1), ("G", 0, 2),
-    ("f", 1, 1), ("c", 1, 2), ("e", 1, 3), ("f", 2, 1), ("Y", 0, 1), ("c", 2, 2), ("B", 0, 1),
-    ("e", 2, 3), ("K", 0, 2), ("O", 0, 2), ("f", 1, 2), ("e", 3, 3), ("H", 0, 3), ("f", 2, 2),
-    ("G", 0, 3), ("b", 1, 2), ("B", 0, 2), ("O", 0, 3), ("c", 1, 3), ("D", 0, 0), ("D", 0, 1),
-    ("c", 2, 3), ("W", 0, 0), ("D", 0, 2), ("Z", 0, 0), ("W", 0, 1), ("K", 0, 3), ("D", 0, 3),
-    ("W", 0, 2), ("f", 1, 3), ("Z", 0, 1), ("b", 2, 2), ("b", 1, 3), ("W", 0, 3), ("D", 0, 4),
-    ("f", 2, 3), ("D", 0, 5), ("W", 0, 4), ("Z", 0, 2), ("W", 0, 5), ("b", 2, 3), ("Y", 0, 2),
-    ("Z", 0, 3), ("B", 0, 3), ("Z", 0, 4), ("Y", 0, 3), ("Z", 0, 5),
+    ("d", 0, 0), ("d", 0, 1), ("d", 1, 1), ("A", 0, 0), ("a", 1, 0), ("d", 1, 0), ("a", 2, 0),
+    ("A", 0, 1), ("d", 2, 0), ("d", 2, 1), ("a", 1, 1), ("J", 0, 0), ("S", 1, 0), ("e", 0, 0),
+    ("a", 2, 1), ("S", 2, 0), ("e", 1, 0), ("e", 2, 0), ("d", 0, 2), ("d", 0, 3), ("J", 0, 1),
+    ("S", 3, 0), ("e", 0, 1), ("e", 3, 0), ("d", 1, 2), ("d", 1, 3), ("A", 0, 2), ("d", 3, 0),
+    ("a", 1, 2), ("e", 1, 1), ("H", 0, 0), ("G", 0, 0), ("d", 2, 2), ("a", 2, 2), ("e", 2, 1),
+    ("c", 1, 0), ("d", 2, 3), ("O", 0, 0), ("b", 1, 0), ("J", 0, 2), ("e", 3, 1), ("e", 0, 2),
+    ("d", 3, 1), ("c", 2, 0), ("A", 0, 3), ("d", 3, 3), ("H", 0, 1), ("e", 1, 2), ("a", 1, 3),
+    ("K", 0, 0), ("G", 0, 1), ("a", 2, 3), ("f", 1, 0), ("c", 1, 1), ("e", 2, 2), ("e", 3, 2),
+    ("J", 0, 3), ("e", 0, 3), ("O", 0, 1), ("f", 2, 0), ("d", 3, 2), ("b", 2, 0), ("H", 0, 2),
+    ("c", 2, 1), ("b", 1, 1), ("Y", 0, 0), ("e", 1, 3), ("B", 0, 0), ("K", 0, 1), ("e", 2, 3),
+    ("G", 0, 2), ("b", 2, 1), ("e", 3, 3), ("f", 1, 1), ("O", 0, 2), ("c", 1, 2), ("H", 0, 3),
+    ("Y", 0, 1), ("f", 2, 1), ("c", 2, 2), ("B", 0, 1), ("G", 0, 3), ("K", 0, 2), ("b", 1, 2),
+    ("O", 0, 3), ("D", 0, 0), ("c", 1, 3), ("D", 0, 1), ("c", 2, 3), ("W", 0, 0), ("D", 0, 2),
+    ("Z", 0, 0), ("f", 1, 2), ("W", 0, 1), ("b", 2, 2), ("D", 0, 3), ("f", 2, 2), ("K", 0, 3),
+    ("Z", 0, 1), ("b", 1, 3), ("W", 0, 2), ("D", 0, 4), ("W", 0, 3), ("Z", 0, 2), ("f", 1, 3),
+    ("W", 0, 4), ("D", 0, 5), ("Y", 0, 2), ("f", 2, 3), ("Z", 0, 3), ("B", 0, 2), ("b", 2, 3),
+    ("W", 0, 5), ("B", 0, 3), ("Z", 0, 4), ("Z", 0, 5), ("Y", 0, 3),
 )
 
 
@@ -1015,11 +1020,12 @@
         norm, hidden, pulled, gbo, gm, local, out,
         spread_sent, spread_came, fold_sent, fold_right, fold_left,
         square_sent, square_came, square_own, load_sem, store_sem,
-        stage, free_sem, task_sent, task_came, left_sem, right_sem, stage_sem,
+        stage, free_sem, task_sent, task_came, left_sem, right_sem, stage_sem, slot_right,
+        slot_left,
     ) = refs
     step, part = x_ref.shape[0] // chunks, x_ref.shape[1]
     features = part * mp
-    hidden_width = w_down.shape[1]
+    hidden_width = w_down.shape[0]
     z, d = lax.axis_index("mp"), lax.axis_index("dp")
     square = dp == 8
     up_half = w_up.at[:, pl.ds(hidden_width, hidden_width)]
@@ -1059,7 +1065,7 @@
     if square:
         squares = [
             Square(
-                d, shard, whole, square_sent.at[k], square_came.at[k], square_own.at[k]
+                d, shard, whole, square_sent.at[k], square_came.at[k], square_own.at[k], k
             )
             for k, (shard, whole) in enumerate(((up_ref, up_half), (down_ref, w_down)))
         ]
@@ -1092,10 +1098,14 @@
     gain_ref[...] = jnp.zeros_like(gain_ref)
     tiles = step // TILE
 
-    def fill(fold, slot, left, weights):
+    def fill(fold, slot, left, weights, columns=True):
         def body(j):
-            rows = pl.ds(pl.multiple_of(j * part, part), part)
-            fold.parts[slot, j] = inner_cols(left, weights[rows, :]).astype(BF16)
+            near = pl.ds(pl.multiple_of(j * part, part), part)
+            if columns:
+                value = matmul(left, weights[:, near])
+            else:
+                value = inner_cols(left, weights[near, :])
+            fold.parts[slot, j] = value.astype(BF16)
 
         tile_loop(mp, body)
 
@@ -1174,7 +1184,7 @@
             gate = matmul(norm[...], w_up[:, near])
             up = matmul(norm[...], w_up[:, off])
             grad = sum(
-                matmul(cots[c, j], w_down[block_cols(j), near]) for j in range(mp)
+                inner_cols(cots[c, j], w_down[near, block_cols(j)]) for j in range(mp)
             )
             value, slope = gelu_and_slope(gate)
             hidden[:, near] = (value * up).astype(BF16)
@@ -1189,7 +1199,7 @@
         slot = c % 2
         if c > 1:
             rs3.drain(slot)
-        fill(rs3, slot, pulled[...], w_up)
+        fill(rs3, slot, pulled[...], w_up, False)
         rs3.start(slot)
         if square and c == chunks - 1:
             for item in squares:
@@ -1204,6 +1214,16 @@
         if c > 1:
             rs2.drain(slot)
         fill(rs2, slot, hidden[...], w_down)
+        if c > 1:
+
+            @pl.when(z < mp - 1)
+            def _():
+                pl.semaphore_wait(slot_right.at[slot], 1)
+
+            @pl.when(z > 0)
+            def _():
+                pl.semaphore_wait(slot_left.at[slot], 1)
+
         rs2.start(slot)
 
     def gather_grad(c):
@@ -1252,7 +1272,7 @@
             )
 
         tile_loop(tiles, body)
-        gm[...] = matmul(gbo[...], wout_ref[...])
+        gm[...] = inner_cols(gbo[...], wout_ref[...])
         store(gbo, gbo_ref, c, 3).start()
         store(local, local_ref, c, 4).start()
         store(gm, gm_ref, c, 5).start()
@@ -1267,6 +1287,21 @@
             out[rows, :] = (mid_mine[c, rows, :] + rs2.total(c % 2, rows)).astype(BF16)
 
         tile_loop(tiles, body)
+        if c + 2 < chunks:
+            slot = c % 2
+
+            @pl.when(z > 0)
+            def _():
+                pl.semaphore_signal(
+                    slot_right.at[slot], inc=1, device_id={"mp": z - 1}, device_id_type=MESH
+                )
+
+            @pl.when(z < mp - 1)
+            def _():
+                pl.semaphore_signal(
+                    slot_left.at[slot], inc=1, device_id={"mp": z + 1}, device_id_type=MESH
+                )
+
         store(out, output_ref, c, 6).start()
 
     own = features // 8
@@ -1413,7 +1448,7 @@
 
 def middle(dp, mp, chunks, mixed, inputs, cotangent, live, gains, w_out, gate, up, down):
     count, part = inputs.shape
-    width, hidden_width = mixed.shape[1], down.shape[1]
+    width, hidden_width = mixed.shape[1], down.shape[0]
     step, features = count // chunks, part * mp
 
     def fold_buffers():
@@ -1444,7 +1479,7 @@
         ),
         scratch_shapes=[
             pltpu.VMEM((features, 2 * hidden_width), BF16),
-            pltpu.VMEM((features, hidden_width), BF16),
+            pltpu.VMEM((hidden_width, features), BF16),
             pltpu.VMEM((chunks, mp, step, part), BF16),
             pltpu.VMEM((chunks, mp, step, part), BF16),
             pltpu.VMEM((chunks, mp, step, part), BF16),
@@ -1477,6 +1512,8 @@
             dma((chunks, mp)),
             dma((2, chunks)),
             dma,
+            pltpu.SemaphoreType.REGULAR((2,)),
+            pltpu.SemaphoreType.REGULAR((2,)),
         ],
         compiler_params=pltpu.CompilerParams(
             collective_id=0, has_side_effects=True, vmem_limit_bytes=62 * 1024 * 1024
@@ -1954,15 +1991,14 @@
     def mine(values):
         return lax.dynamic_slice_in_dim(values, spot, part, values.ndim - 1)
 
-    in_shard = jnp.concatenate([rnn_in, branch_gate], axis=1)
-    out_shard = rnn_out.T
     gates_shard = jnp.concatenate([recur_gate, input_gate], axis=1)
-    gate, up, down = mlp_gate, mlp_up, mlp_down.T
     if dp == 8:
         gates_shard = jnp.pad(gates_shard, ((0, 32 - span // 8), (0, 0)))
     else:
-        in_shard, out_shard = square_gather(in_shard, "dp", dp), square_gather(out_shard, "dp", dp)
-        gate, up, down = [square_gather(w, "dp", dp) for w in (gate, up, down)]
+        rnn_in, branch_gate, mlp_gate, mlp_up = [
+            square_gather(w, "dp", dp) for w in (rnn_in, branch_gate, mlp_gate, mlp_up)
+        ]
+        rnn_out, mlp_down = [square_gather(w.T, "dp", dp).T for w in (rnn_out, mlp_down)]
         gates_shard = pair_gather(gates_shard, "dp", dp).reshape(8, span // 8, 2 * width)
         gates_shard = jnp.pad(gates_shard, ((0, 0), (0, 32 - span // 8), (0, 0)))
         gates_shard = gates_shard.reshape(256, 2 * width)
@@ -1971,13 +2007,14 @@
     mask_tail = jnp.concatenate([mask, jnp.zeros((8, LANES), F32)], axis=0)
     tail_masks = [mask_tail[c * step : (c + 1) * step + 8] for c in range(CHUNKS)]
     w_in, w_out, w_gate, dense, normed, both, conv, r, i, state, mixed, s1 = head(
-        dp, mp, 4, inputs, gains, rnn_params, mask, in_shard, out_shard, gate, gates_shard, span
+        dp, mp, 4, inputs, gains, rnn_params, mask, rnn_in, branch_gate, rnn_out, mlp_gate,
+        gates_shard, span,
     )
     (
         output, gm, gbo, local, hidden, pulled, normed2, grad_y, grad_gate, grad_up, gain2,
     ) = middle(
         dp, mp, 4, mixed, inputs, cotangent, mask, gains, w_out,
-        w_gate, up, down,
+        w_gate, mlp_up, mlp_down,
     )
     if dp == 8:
         rows = span // dp

time: 554 us -> 531 us (0.958)
  Pallas kernels: 522 us -> 503 us
    pallas_call x1, Pallas kernels: 319 us -> 301 us  [middle(): pl.pallas_call(functools.partial(middle_kernel, dp, mp, chunks), in_specs...]
    unnamed x30 -> x22, local copies, waits for them, and re-layouts: 11.5 us -> 8.49 us
where the time goes in v7:
time: 531 us; the launch traced here: 521 us
  Pallas kernels  503 us (95%)
  local copies, waits for them, and re-layouts  15 us (3%)
    pallas_call x1, Pallas kernels, middle(): pl.pallas_call(functools.partial(middle_kernel, dp, mp, chunks), in_specs...  301 us
    pallas_call x1, Pallas kernels, tail(): pl.pallas_call(functools.partial(tail_kernel, mp, tuple(tasks), tuple(nam...  109 us
    pallas_call x1, Pallas kernels, head(): pl.pallas_call(functools.partial(head_kernel, dp, mp, tuple(names)), in_s...  93.5 us

profile of v7, /device:TPU:0, one launch (start us, length us, event | category | flops | bytes accessed | tf_op | source)
XLA Modules:
  0.0 521.4 jit_solution(5083268621398615768)
XLA Ops:
  0.7 0.8 reduce-window.8
  1.5 0.1 convert_reduce_fusion
  1.6 0.1 compare_convert_fusion
  1.7 0.1 stack.40
  1.7 1.0 copy.39.refs_3_
  2.7 1.4 fusion.2.refs_8_
  4.1 93.5 %head.1 = (bf16[2048,1280]{1,0:T(8,128)(2,1)}, bf16[640,2048]{1,0:T(8,128)(2,1)}, bf16[2048,1536]{1,0:T(8,128)(2,1)}, bf16[640,1280]{1,0:T(8,128)(2,1)}, bf16[10...) custom-call(bf16[1024,512]{1,0:T(8,128)(2,1)} %refs_16_.1, ...), custom_call_target="tpu_custom_call" | custom-call | tf_op jit(solution)/shard_map/head/pallas_call | solution.py:978
  97.6 0.0 copy-start
  97.6 300.6 %middle.1 = (bf16[1024,512]{1,0:T(8,128)(2,1)}, f32[1024,640]{1,0:T(8,128)}, bf16[1024,2048]{1,0:T(8,128)(2,1)}, f32[1024,512]{1,0:T(8,128)}, bf16[1024,1536]{1,...) custom-call(bf16[1024,640]{1,0:T(8,128)(2,1)} %get-tuple-element.39., ...), custom_call_target="tpu_custom_call" | custom-call | tf_op jit(solution)/shard_map/middle/pallas_call | solution.py:1463
  398.3 0.0 copy-done
  398.3 0.8 concatenate.7.refs_6_
  399.1 109.0 %tail.1 = (bf16[1024,512]{1,0:T(8,128)(2,1)}, f32[256,1536]{1,0:T(8,128)}, f32[256,640]{1,0:T(8,128)}, f32[256,1280]{1,0:T(8,128)}, f32[32,1280]{1,0:T(8,128)}, /*index=5*/f32[16,2048]{1,0:T(8,128)}) custom-call(f32[1024,640]{1,0:T(8,128)} %get-tuple-element.43.refs_0_, f32[1024,1280]{1,0:T(8,128)} %get-tuple-element.44.refs_1_, ...), custom_call_target="tpu_custom_call" | custom-call | tf_op jit(solution)/shard_map/tail/pallas_call | solution.py:1932
  508.1 3.2 copy.43
  511.3 0.0 copy-done.3
  511.3 1.1 fusion.6
  512.4 0.0 copy-done.6
  512.4 1.1 copy.42
  513.5 0.7 fusion.7
  514.2 1.3 slice.38
  515.5 1.4 slice.37
  516.9 1.0 copy.48
  517.9 1.0 copy.49
  518.9 1.1 copy.50
  520.0 1.1 copy.51
  (16 shorter events, 0.0 us)
Async XLA Ops:
  97.6 300.7 %copy-start = (f32[1024,8]{1,0:T(8,128)S(1)}, f32[1024,8]{1,0:T(8,128)}, u32[]{:S(2)}) copy-start(f32[1024,8]{1,0:T(8,128)} %copy.39.refs_3_) | copy-start | bytes 98308
  508.1 3.2 copy-start.3
  508.1 4.3 copy-start.6
  511.3 2.2 copy-start.7
  511.3 5.7 %copy-start.4 = (bf16[1024,512]{1,0:T(8,128)(2,1)S(1)}, bf16[1024,512]{1,0:T(8,128)(2,1)}, u32[]{:S(2)}) copy-start(bf16[1024,512]{1,0:T(8,128)(2,1)} %get-tuple-element.134) | copy-start | bytes 3145732
  512.4 6.5 %copy-start.2 = (f32[256,1536]{1,0:T(8,128)S(1)}, f32[256,1536]{1,0:T(8,128)}, u32[]{:S(2)}) copy-start(f32[256,1536]{1,0:T(8,128)} %get-tuple-element.142) | copy-start | bytes 4718596
  513.5 4.4 copy-start.5
  517.9 2.1 copy-start.1

commit v8 on v7

--- a/solution.py
+++ b/solution.py
@@ -14,6 +14,7 @@
 LANES = 8
 CHUNKS = 1
 TILE = 32
+RNN_TILE = 64
 F32 = jnp.float32
 BF16 = jnp.bfloat16
 VMEM_BYTES = 56 * 1024 * 1024
@@ -196,21 +197,21 @@
     padded, high, low,
 ):
     count, width = conv_ref.shape
-    tiles = count // TILE
+    tiles = count // RNN_TILE
     padded[0:8, :] = halo_ref[...]
     padded[8:, :] = both_ref[:, 0:width]
 
     def convolve(t):
-        span = padded[pl.ds(pl.multiple_of(t * TILE, TILE), TILE + 8), :]
-        mask = mask_ref[rows_at(t, TILE), :]
+        span = padded[pl.ds(pl.multiple_of(t * RNN_TILE, RNN_TILE), RNN_TILE + 8), :]
+        mask = mask_ref[rows_at(t, RNN_TILE), :]
         conv = params_ref[0:1, :] * span[8:, :] + params_ref[TAPS : TAPS + 1, :]
         for k in range(1, TAPS):
-            moved = span[8 - k : 8 - k + TILE, :]
+            moved = span[8 - k : 8 - k + RNN_TILE, :]
             conv = conv + params_ref[k : k + 1, :] * (moved * mask[:, k : k + 1])
-        conv_ref[rows_at(t, TILE), :] = conv
+        conv_ref[rows_at(t, RNN_TILE), :] = conv
         top = conv.astype(BF16)
-        high[rows_at(t, TILE), :] = top
-        low[rows_at(t, TILE), :] = (conv - top.astype(F32)).astype(BF16)
+        high[rows_at(t, RNN_TILE), :] = top
+        low[rows_at(t, RNN_TILE), :] = (conv - top.astype(F32)).astype(BF16)
 
     tile_loop(tiles, convolve)
 
@@ -231,7 +232,7 @@
     place = lax.broadcasted_iota(jnp.int32, (8, width), 0)
 
     def advance(t, carry):
-        rows = rows_at(t, TILE)
+        rows = rows_at(t, RNN_TILE)
         keep = mask_ref[rows, :][:, 0:1]
         r = jax.nn.sigmoid(r_ref[rows, :] + params_ref[TAPS + 1 : TAPS + 2, :])
         i = jax.nn.sigmoid(i_ref[rows, :] + params_ref[TAPS + 2 : TAPS + 3, :])
@@ -243,7 +244,7 @@
         r_ref[rows, :] = r
         i_ref[rows, :] = i
         states = []
-        for g in range(0, TILE, 8):
+        for g in range(0, RNN_TILE, 8):
             a, held = decay[g : g + 8, :], drive[g : g + 8, :]
             for s in (1, 2, 4):
                 inside = place >= s
@@ -292,7 +293,7 @@
     padded, before, dconv, sums,
 ):
     count, width = conv_ref.shape
-    tiles = count // TILE
+    tiles = count // RNN_TILE
     padded[0:8, :] = halo_ref[...]
     padded[8:, :] = both_ref[:, 0:width]
     before[0:8, :] = start_ref[...]
@@ -307,8 +308,8 @@
 
     def chain(t, carry):
         later, later_decay = carry
-        base = pl.multiple_of((tiles - 1 - t) * TILE, TILE)
-        rows = pl.ds(base, TILE)
+        base = pl.multiple_of((tiles - 1 - t) * RNN_TILE, RNN_TILE)
+        rows = pl.ds(base, RNN_TILE)
         keep = mask_ref[rows, :][:, 0:1]
         gm = gm_ref[rows, :]
         value, slope = gelu_and_slope(both_ref[rows, width:])
@@ -317,7 +318,7 @@
         r, i, conv = r_ref[rows, :], i_ref[rows, :], conv_ref[rows, :]
         fall = jnp.exp(-strength * r) * keep
         adjoints = []
-        for g in reversed(range(0, TILE, 8)):
+        for g in reversed(range(0, RNN_TILE, 8)):
             a = fall[g : g + 8, :]
             ahead = jnp.where(place == 7, later_decay, pltpu.roll(a, 7, 0))
             held = given[g : g + 8, :]
@@ -330,7 +331,7 @@
             later_decay = jnp.broadcast_to(a[0:1, :], (8, width))
             adjoints.append(held)
         a = jnp.concatenate(adjoints[::-1], axis=0)
-        prior = before[pl.ds(base, TILE + 8), :][7 : 7 + TILE, :]
+        prior = before[pl.ds(base, RNN_TILE + 8), :][7 : 7 + RNN_TILE, :]
         room = one_less_exp(-2.0 * strength * r)
         bound = jnp.maximum(room, ROOT_FLOOR)
         inverse = lax.rsqrt(bound)
@@ -369,25 +370,25 @@
     tail_out_ref[...] = dconv[0:8, :]
 
     def unconvolve(t):
-        base = pl.multiple_of(t * TILE, TILE)
-        rows = pl.ds(base, TILE)
-        span = dconv[pl.ds(base, TILE + 8), :]
-        mask = mask_ref[pl.ds(base, TILE + 8), :]
-        source = padded[pl.ds(base, TILE + 8), :]
-        here = span[0:TILE, :]
+        base = pl.multiple_of(t * RNN_TILE, RNN_TILE)
+        rows = pl.ds(base, RNN_TILE)
+        span = dconv[pl.ds(base, RNN_TILE + 8), :]
+        mask = mask_ref[pl.ds(base, RNN_TILE + 8), :]
+        source = padded[pl.ds(base, RNN_TILE + 8), :]
+        here = span[0:RNN_TILE, :]
         out = params_ref[0:1, :] * here
         sums[0] += fold(here * source[8:, :])
         sums[4] += fold(here)
         for k in range(1, TAPS):
             kept = span * mask[:, k : k + 1]
-            out = out + params_ref[k : k + 1, :] * kept[k : k + TILE, :]
-            sums[k] += fold(kept[0:TILE, :] * source[8 - k : 8 - k + TILE, :])
+            out = out + params_ref[k : k + 1, :] * kept[k : k + RNN_TILE, :]
+            sums[k] += fold(kept[0:RNN_TILE, :] * source[8 - k : 8 - k + RNN_TILE, :])
         grads_ref[rows, 0:width] = out.astype(BF16)
         dot = jnp.sum(
             out * source[8:, :] + grads_ref[rows, width:].astype(F32) * both_ref[rows, width:],
             axis=1, keepdims=True,
         )
-        dots_ref[rows, :] = jnp.broadcast_to(dot, (TILE, 128))
+        dots_ref[rows, :] = jnp.broadcast_to(dot, (RNN_TILE, 128))
 
     tile_loop(tiles, unconvolve)
     for k in range(8):
@@ -710,12 +711,12 @@
         held = self.held(self.second_at)
 
         def body(t):
-            rows = rows_at(t, 16)
+            rows = rows_at(t, 32)
             held[rows, :] = (
                 held[rows, :].astype(F32) + self.far_in[rows, :].astype(F32)
             ).astype(BF16)
 
-        tile_loop(self.count // 16, body)
+        tile_loop(self.count // 32, body)
         self.to_second().start()
 
     def finish(self, target):
@@ -724,14 +725,14 @@
         held = self.held(0)
 
         def body(t):
-            rows = rows_at(t, 16)
+            rows = rows_at(t, 32)
             target[rows, :] = (
                 held[rows, :].astype(F32)
                 + self.first_in[rows, :].astype(F32)
                 + self.second_in[rows, :].astype(F32)
             )
 
-        tile_loop(self.count // 16, body)
+        tile_loop(self.count // 32, body)
 
     def drain(self):
         self.to_far().wait_send()
@@ -1635,8 +1636,7 @@
             ref["halo"][...] = jnp.zeros_like(ref["halo"])
             ref["start"][...] = jnp.zeros_like(ref["start"])
         if c == last:
-            for copy in whole_copies:
-                copy.wait()
+            whole_copies[0].wait()
         rnn_backward_kernel(
             ref["gm_here"], ref["both_here"], ref["halo"], ref["start"], ref["conv_here"],
             ref["r_here"], ref["i_here"], ref["state_here"],
@@ -1655,6 +1655,7 @@
             turned = jnp.transpose(ref["dots"][q * 128 : (q + 1) * 128, :])
             ref["dots_row"][c, :, q * 128 : (q + 1) * 128] = turned[0:8, :]
         if c == last:
+            whole_copies[1].wait()
             pl.semaphore_wait(barrier, jnp.where((z > 0) & (z < mp - 1), 6, 5))
         dots_copy(c, 0).start()
         norm_copy(c).wait()
@@ -1790,6 +1791,9 @@
         small[0:rows, :] += small_in[k, 0:rows, :]
         if k < 4:
             small_copy(k + 1).start()
+        else:
+            ref["grad_gains"][...] = small[0:2, :]
+            ref["grad_params"][...] = small[8:16, 0:width]
 
     def gate_blocks():
         flat, gates = ref["flat"], ref["gates"]
@@ -1883,7 +1887,8 @@
     outs = [("grad_x", shape((count, part), BF16), vmem)]
     for name, columns in widths.items():
         outs.append(("grad_" + name, shape((heights[name], columns), F32), any_))
-    outs.append(("small", shape((16, features), F32), vmem))
+    outs.append(("grad_gains", shape((2, features), F32), vmem))
+    outs.append(("grad_params", shape((8, width), F32), vmem))
     wide = pltpu.VMEM((step, width), F32)
     tall = pltpu.VMEM((step + 8, width), F32)
     eight = pltpu.VMEM((8, width), F32)
@@ -1914,6 +1919,7 @@
         ("dots_row", pltpu.VMEM((chunks, 8, step), F32)),
         ("dots_in", pltpu.VMEM((chunks, 2, 8, step), F32)),
         ("dots_col", pltpu.VMEM((step, 128), F32)),
+        ("small", pltpu.VMEM((16, features), F32)),
         ("small_in", pltpu.VMEM((5, 16, features), F32)),
         ("chunk_sem", dma((8,))), ("norm_sem", dma), ("left_sem", dma), ("right_sem", dma((2,))),
         ("end_sem", dma((3,))), ("whole_sem", dma((2,))), ("store_sem", dma((2,))),
@@ -2018,12 +2024,11 @@
     )
     if dp == 8:
         rows = span // dp
-        input_grad, grad_down, grad_out, grad_in, grad_gates, small = tail(
+        input_grad, grad_down, grad_out, grad_in, grad_gates, grad_gains, grad_params = tail(
             mp, 4, span, (gm, both, conv, r, i, state), mask_tail, rnn_params, dense, w_in, normed,
             grad_y, hidden, gbo, mixed, s1, inputs, local, gains, gain2,
         )
         grad_gates = grad_gates[:rows]
-        grad_gains, grad_params = small[0:2], small[8:16, :width]
     else:
         blank = jnp.zeros((8, width), F32)
         back, tail_rows = blank, blank

time: 531 us -> 527 us (level)
  no operation moved by 1% of the time
where the time goes in v8:
time: 527 us; the launch traced here: 518 us
  Pallas kernels  501 us (95%)
  local copies, waits for them, and re-layouts  13.4 us (3%)
    pallas_call x1, Pallas kernels, middle(): pl.pallas_call(functools.partial(middle_kernel, dp, mp, chunks), in_specs...  301 us
    pallas_call x1, Pallas kernels, tail(): pl.pallas_call(functools.partial(tail_kernel, mp, tuple(tasks), tuple(nam...  106 us
    pallas_call x1, Pallas kernels, head(): pl.pallas_call(functools.partial(head_kernel, dp, mp, tuple(names)), in_s...  93.3 us

profile of v8, /device:TPU:0, one launch (start us, length us, event | category | flops | bytes accessed | tf_op | source)
XLA Modules:
  0.0 517.7 jit_solution(14207645554992933052)
XLA Ops:
  0.7 0.8 reduce-window.8
  1.5 0.1 convert_reduce_fusion
  1.6 0.1 compare_convert_fusion
  1.7 0.1 stack.40
  1.7 1.0 copy.39.refs_3_
  2.7 1.4 fusion.2.refs_8_
  4.1 93.3 %head.1 = (bf16[2048,1280]{1,0:T(8,128)(2,1)}, bf16[640,2048]{1,0:T(8,128)(2,1)}, bf16[2048,1536]{1,0:T(8,128)(2,1)}, bf16[640,1280]{1,0:T(8,128)(2,1)}, bf16[10...) custom-call(bf16[1024,512]{1,0:T(8,128)(2,1)} %refs_16_.1, ...), custom_call_target="tpu_custom_call" | custom-call | tf_op jit(solution)/shard_map/head/pallas_call | solution.py:979
  97.5 0.0 copy-start
  97.5 301.0 %middle.1 = (bf16[1024,512]{1,0:T(8,128)(2,1)}, f32[1024,640]{1,0:T(8,128)}, bf16[1024,2048]{1,0:T(8,128)(2,1)}, f32[1024,512]{1,0:T(8,128)}, bf16[1024,1536]{1,...) custom-call(bf16[1024,640]{1,0:T(8,128)(2,1)} %get-tuple-element.40., ...), custom_call_target="tpu_custom_call" | custom-call | tf_op jit(solution)/shard_map/middle/pallas_call | solution.py:1464
  398.5 0.0 copy-done
  398.5 0.8 concatenate.7.refs_6_
  399.3 106.4 %tail.1 = (bf16[1024,512]{1,0:T(8,128)(2,1)}, f32[256,1536]{1,0:T(8,128)}, f32[256,640]{1,0:T(8,128)}, f32[256,1280]{1,0:T(8,128)}, f32[32,1280]{1,0:T(8,128)}, /*index=5*/f32[2,2048]{1,0:T(2,128)}, f32[8,640]{1,0:T(8,128)}) custom-call(f32[1024,640]{1,0:T(8,128)} %get-tuple-element.44.refs_0_, f32[1024,1280]{1,0:T(8,128)} %get-tuple-element.45.refs_1_, ...), custom_call_target="tpu_custom_call" | custom-call | tf_op jit(solution)/shard_map/tail/pallas_call | solution.py:1938
  505.8 0.0 copy-start.3
  505.8 0.0 copy-start.6
  505.8 3.2 copy.43
  509.0 1.1 fusion.6
  510.1 1.1 copy.42
  511.2 0.7 fusion.7
  511.8 1.0 copy.50
  512.8 1.0 copy.51
  513.8 0.6 copy.52
  514.4 0.6 copy.53
  515.0 1.1 copy.54
  516.2 1.1 copy.55
  (20 shorter events, 0.0 us)
Async XLA Ops:
  97.5 301.0 %copy-start = (f32[1024,8]{1,0:T(8,128)S(1)}, f32[1024,8]{1,0:T(8,128)}, u32[]{:S(2)}) copy-start(f32[1024,8]{1,0:T(8,128)} %copy.39.refs_3_) | copy-start | bytes 98308
  505.8 3.2 copy-start.3
  505.8 4.3 copy-start.6
  509.0 2.2 copy-start.7
  509.0 2.9 copy-start.4
  510.1 3.7 copy-start.9
  510.1 4.3 copy-start.8
  510.1 4.9 copy-start.2
  511.2 1.6 copy-start.5
  512.8 3.3 copy-start.1
